TPU v7x, 32 devices: a whole 2x2x4 slice. The times are simulated.
32 devices in a mesh: row: 8 (over z, x), col: 4 (over y, core).
Axes of the slice: x: 2, y: 2, z: 4, core: 2. Of those that a mesh axis runs over, the one named last changes fastest.
Arguments:
- weight: float32 [4096, 4096], P('row', 'col'), may hold values from -6 to 6
- blocks: float32 [5, 4096, 512], P(None, ('row', 'col')), may hold values from -0.2 to 1.2
Outputs:
- merged: float32 [4096, 4096], P('row', 'col')
All inputs are finite; a program needn't handle non-finite values.
Results may differ from a plain program's by a relative error of at most 0.00017.
Values sent between devices are 32-bit elements; how exact they have to be, the bound alone decides.
No kernel may reach another device: no remote copies, remote signals or barrier semaphores. Data moves between devices by JAX's collectives and lax.ppermute only.
A program may use at most 64 MiB of HBM per device.

v0:
```python
import functools

import jax
import jax.numpy as jnp
from jax import lax
from jax.experimental import pallas as pl
from jax.experimental.pallas import tpu as pltpu
from jax.sharding import PartitionSpec as P

CHUNKS = ((0, 2), (0, 2), (0, 4), (1, 4), (1, 2), (1, 2))
EIGHTHS = 8
STEPS = (
    (((0, 0),), ()),
    (((1, 0),), ("across",)),
    ((), ("near",)),
    (((0, 1), (2, 0)), ()),
    (((1, 1),), ()),
    (((0, 2),), ()),
    (((3, 0),), ()),
    (((1, 2),), ()),
    (((2, 1),), ()),
    ((), ("across cores",)),
    (((0, 3),), ()),
    ((), ("far",)),
    (((3, 1), (4, 0)), ()),
    (((0, 4),), ()),
    (((2, 2), (1, 3)), ()),
    (((4, 1),), ()),
    (((3, 2),), ()),
    (((1, 4),), ()),
    (((0, 5), (5, 0)), ()),
    (((5, 1),), ()),
    (((2, 3),), ()),
    (((4, 2),), ()),
    (((2, 4),), ()),
    (((1, 5),), ()),
    (((3, 3),), ()),
    (((5, 2),), ()),
    (((4, 3),), ()),
    (((3, 4),), ()),
    (((2, 5),), ()),
    (((4, 4),), ()),
    (((5, 3),), ()),
    (((5, 4),), ()),
    (((3, 5),), ()),
    (((4, 5),), ()),
    (((5, 5),), ()),
)
HANDED = {
    "across": (("blocks", 0, 5), "across"),
    "across cores": (("across", 0, 5), "cores"),
}
MADE = {
    "near": (0, 0, "blocks", "cores"),
    "far": (1, 0, "across", "across cores"),
}


def partner_route(count, mask):
    return [(low, low ^ mask) for low in range(count) if low ^ mask < count]


def two_terms(values):
    high = values.astype(jnp.bfloat16)
    return high, (values - high.astype(jnp.float32)).astype(jnp.bfloat16)


def product(table, first, second):
    high = jnp.concatenate([first[0], second[0]], axis=0)
    low = jnp.concatenate([first[1], second[1]], axis=0)
    dot = functools.partial(jnp.dot, preferred_element_type=jnp.float32)
    return dot(table[0], high) + (dot(table[0], low) + dot(table[1], high))


class Operands:
    def __init__(self):
        self.arrays, self.places = [], {}

    def add(self, array):
        if id(array) not in self.places:
            self.places[id(array)] = len(self.arrays)
            self.arrays.append(array)
        return self.places[id(array)]


def step(place, weight, blocks, merged, state, tables, rows, tasks, work, chunks, bit_count):
    half = blocks.shape[2] // 2
    stages = blocks.shape[0]
    operands, held, table_at = Operands(), {}, {}
    for index, stage in tasks:
        if stage > 0:
            sent, came = state[index]
            held[index] = [(operands.add(sent[0]), sent[1]), (operands.add(came[0]), came[1])]
            table_at[index] = operands.add(tables[chunks[index][0], stage - 1])
    handing = [name for name in work if name in HANDED]
    making = [name for name in work if name in MADE]
    hand_from = {}
    for name in handing:
        (source, first, last), _ = HANDED[name]
        hand_from[name] = source == "blocks" or operands.add(rows[source])
    make_from = {
        name: [operands.add(rows[source]) for source in MADE[name][2:]] for name in making
    }

    arrays, slots = [], {}
    for index, stage in tasks:
        if stage < stages:
            way = stage % bit_count
            for at, (width, other, total) in enumerate(arrays):
                if (width, other) == (chunks[index][2], way):
                    break
            else:
                at, total = len(arrays), 0
                arrays.append(None)
            arrays[at] = (chunks[index][2], way, total + 1)
            slots[index] = (at, total)
    entering = [index for index, stage in tasks if stage == 0]
    leaving = [index for index, stage in tasks if stage == stages]
    whole = {}
    if entering:
        whole["weight"] = weight
    if True in hand_from.values():
        whole["blocks"] = blocks
    if merged is not None:
        whole["merged"] = merged

    def kernel(*refs):
        place_ref, refs = refs[0], refs[1:]
        whole_refs, refs = dict(zip(whole, refs)), refs[len(whole) :]
        ins, refs = refs[: len(operands.arrays)], refs[len(operands.arrays) :]
        merged_ref, refs = refs[0], refs[1:]
        sends, refs = refs[: len(arrays)], refs[len(arrays) :]
        handed, refs = dict(zip(handing, refs)), refs[len(handing) :]
        made, refs = refs[:made_count], refs[made_count:]
        results, sems = dict(zip(leaving, refs)), refs[len(leaving)]

        def region(ref, index):
            half_block, column, width = chunks[index]
            first = pl.multiple_of(place_ref[half_block] * half, half)
            return ref.at[pl.ds(first, half), pl.ds(column, width)]

        moves = []

        def move(source, target):
            moves.append(pltpu.make_async_copy(source, target, sems.at[len(moves)]))
            moves[-1].start()

        for index in entering:
            at, slot = slots[index]
            move(region(whole_refs["weight"], index), sends[at].at[slot])
        for name in handing:
            (source, first, last), _ = HANDED[name]
            ref = whole_refs["blocks"] if source == "blocks" else ins[hand_from[name]]
            move(ref.at[pl.ds(first, last - first)], handed[name])
        for index, stage in tasks:
            if stage > 0:
                mine, theirs = [two_terms(ins[at][slot]) for at, slot in held[index]]
                if stage == stages:
                    target = results[index]
                else:
                    at, slot = slots[index]
                    target = sends[at].at[slot]
                target[...] = product(ins[table_at[index]], mine, theirs)
                if stage == stages:
                    move(results[index], region(merged_ref, index))
        position = 0
        for name in making:
            mine, mates = [ins[at] for at in make_from[name]]
            low_core = place_ref[2] == 0
            depth = mine.shape[1]
            for k in range(mine.shape[0]):
                for side in range(2):
                    low, high = (mine, mates) if side == 0 else (mates, mine)
                    terms = two_terms(jnp.where(low_core, low[k], high[k]))
                    for term in range(2):
                        made[position][term, side * depth : (side + 1) * depth] = terms[term]
                position += 1
        for each in moves:
            each.wait()

    shape = lambda *dims: jax.ShapeDtypeStruct(dims, jnp.float32)
    outs = [shape(units, half, width) for width, _, units in arrays]
    for name in handing:
        (_, first, last), _ = HANDED[name]
        outs.append(shape(last - first, *blocks.shape[1:]))
    made_keys = [
        (MADE[name][0], MADE[name][1] + k)
        for name in making
        for k in range(rows[MADE[name][2]].shape[0])
    ]
    made_count = len(made_keys)
    outs += [jax.ShapeDtypeStruct((2, half, 2 * half), jnp.bfloat16)] * made_count
    hbm = pl.BlockSpec(memory_space=pltpu.HBM)
    vmem = pl.BlockSpec(memory_space=pltpu.VMEM)
    products = sum(chunks[index][2] for index, stage in tasks if stage > 0)
    merged, *new = pl.pallas_call(
        kernel,
        out_shape=[shape(*weight.shape)] + outs,
        in_specs=[pl.BlockSpec(memory_space=pltpu.SMEM)]
        + [hbm] * len(whole)
        + [vmem] * len(operands.arrays),
        out_specs=[hbm] + [vmem] * len(outs),
        scratch_shapes=[pltpu.VMEM((half, chunks[index][2]), jnp.float32) for index in leaving]
        + [pltpu.SemaphoreType.DMA((len(entering) + len(handing) + len(leaving) + 1,))],
        input_output_aliases={len(whole): 0} if merged is not None else {},
        compiler_params=pltpu.CompilerParams(vmem_limit_bytes=(60 if merged is None else 40) * 2**20),
        cost_estimate=pl.CostEstimate(
            flops=12 * half * half * products,
            bytes_accessed=sum(4 * array.size for array in operands.arrays + outs),
            transcendentals=0,
        ),
    )(place, *whole.values(), *operands.arrays)
    sent, new = new[: len(arrays)], new[len(arrays) :]
    handed, made = dict(zip(handing, new)), dict(zip(made_keys, new[len(handing) :]))
    ways = [way for _, way, _ in arrays]
    return merged, sent, ways, slots, handed, made


def pipelined(weight, blocks):
    count, columns = lax.axis_size("row"), lax.axis_size("col")
    bit_count = count.bit_length() - 1
    col = lax.axis_index("col")
    own = col // 2
    place = jnp.stack([own, 1 - own, col % 2]).astype(jnp.int32)
    ways = {
        "cores": partner_route(columns, 1),
        "across": partner_route(columns, 2),
    }
    chunks, column = [], [0, 0]
    for half_block, eighths in CHUNKS:
        width = weight.shape[1] * eighths // EIGHTHS
        chunks.append((half_block, column[half_block], width))
        column[half_block] += width
    rows = {"blocks": blocks, "cores": lax.ppermute(blocks, "col", ways["cores"])}
    merged, state, tables = None, {}, {}
    for tasks, work in STEPS:
        merged, sent, sent_ways, slots, handed, made = step(
            place, weight, blocks, merged, state, tables, rows, tasks, work, chunks, bit_count
        )
        tables.update(made)
        came = [
            lax.ppermute(array, "row", partner_route(count, 1 << way))
            for array, way in zip(sent, sent_ways)
        ]
        for index, (at, slot) in slots.items():
            state[index] = ((sent[at], slot), (came[at], slot))
        for name, array in handed.items():
            rows[name] = lax.ppermute(array, "col", ways[HANDED[name][1]])
    return merged


def plain(weight, blocks):
    count = lax.axis_size("row")
    bit_count = count.bit_length() - 1
    factors = blocks.shape[0]
    half = blocks.shape[2] // 2
    halves = weight.shape[0] // half
    tables = [lax.all_gather(blocks[k], "col", axis=0, tiled=True) for k in range(factors)]
    bands = []
    for t in range(halves):
        rows = slice(t * half, (t + 1) * half)
        held = weight[rows]
        for factor in range(factors):
            table = tables[factor][rows]
            partner = lax.ppermute(held, "row", partner_route(count, 1 << factor % bit_count))
            dot = functools.partial(jnp.dot, precision=lax.Precision.HIGHEST)
            held = dot(table[:, :half], held) + dot(table[:, half:], partner)
        bands.append(held)
    return jnp.concatenate(bands, axis=0)


def body(weight, blocks):
    fits = lax.axis_size("row") == 8 and lax.axis_size("col") == 4 and blocks.shape[0] == 5
    fits = fits and weight.shape[0] == blocks.shape[2] == 4 * blocks.shape[1]
    fits = fits and weight.shape[1] % (128 * EIGHTHS) == 0
    return (pipelined if fits else plain)(weight, blocks)


def solution(mesh):
    return jax.shard_map(
        body,
        mesh=mesh,
        in_specs=(P("row", "col"), P(None, ("row", "col"), None)),
        out_specs=P("row", "col"),
        check_vma=False,
    )
```

profile of v0, /device:TPU:0, one launch (start us, length us, event | category | flops | bytes accessed | tf_op | source)
XLA Modules:
  0.0 189.1 jit_solution(13263859692712511622)
XLA Ops:
  1.1 2.5 %shard_map.28 = (f32[512,1024]{1,0:T(8,128)}, f32[1,256,256]{2,1,0:T(8,128)}) custom-call(s32[3]{0:T(128)} %pad_add_fusion.refs_0_, f32[512,1024]{1,0:T(8,128)} %refs_1_.11), custom_call_target="tpu_custom_call" | custom-call | bytes 262144 | tf_op jit(solution)/shard_map/pallas_call | solution.py:196
  5.6 2.6 %collective-permute-start.6 = (f32[5,128,512]{2,1,0:T(8,128)S(1)}, f32[5,128,512]{2,1,0:T(8,128)S(1)}, u32[]{:S(2)}, u32[]{:S(2)}) collective-permute-start(f32[5,128,512]{2,1,0:T(8,128)S(1)} %get-tuple-element.93), channel_id=1, source_target_pairs={{0,2},{1,3},{2,0},{3,1},{4,6},{5,7},{6,4},{7,5},{8,10},{9,11},{10,... | collective-permute-start | bytes 3932168 | tf_op jit(solution)/shard_map/ppermute | solution.py:248
  11.3 6.0 %collective-permute-done.1.refs_4_ = f32[1,256,256]{2,1,0:T(8,128)S(1)} collective-permute-done((f32[1,256,256]{2,1,0:T(8,128)S(1)}, f32[1,256,256]{2,1,0:T(8,128)S(1)}, u32[]{:S(2)}, u32[]{:S(2)}) %collective-permute-start.1) | collective-permute-done | bytes 262176 | tf_op jit(solution)/shard_map/ppermute | solution.py:242
  25.5 2.2 %collective-permute-done.3.refs_3_ = f32[1,256,256]{2,1,0:T(8,128)S(1)} collective-permute-done((f32[1,256,256]{2,1,0:T(8,128)S(1)}, f32[1,256,256]{2,1,0:T(8,128)S(1)}, u32[]{:S(2)}, u32[]{:S(2)}) %collective-permute-start.3) | collective-permute-done | bytes 262176 | tf_op jit(solution)/shard_map/ppermute | solution.py:242
  29.3 2.8 %collective-permute-done.4.refs_3_ = f32[1,256,256]{2,1,0:T(8,128)S(1)} collective-permute-done((f32[1,256,256]{2,1,0:T(8,128)S(1)}, f32[1,256,256]{2,1,0:T(8,128)S(1)}, u32[]{:S(2)}, u32[]{:S(2)}) %collective-permute-start.4) | collective-permute-done | bytes 262176 | tf_op jit(solution)/shard_map/ppermute | solution.py:242
  34.6 3.0 %collective-permute-done.6.refs_2_ = f32[5,128,512]{2,1,0:T(8,128)S(1)} collective-permute-done((f32[5,128,512]{2,1,0:T(8,128)S(1)}, f32[5,128,512]{2,1,0:T(8,128)S(1)}, u32[]{:S(2)}, u32[]{:S(2)}) %collective-permute-start.6) | collective-permute-done | bytes 1310752 | tf_op jit(solution)/shard_map/ppermute | solution.py:248
  40.1 2.6 %collective-permute-start.7 = (f32[1,256,256]{2,1,0:T(8,128)S(1)}, f32[1,256,256]{2,1,0:T(8,128)S(1)}, u32[]{:S(2)}, u32[]{:S(2)}) collective-permute-start(f32[1,256,256]{2,1,0:T(8,128)S(1)} %get-tuple-element.95.refs_2_), channel_id=1, source_target_pairs={{0,16},{4,20},{8,24},{12,28},{16,0},{20,4},{24,8},{28,12},{1,17},{... | collective-permute-start | bytes 786440 | tf_op jit(solution)/shard_map/ppermute | solution.py:242
  44.6 11.3 %collective-permute-done.7.refs_3_ = f32[1,256,256]{2,1,0:T(8,128)S(1)} collective-permute-done((f32[1,256,256]{2,1,0:T(8,128)S(1)}, f32[1,256,256]{2,1,0:T(8,128)S(1)}, u32[]{:S(2)}, u32[]{:S(2)}) %collective-permute-start.7) | collective-permute-done | bytes 262176 | tf_op jit(solution)/shard_map/ppermute | solution.py:242
  61.4 4.0 %collective-permute-done.10.refs_3_ = f32[1,256,256]{2,1,0:T(8,128)S(1)} collective-permute-done((f32[1,256,256]{2,1,0:T(8,128)S(1)}, f32[1,256,256]{2,1,0:T(8,128)S(1)}, u32[]{:S(2)}, u32[]{:S(2)}) %collective-permute-start.10) | collective-permute-done | bytes 262176 | tf_op jit(solution)/shard_map/ppermute | solution.py:242
  70.7 2.0 %collective-permute-start.18 = (f32[1,256,512]{2,1,0:T(8,128)S(1)}, f32[1,256,512]{2,1,0:T(8,128)S(1)}, u32[]{:S(2)}, u32[]{:S(2)}) collective-permute-start(f32[1,256,512]{2,1,0:T(8,128)S(1)} %get-tuple-element.121.refs_2_), channel_id=1, source_target_pairs={{0,16},{4,20},{8,24},{12,28},{16,0},{20,4},{24,8},{28,12},{1,17},{... | collective-permute-start | bytes 1572872 | tf_op jit(solution)/shard_map/ppermute | solution.py:242
  73.6 16.5 %collective-permute-done.14.refs_3_ = f32[1,256,512]{2,1,0:T(8,128)S(1)} collective-permute-done((f32[1,256,512]{2,1,0:T(8,128)S(1)}, f32[1,256,512]{2,1,0:T(8,128)S(1)}, u32[]{:S(2)}, u32[]{:S(2)}) %collective-permute-start.14) | collective-permute-done | bytes 524320 | tf_op jit(solution)/shard_map/ppermute | solution.py:242
  92.2 2.4 %collective-permute-done.16.refs_4_ = f32[1,256,256]{2,1,0:T(8,128)S(1)} collective-permute-done((f32[1,256,256]{2,1,0:T(8,128)S(1)}, f32[1,256,256]{2,1,0:T(8,128)S(1)}, u32[]{:S(2)}, u32[]{:S(2)}) %collective-permute-start.16) | collective-permute-done | bytes 262176 | tf_op jit(solution)/shard_map/ppermute | solution.py:242
  96.9 6.9 %collective-permute-done.17.refs_3_ = f32[1,256,256]{2,1,0:T(8,128)S(1)} collective-permute-done((f32[1,256,256]{2,1,0:T(8,128)S(1)}, f32[1,256,256]{2,1,0:T(8,128)S(1)}, u32[]{:S(2)}, u32[]{:S(2)}) %collective-permute-start.17) | collective-permute-done | bytes 262176 | tf_op jit(solution)/shard_map/ppermute | solution.py:242
  106.9 2.5 %collective-permute-start.19 = (f32[1,256,256]{2,1,0:T(8,128)S(1)}, f32[1,256,256]{2,1,0:T(8,128)S(1)}, u32[]{:S(2)}, u32[]{:S(2)}) collective-permute-start(f32[1,256,256]{2,1,0:T(8,128)S(1)} %get-tuple-element.123.refs_2_), channel_id=1, source_target_pairs={{0,8},{4,12},{8,0},{12,4},{16,24},{20,28},{24,16},{28,20},{1,9},{5... | collective-permute-start | bytes 786440 | tf_op jit(solution)/shard_map/ppermute | solution.py:242
  109.4 15.1 %collective-permute-done.19.refs_3_ = f32[1,256,256]{2,1,0:T(8,128)S(1)} collective-permute-done((f32[1,256,256]{2,1,0:T(8,128)S(1)}, f32[1,256,256]{2,1,0:T(8,128)S(1)}, u32[]{:S(2)}, u32[]{:S(2)}) %collective-permute-start.19) | collective-permute-done | bytes 262176 | tf_op jit(solution)/shard_map/ppermute | solution.py:242
  126.7 3.6 %collective-permute-done.21.refs_3_ = f32[1,256,256]{2,1,0:T(8,128)S(1)} collective-permute-done((f32[1,256,256]{2,1,0:T(8,128)S(1)}, f32[1,256,256]{2,1,0:T(8,128)S(1)}, u32[]{:S(2)}, u32[]{:S(2)}) %collective-permute-start.21) | collective-permute-done | bytes 262176 | tf_op jit(solution)/shard_map/ppermute | solution.py:242
  134.8 2.0 %collective-permute-start.26 = (f32[1,256,512]{2,1,0:T(8,128)S(1)}, f32[1,256,512]{2,1,0:T(8,128)S(1)}, u32[]{:S(2)}, u32[]{:S(2)}) collective-permute-start(f32[1,256,512]{2,1,0:T(8,128)S(1)} %get-tuple-element.138.refs_2_), channel_id=1, source_target_pairs={{0,8},{4,12},{8,0},{12,4},{16,24},{20,28},{24,16},{28,20},{1,9},{5... | collective-permute-start | bytes 1572872 | tf_op jit(solution)/shard_map/ppermute | solution.py:242
  137.2 11.8 %collective-permute-done.23.refs_3_ = f32[1,256,256]{2,1,0:T(8,128)S(1)} collective-permute-done((f32[1,256,256]{2,1,0:T(8,128)S(1)}, f32[1,256,256]{2,1,0:T(8,128)S(1)}, u32[]{:S(2)}, u32[]{:S(2)}) %collective-permute-start.23) | collective-permute-done | bytes 262176 | tf_op jit(solution)/shard_map/ppermute | solution.py:242
  150.0 5.6 %collective-permute-done.24.refs_3_ = f32[1,256,256]{2,1,0:T(8,128)S(1)} collective-permute-done((f32[1,256,256]{2,1,0:T(8,128)S(1)}, f32[1,256,256]{2,1,0:T(8,128)S(1)}, u32[]{:S(2)}, u32[]{:S(2)}) %collective-permute-start.24) | collective-permute-done | bytes 262176 | tf_op jit(solution)/shard_map/ppermute | solution.py:242
  156.9 3.4 %collective-permute-start.28 = (f32[1,256,256]{2,1,0:T(8,128)S(1)}, f32[1,256,256]{2,1,0:T(8,128)S(1)}, u32[]{:S(2)}, u32[]{:S(2)}) collective-permute-start(f32[1,256,256]{2,1,0:T(8,128)S(1)} %get-tuple-element.141.refs_2_), channel_id=1, source_target_pairs={{0,16},{4,20},{8,24},{12,28},{16,0},{20,4},{24,8},{28,12},{1,17},{... | collective-permute-start | bytes 786440 | tf_op jit(solution)/shard_map/ppermute | solution.py:242
  161.6 2.0 %shard_map.56.refs_1_ = f32[512,1024]{1,0:T(8,128)} custom-call(s32[3]{0:T(128)S(1)} %copy-done.2, f32[512,1024]{1,0:T(8,128)} %get-tuple-element.137.refs_1_, f32[1,256,512]{2,1,0:T(8,128)S(1)} %get-tuple-element.138.refs_2_, f32[1,256,512]{2,1,0:T(8,128)S(1)} %collective-permute-done.26.refs_3_, ...), custom_call_target="tpu_custom_call", output_to_operand_aliasing={{}: (1, {})} | custom-call | flops 402653184 | bytes 2097152 | tf_op jit(solution)/shard_map/pallas_call | solution.py:196
  164.5 4.5 %collective-permute-done.28.refs_3_ = f32[1,256,256]{2,1,0:T(8,128)S(1)} collective-permute-done((f32[1,256,256]{2,1,0:T(8,128)S(1)}, f32[1,256,256]{2,1,0:T(8,128)S(1)}, u32[]{:S(2)}, u32[]{:S(2)}) %collective-permute-start.28) | collective-permute-done | bytes 262176 | tf_op jit(solution)/shard_map/ppermute | solution.py:242
  172.4 4.0 %collective-permute-done.29.refs_3_ = f32[1,256,256]{2,1,0:T(8,128)S(1)} collective-permute-done((f32[1,256,256]{2,1,0:T(8,128)S(1)}, f32[1,256,256]{2,1,0:T(8,128)S(1)}, u32[]{:S(2)}, u32[]{:S(2)}) %collective-permute-start.29) | collective-permute-done | bytes 262176 | tf_op jit(solution)/shard_map/ppermute | solution.py:242
  180.3 3.6 %collective-permute-done.31.refs_3_ = f32[1,256,256]{2,1,0:T(8,128)S(1)} collective-permute-done((f32[1,256,256]{2,1,0:T(8,128)S(1)}, f32[1,256,256]{2,1,0:T(8,128)S(1)}, u32[]{:S(2)}, u32[]{:S(2)}) %collective-permute-start.31) | collective-permute-done | bytes 262176 | tf_op jit(solution)/shard_map/ppermute | solution.py:242
  (86 shorter events, 65.9 us)
Async XLA Ops:
  5.6 32.0 %collective-permute-start.6 = (f32[5,128,512]{2,1,0:T(8,128)S(1)}, f32[5,128,512]{2,1,0:T(8,128)S(1)}, u32[]{:S(2)}, u32[]{:S(2)}) collective-permute-start(f32[5,128,512]{2,1,0:T(8,128)S(1)} %get-tuple-element.93), channel_id=1, source_target_pairs={{0,2},{1,3},{2,0},{3,1},{4,6},{5,7},{6,4},{7,5},{8,10},{9,11},{10,... | collective-permute-start | bytes 3932168 | tf_op jit(solution)/shard_map/ppermute | solution.py:248
  9.6 13.3 %collective-permute-start.2 = (f32[1,256,256]{2,1,0:T(8,128)S(1)}, f32[1,256,256]{2,1,0:T(8,128)S(1)}, u32[]{:S(2)}, u32[]{:S(2)}) collective-permute-start(f32[1,256,256]{2,1,0:T(8,128)S(1)} %get-tuple-element.83.refs_2_), channel_id=1, source_target_pairs={{0,4},{4,0},{8,12},{12,8},{16,20},{20,16},{24,28},{28,24},{1,5},{5... | collective-permute-start | bytes 786440 | tf_op jit(solution)/shard_map/ppermute | solution.py:242
  18.3 15.1 %collective-permute-start.5 = (f32[1,256,512]{2,1,0:T(8,128)S(1)}, f32[1,256,512]{2,1,0:T(8,128)S(1)}, u32[]{:S(2)}, u32[]{:S(2)}) collective-permute-start(f32[1,256,512]{2,1,0:T(8,128)S(1)} %get-tuple-element.91.refs_2_), channel_id=1, source_target_pairs={{0,4},{4,0},{8,12},{12,8},{16,20},{20,16},{24,28},{28,24},{1,5},{5... | collective-permute-start | bytes 1572872 | tf_op jit(solution)/shard_map/ppermute | solution.py:242
  38.2 18.9 %collective-permute-start.8 = (f32[5,128,512]{2,1,0:T(8,128)S(1)}, f32[5,128,512]{2,1,0:T(8,128)S(1)}, u32[]{:S(2)}, u32[]{:S(2)}) collective-permute-start(f32[5,128,512]{2,1,0:T(8,128)S(1)} %get-tuple-element.98), channel_id=1, source_target_pairs={{0,1},{1,0},{2,3},{3,2},{4,5},{5,4},{6,7},{7,6},{8,9},{9,8},{10,11... | collective-permute-start | bytes 3932168 | tf_op jit(solution)/shard_map/ppermute | solution.py:248
  38.3 20.0 %collective-permute-start.9 = (f32[1,256,512]{2,1,0:T(8,128)S(1)}, f32[1,256,512]{2,1,0:T(8,128)S(1)}, u32[]{:S(2)}, u32[]{:S(2)}) collective-permute-start(f32[1,256,512]{2,1,0:T(8,128)S(1)} %get-tuple-element.100.refs_3_), channel_id=1, source_target_pairs={{0,4},{4,0},{8,12},{12,8},{16,20},{20,16},{24,28},{28,24},{1,5},{5... | collective-permute-start | bytes 1572872 | tf_op jit(solution)/shard_map/ppermute | solution.py:242
  40.1 15.8 %collective-permute-start.7 = (f32[1,256,256]{2,1,0:T(8,128)S(1)}, f32[1,256,256]{2,1,0:T(8,128)S(1)}, u32[]{:S(2)}, u32[]{:S(2)}) collective-permute-start(f32[1,256,256]{2,1,0:T(8,128)S(1)} %get-tuple-element.95.refs_2_), channel_id=1, source_target_pairs={{0,16},{4,20},{8,24},{12,28},{16,0},{20,4},{24,8},{28,12},{1,17},{... | collective-permute-start | bytes 786440 | tf_op jit(solution)/shard_map/ppermute | solution.py:242
  42.7 24.9 %collective-permute-start.11 = (f32[1,256,512]{2,1,0:T(8,128)S(1)}, f32[1,256,512]{2,1,0:T(8,128)S(1)}, u32[]{:S(2)}, u32[]{:S(2)}) collective-permute-start(f32[1,256,512]{2,1,0:T(8,128)S(1)} %get-tuple-element.106.refs_2_), channel_id=1, source_target_pairs={{0,8},{4,12},{8,0},{12,4},{16,24},{20,28},{24,16},{28,20},{1,9},{5... | collective-permute-start | bytes 1572872 | tf_op jit(solution)/shard_map/ppermute | solution.py:242
  44.3 22.0 %collective-permute-start.12 = (f32[1,256,256]{2,1,0:T(8,128)S(1)}, f32[1,256,256]{2,1,0:T(8,128)S(1)}, u32[]{:S(2)}, u32[]{:S(2)}) collective-permute-start(f32[1,256,256]{2,1,0:T(8,128)S(1)} %get-tuple-element.107.refs_5_), channel_id=1, source_target_pairs={{0,16},{4,20},{8,24},{12,28},{16,0},{20,4},{24,8},{28,12},{1,17},{... | collective-permute-start | bytes 786440 | tf_op jit(solution)/shard_map/ppermute | solution.py:242
  59.5 30.6 %collective-permute-start.14 = (f32[1,256,512]{2,1,0:T(8,128)S(1)}, f32[1,256,512]{2,1,0:T(8,128)S(1)}, u32[]{:S(2)}, u32[]{:S(2)}) collective-permute-start(f32[1,256,512]{2,1,0:T(8,128)S(1)} %get-tuple-element.111.refs_2_), channel_id=1, source_target_pairs={{0,8},{4,12},{8,0},{12,4},{16,24},{20,28},{24,16},{28,20},{1,9},{5... | collective-permute-start | bytes 1572872 | tf_op jit(solution)/shard_map/ppermute | solution.py:242
  59.8 12.9 %collective-permute-start.13 = (f32[1,256,256]{2,1,0:T(8,128)S(1)}, f32[1,256,256]{2,1,0:T(8,128)S(1)}, u32[]{:S(2)}, u32[]{:S(2)}) collective-permute-start(f32[1,256,256]{2,1,0:T(8,128)S(1)} %get-tuple-element.109.refs_2_), channel_id=1, source_target_pairs={{0,4},{4,0},{8,12},{12,8},{16,20},{20,16},{24,28},{28,24},{1,5},{5... | collective-permute-start | bytes 786440 | tf_op jit(solution)/shard_map/ppermute | solution.py:242
  69.0 22.2 %collective-permute-start.15 = (f32[1,256,256]{2,1,0:T(8,128)S(1)}, f32[1,256,256]{2,1,0:T(8,128)S(1)}, u32[]{:S(2)}, u32[]{:S(2)}) collective-permute-start(f32[1,256,256]{2,1,0:T(8,128)S(1)} %get-tuple-element.114.refs_2_), channel_id=1, source_target_pairs={{0,4},{4,0},{8,12},{12,8},{16,20},{20,16},{24,28},{28,24},{1,5},{5... | collective-permute-start | bytes 786440 | tf_op jit(solution)/shard_map/ppermute | solution.py:242
  69.6 25.0 %collective-permute-start.16 = (f32[1,256,256]{2,1,0:T(8,128)S(1)}, f32[1,256,256]{2,1,0:T(8,128)S(1)}, u32[]{:S(2)}, u32[]{:S(2)}) collective-permute-start(f32[1,256,256]{2,1,0:T(8,128)S(1)} %get-tuple-element.116.refs_3_), channel_id=1, source_target_pairs={{0,8},{4,12},{8,0},{12,4},{16,24},{20,28},{24,16},{28,20},{1,9},{5... | collective-permute-start | bytes 786440 | tf_op jit(solution)/shard_map/ppermute | solution.py:242
  70.7 34.1 %collective-permute-start.18 = (f32[1,256,512]{2,1,0:T(8,128)S(1)}, f32[1,256,512]{2,1,0:T(8,128)S(1)}, u32[]{:S(2)}, u32[]{:S(2)}) collective-permute-start(f32[1,256,512]{2,1,0:T(8,128)S(1)} %get-tuple-element.121.refs_2_), channel_id=1, source_target_pairs={{0,16},{4,20},{8,24},{12,28},{16,0},{20,4},{24,8},{28,12},{1,17},{... | collective-permute-start | bytes 1572872 | tf_op jit(solution)/shard_map/ppermute | solution.py:242
  105.9 19.6 %collective-permute-start.20 = (f32[1,256,512]{2,1,0:T(8,128)S(1)}, f32[1,256,512]{2,1,0:T(8,128)S(1)}, u32[]{:S(2)}, u32[]{:S(2)}) collective-permute-start(f32[1,256,512]{2,1,0:T(8,128)S(1)} %get-tuple-element.125.refs_2_), channel_id=1, source_target_pairs={{0,4},{4,0},{8,12},{12,8},{16,20},{20,16},{24,28},{28,24},{1,5},{5... | collective-permute-start | bytes 1572872 | tf_op jit(solution)/shard_map/ppermute | solution.py:242
  106.3 25.6 %collective-permute-start.22 = (f32[1,256,512]{2,1,0:T(8,128)S(1)}, f32[1,256,512]{2,1,0:T(8,128)S(1)}, u32[]{:S(2)}, u32[]{:S(2)}) collective-permute-start(f32[1,256,512]{2,1,0:T(8,128)S(1)} %get-tuple-element.128.refs_2_), channel_id=1, source_target_pairs={{0,16},{4,20},{8,24},{12,28},{16,0},{20,4},{24,8},{28,12},{1,17},{... | collective-permute-start | bytes 1572872 | tf_op jit(solution)/shard_map/ppermute | solution.py:242
  106.9 17.6 %collective-permute-start.19 = (f32[1,256,256]{2,1,0:T(8,128)S(1)}, f32[1,256,256]{2,1,0:T(8,128)S(1)}, u32[]{:S(2)}, u32[]{:S(2)}) collective-permute-start(f32[1,256,256]{2,1,0:T(8,128)S(1)} %get-tuple-element.123.refs_2_), channel_id=1, source_target_pairs={{0,8},{4,12},{8,0},{12,4},{16,24},{20,28},{24,16},{28,20},{1,9},{5... | collective-permute-start | bytes 786440 | tf_op jit(solution)/shard_map/ppermute | solution.py:242
  109.4 20.9 %collective-permute-start.21 = (f32[1,256,256]{2,1,0:T(8,128)S(1)}, f32[1,256,256]{2,1,0:T(8,128)S(1)}, u32[]{:S(2)}, u32[]{:S(2)}) collective-permute-start(f32[1,256,256]{2,1,0:T(8,128)S(1)} %get-tuple-element.127.refs_2_), channel_id=1, source_target_pairs={{0,8},{4,12},{8,0},{12,4},{16,24},{20,28},{24,16},{28,20},{1,9},{5... | collective-permute-start | bytes 786440 | tf_op jit(solution)/shard_map/ppermute | solution.py:242
  133.1 27.2 %collective-permute-start.25 = (f32[1,256,512]{2,1,0:T(8,128)S(1)}, f32[1,256,512]{2,1,0:T(8,128)S(1)}, u32[]{:S(2)}, u32[]{:S(2)}) collective-permute-start(f32[1,256,512]{2,1,0:T(8,128)S(1)} %get-tuple-element.135.refs_2_), channel_id=1, source_target_pairs={{0,4},{4,0},{8,12},{12,8},{16,20},{20,16},{24,28},{28,24},{1,5},{5... | collective-permute-start | bytes 1572872 | tf_op jit(solution)/shard_map/ppermute | solution.py:242
  134.8 14.2 %collective-permute-start.23 = (f32[1,256,256]{2,1,0:T(8,128)S(1)}, f32[1,256,256]{2,1,0:T(8,128)S(1)}, u32[]{:S(2)}, u32[]{:S(2)}) collective-permute-start(f32[1,256,256]{2,1,0:T(8,128)S(1)} %get-tuple-element.131.refs_2_), channel_id=1, source_target_pairs={{0,8},{4,12},{8,0},{12,4},{16,24},{20,28},{24,16},{28,20},{1,9},{5... | collective-permute-start | bytes 786440 | tf_op jit(solution)/shard_map/ppermute | solution.py:242
  134.8 26.7 %collective-permute-start.26 = (f32[1,256,512]{2,1,0:T(8,128)S(1)}, f32[1,256,512]{2,1,0:T(8,128)S(1)}, u32[]{:S(2)}, u32[]{:S(2)}) collective-permute-start(f32[1,256,512]{2,1,0:T(8,128)S(1)} %get-tuple-element.138.refs_2_), channel_id=1, source_target_pairs={{0,8},{4,12},{8,0},{12,4},{16,24},{20,28},{24,16},{28,20},{1,9},{5... | collective-permute-start | bytes 1572872 | tf_op jit(solution)/shard_map/ppermute | solution.py:242
  136.8 18.7 %collective-permute-start.24 = (f32[1,256,256]{2,1,0:T(8,128)S(1)}, f32[1,256,256]{2,1,0:T(8,128)S(1)}, u32[]{:S(2)}, u32[]{:S(2)}) collective-permute-start(f32[1,256,256]{2,1,0:T(8,128)S(1)} %get-tuple-element.133.refs_2_), channel_id=1, source_target_pairs={{0,16},{4,20},{8,24},{12,28},{16,0},{20,4},{24,8},{28,12},{1,17},{... | collective-permute-start | bytes 786440 | tf_op jit(solution)/shard_map/ppermute | solution.py:242
  156.9 12.0 %collective-permute-start.28 = (f32[1,256,256]{2,1,0:T(8,128)S(1)}, f32[1,256,256]{2,1,0:T(8,128)S(1)}, u32[]{:S(2)}, u32[]{:S(2)}) collective-permute-start(f32[1,256,256]{2,1,0:T(8,128)S(1)} %get-tuple-element.141.refs_2_), channel_id=1, source_target_pairs={{0,16},{4,20},{8,24},{12,28},{16,0},{20,4},{24,8},{28,12},{1,17},{... | collective-permute-start | bytes 786440 | tf_op jit(solution)/shard_map/ppermute | solution.py:242
  161.5 16.9 %collective-permute-start.30 = (f32[1,256,512]{2,1,0:T(8,128)S(1)}, f32[1,256,512]{2,1,0:T(8,128)S(1)}, u32[]{:S(2)}, u32[]{:S(2)}) collective-permute-start(f32[1,256,512]{2,1,0:T(8,128)S(1)} %get-tuple-element.145.refs_2_), channel_id=1, source_target_pairs={{0,8},{4,12},{8,0},{12,4},{16,24},{20,28},{24,16},{28,20},{1,9},{5... | collective-permute-start | bytes 1572872 | tf_op jit(solution)/shard_map/ppermute | solution.py:242
  171.6 12.3 %collective-permute-start.31 = (f32[1,256,256]{2,1,0:T(8,128)S(1)}, f32[1,256,256]{2,1,0:T(8,128)S(1)}, u32[]{:S(2)}, u32[]{:S(2)}) collective-permute-start(f32[1,256,256]{2,1,0:T(8,128)S(1)} %get-tuple-element.147.refs_2_), channel_id=1, source_target_pairs={{0,8},{4,12},{8,0},{12,4},{16,24},{20,28},{24,16},{28,20},{1,9},{5... | collective-permute-start | bytes 786440 | tf_op jit(solution)/shard_map/ppermute | solution.py:242
  (13 other events, 85.4 us)
where the time goes:
time: 189 us
  waiting for transfers between devices  108 us (57%)
  Pallas kernels  41.1 us (22%)
  starting transfers between devices  37.2 us (20%)
    ppermute x30, waiting for transfers between devices, pipelined(): lax.ppermute(array, 'row', partner_route(count, 1 << way))  105 us
    pallas_call x35, Pallas kernels, step(): pl.pallas_call(kernel, out_shape=[shape(*weight.shape)] + outs, in_specs=...  41.1 us
    ppermute x30, starting transfers between devices, pipelined(): lax.ppermute(array, 'row', partner_route(count, 1 << way))  34.1 us
  transfers between devices with their start and end apart: 33, of which 21 were waited for; matrix products, arithmetic and copies ran while one was open for 0% of the time, Pallas kernels for 19%

commit v1 on v0

v1 whole, which is shorter than its diff:
```python
import functools

import jax
import jax.numpy as jnp
from jax import lax
from jax.experimental import pallas as pl
from jax.experimental.pallas import tpu as pltpu
from jax.sharding import PartitionSpec as P

CHUNKS = ((0, 2), (0, 2), (0, 2), (0, 2), (1, 2), (1, 2), (1, 2), (1, 2))
EIGHTHS = 8
STEPS = (
    (((0, 0),), ()),
    (((1, 0),), ()),
    (((0, 1), (2, 0)), ("near",)),
    (((1, 1),), ()),
    (((0, 2),), ()),
    (((2, 1), (3, 0)), ()),
    (((1, 2),), ()),
    (((0, 3),), ()),
    (((2, 2),), ()),
    (((3, 1),), ()),
    (((1, 3),), ()),
    (((0, 4),), ()),
    (((2, 3),), ()),
    (((3, 2),), ()),
    (((1, 4), (0, 5), (4, 0)), ()),
    (((2, 4), (5, 0)), ("far",)),
    (((3, 3), (1, 5)), ()),
    (((4, 1), (6, 0)), ()),
    (((2, 5),), ()),
    (((5, 1), (7, 0)), ()),
    (((4, 2), (3, 4)), ()),
    (((6, 1),), ()),
    (((5, 2),), ()),
    (((7, 1),), ()),
    (((4, 3),), ()),
    (((3, 5),), ()),
    (((6, 2),), ()),
    (((5, 3),), ()),
    (((7, 2),), ()),
    (((4, 4),), ()),
    (((6, 3),), ()),
    (((5, 4),), ()),
    (((7, 3),), ()),
    (((4, 5),), ()),
    (((6, 4),), ()),
    (((5, 5),), ()),
    (((7, 4),), ()),
    (((6, 5),), ()),
    (((7, 5),), ()),
)
NEAR, FAR = "near", "far"


def partner_route(count, mask):
    return [(low, low ^ mask) for low in range(count) if low ^ mask < count]


def two_terms(values):
    high = values.astype(jnp.bfloat16)
    return high, (values - high.astype(jnp.float32)).astype(jnp.bfloat16)


def product(table, first, second):
    high = jnp.concatenate([first[0], second[0]], axis=0)
    low = jnp.concatenate([first[1], second[1]], axis=0)
    dot = functools.partial(jnp.dot, preferred_element_type=jnp.float32)
    return dot(table[0], high) + (dot(table[0], low) + dot(table[1], high))


class Operands:
    def __init__(self):
        self.arrays, self.places = [], {}

    def add(self, array):
        if id(array) not in self.places:
            self.places[id(array)] = len(self.arrays)
            self.arrays.append(array)
        return self.places[id(array)]


def step(place, weight, blocks, merged, state, tables, rows, tasks, work, chunks, bit_count):
    half = blocks.shape[2] // 2
    stages = blocks.shape[0]
    operands, held, table_at = Operands(), {}, {}
    for index, stage in tasks:
        if stage > 0:
            sent, came = state[index]
            held[index] = [(operands.add(sent[0]), sent[1]), (operands.add(came[0]), came[1])]
            key = (chunks[index][0], stage - 1)
            table_at[index] = key if key not in tables else operands.add(tables[key])
    if NEAR in work:
        table_from = [operands.add(rows[name]) for name in ("blocks", "cores")]
    if FAR in work:
        table_from = [operands.add(rows["across"])]

    arrays, slots = [], {}
    for index, stage in tasks:
        if stage < stages:
            way = stage % bit_count
            for at, (width, other, total) in enumerate(arrays):
                if (width, other) == (chunks[index][2], way):
                    break
            else:
                at, total = len(arrays), 0
                arrays.append(None)
            arrays[at] = (chunks[index][2], way, total + 1)
            slots[index] = (at, total)
    entering = [index for index, stage in tasks if stage == 0]
    leaving = [index for index, stage in tasks if stage == stages]
    whole = {}
    if entering:
        whole["weight"] = weight
    if merged is not None:
        whole["merged"] = merged

    def kernel(*refs):
        place_ref, refs = refs[0], refs[1:]
        whole_refs, refs = dict(zip(whole, refs)), refs[len(whole) :]
        ins, refs = refs[: len(operands.arrays)], refs[len(operands.arrays) :]
        merged_ref, refs = refs[0], refs[1:]
        sends, refs = refs[: len(arrays)], refs[len(arrays) :]
        ordered, refs = refs[: int(NEAR in work)], refs[int(NEAR in work) :]
        made, refs = refs[: len(made_keys)], refs[len(made_keys) :]
        results, sems = dict(zip(leaving, refs)), refs[len(leaving)]

        def region(ref, index):
            half_block, column, width = chunks[index]
            first = pl.multiple_of(place_ref[half_block] * half, half)
            return ref.at[pl.ds(first, half), pl.ds(column, width)]

        moves = []

        def move(source, target):
            moves.append(pltpu.make_async_copy(source, target, sems.at[len(moves)]))
            moves[-1].start()

        for index in entering:
            at, slot = slots[index]
            move(region(whole_refs["weight"], index), sends[at].at[slot])
        for k, table in enumerate(made):
            if NEAR in work:
                mine, mates = [ins[at][k] for at in table_from]
                low_core = place_ref[2] == 0
                depth = mine.shape[0]
                ordered[0][k, :depth] = jnp.where(low_core, mine, mates)
                ordered[0][k, depth:] = jnp.where(low_core, mates, mine)
            source = ordered[0] if NEAR in work else ins[table_from[0]]
            table[0], table[1] = two_terms(source[k])
        for index, stage in tasks:
            if stage > 0:
                mine, theirs = [two_terms(ins[at][slot]) for at, slot in held[index]]
                if stage == stages:
                    target = results[index]
                else:
                    at, slot = slots[index]
                    target = sends[at].at[slot]
                at = table_at[index]
                table = ins[at] if isinstance(at, int) else made[made_keys.index(at)]
                target[...] = product(table, mine, theirs)
                if stage == stages:
                    move(results[index], region(merged_ref, index))
        for each in moves:
            each.wait()

    shape = lambda *dims: jax.ShapeDtypeStruct(dims, jnp.float32)
    outs = [shape(units, half, width) for width, _, units in arrays]
    if NEAR in work:
        outs.append(shape(stages, half, 2 * half))
    made_keys = []
    if NEAR in work or FAR in work:
        made_keys = [(int(FAR in work), k) for k in range(stages)]
    outs += [jax.ShapeDtypeStruct((2, half, 2 * half), jnp.bfloat16)] * len(made_keys)
    hbm = pl.BlockSpec(memory_space=pltpu.HBM)
    vmem = pl.BlockSpec(memory_space=pltpu.VMEM)
    merged, *new = pl.pallas_call(
        kernel,
        out_shape=[shape(*weight.shape)] + outs,
        in_specs=[pl.BlockSpec(memory_space=pltpu.SMEM)]
        + [hbm] * len(whole)
        + [vmem] * len(operands.arrays),
        out_specs=[hbm] + [vmem] * len(outs),
        scratch_shapes=[pltpu.VMEM((half, chunks[index][2]), jnp.float32) for index in leaving]
        + [pltpu.SemaphoreType.DMA((len(entering) + len(leaving) + 1,))],
        input_output_aliases={len(whole): 0} if merged is not None else {},
        compiler_params=pltpu.CompilerParams(vmem_limit_bytes=(60 if merged is None else 40) * 2**20),
        cost_estimate=pl.CostEstimate(flops=1, bytes_accessed=1, transcendentals=0),
    )(place, *whole.values(), *operands.arrays)
    sent, new = new[: len(arrays)], new[len(arrays) :]
    ordered = new.pop(0) if NEAR in work else None
    made = dict(zip(made_keys, new))
    ways = [way for _, way, _ in arrays]
    return merged, sent, ways, slots, ordered, made


def pipelined(weight, blocks):
    count, columns = lax.axis_size("row"), lax.axis_size("col")
    bit_count = count.bit_length() - 1
    col = lax.axis_index("col")
    own = col // 2
    place = jnp.stack([own, 1 - own, col % 2]).astype(jnp.int32)
    chunks, column = [], [0, 0]
    for half_block, eighths in CHUNKS:
        width = weight.shape[1] * eighths // EIGHTHS
        chunks.append((half_block, column[half_block], width))
        column[half_block] += width
    rows = {"blocks": blocks, "cores": lax.ppermute(blocks, "col", partner_route(columns, 1))}
    merged, state, tables = None, {}, {}
    for tasks, work in STEPS:
        merged, sent, sent_ways, slots, ordered, made = step(
            place, weight, blocks, merged, state, tables, rows, tasks, work, chunks, bit_count
        )
        tables.update(made)
        came = [
            lax.ppermute(array, "row", partner_route(count, 1 << way))
            for array, way in zip(sent, sent_ways)
        ]
        for index, (at, slot) in slots.items():
            state[index] = ((sent[at], slot), (came[at], slot))
        if ordered is not None:
            rows["across"] = lax.ppermute(ordered, "col", partner_route(columns, 2))
    return merged


def plain(weight, blocks):
    count = lax.axis_size("row")
    bit_count = count.bit_length() - 1
    factors = blocks.shape[0]
    half = blocks.shape[2] // 2
    halves = weight.shape[0] // half
    tables = [lax.all_gather(blocks[k], "col", axis=0, tiled=True) for k in range(factors)]
    bands = []
    for t in range(halves):
        rows = slice(t * half, (t + 1) * half)
        held = weight[rows]
        for factor in range(factors):
            table = tables[factor][rows]
            partner = lax.ppermute(held, "row", partner_route(count, 1 << factor % bit_count))
            dot = functools.partial(jnp.dot, precision=lax.Precision.HIGHEST)
            held = dot(table[:, :half], held) + dot(table[:, half:], partner)
        bands.append(held)
    return jnp.concatenate(bands, axis=0)


def body(weight, blocks):
    fits = lax.axis_size("row") == 8 and lax.axis_size("col") == 4 and blocks.shape[0] == 5
    fits = fits and weight.shape[0] == blocks.shape[2] == 4 * blocks.shape[1]
    fits = fits and weight.shape[1] % (128 * EIGHTHS) == 0
    return (pipelined if fits else plain)(weight, blocks)


def solution(mesh):
    return jax.shard_map(
        body,
        mesh=mesh,
        in_specs=(P("row", "col"), P(None, ("row", "col"), None)),
        out_specs=P("row", "col"),
        check_vma=False,
    )
```

time: 189 us -> 167 us (0.88)
  waiting for transfers between devices: 108 us -> 63.6 us
  starting transfers between devices: 37.2 us -> 56.4 us
  Pallas kernels: 41.1 us -> 46.1 us
    ppermute x30 -> x40, waiting for transfers between devices: 105 us -> 63.6 us  [pipelined(): lax.ppermute(array, 'row', partner_route(count, 1 << way))]
    ppermute x30 -> x40, starting transfers between devices: 34.1 us -> 54.1 us  [pipelined(): lax.ppermute(array, 'row', partner_route(count, 1 << way))]
    pallas_call x35 -> x39, Pallas kernels: 41.1 us -> 46.1 us  [step(): pl.pallas_call(kernel, out_shape=[shape(*weight.shape)] + outs, in_specs=...]
    ppermute x3 -> x2, waiting for transfers between devices: 2.99 us -> 0.01 us  [the longest x1 0.01 us: pipelined(): lax.ppermute(blocks, 'col', partner_route(columns, 1))]
  transfers between devices with their start and end apart: 33 -> 42, of which waited for: 21 -> 18; matrix products, arithmetic and copies ran while one was open for 0% -> 0% of each run, Pallas kernels for 19% -> 25%
where the time goes in v1:
time: 167 us
  waiting for transfers between devices  63.6 us (38%)
  starting transfers between devices  56.4 us (34%)
  Pallas kernels  46.1 us (28%)
    ppermute x40, waiting for transfers between devices, pipelined(): lax.ppermute(array, 'row', partner_route(count, 1 << way))  63.6 us
    ppermute x40, starting transfers between devices, pipelined(): lax.ppermute(array, 'row', partner_route(count, 1 << way))  54.1 us
    pallas_call x39, Pallas kernels, step(): pl.pallas_call(kernel, out_shape=[shape(*weight.shape)] + outs, in_specs=...  46.1 us
  transfers between devices with their start and end apart: 42, of which 18 were waited for; matrix products, arithmetic and copies ran while one was open for 0% of the time, Pallas kernels for 25%

profile of v1, /device:TPU:0, one launch (start us, length us, event | category | flops | bytes accessed | tf_op | source)
XLA Modules:
  0.0 167.3 jit_solution(17862241640117979844)
XLA Ops:
  1.0 2.5 %shard_map.28 = (f32[512,1024]{1,0:T(8,128)}, f32[1,256,256]{2,1,0:T(8,128)}) custom-call(s32[3]{0:T(128)} %pad_add_fusion.refs_0_, f32[512,1024]{1,0:T(8,128)} %refs_1_.15), custom_call_target="tpu_custom_call" | custom-call | flops 1 | bytes 1 | tf_op jit(solution)/shard_map/pallas_call | solution.py:177
  3.5 2.6 %collective-permute-start = (f32[1,256,256]{2,1,0:T(8,128)}, f32[1,256,256]{2,1,0:T(8,128)S(1)}, u32[]{:S(2)}, u32[]{:S(2)}) collective-permute-start(f32[1,256,256]{2,1,0:T(8,128)} %get-tuple-element.91.refs_3_), channel_id=1, source_target_pairs={{0,4},{4,0},{8,12},{12,8},{16,20},{20,16},{24,28},{28,24},{1,5},{5... | collective-permute-start | bytes 786440 | tf_op jit(solution)/shard_map/ppermute | solution.py:216
  6.7 6.6 %collective-permute-done.refs_4_ = f32[1,256,256]{2,1,0:T(8,128)S(1)} collective-permute-done((f32[1,256,256]{2,1,0:T(8,128)}, f32[1,256,256]{2,1,0:T(8,128)S(1)}, u32[]{:S(2)}, u32[]{:S(2)}) %collective-permute-start) | collective-permute-done | bytes 262176 | tf_op jit(solution)/shard_map/ppermute | solution.py:216
  20.5 5.6 %collective-permute-done.2.refs_3_ = f32[1,256,256]{2,1,0:T(8,128)S(1)} collective-permute-done((f32[1,256,256]{2,1,0:T(8,128)S(1)}, f32[1,256,256]{2,1,0:T(8,128)S(1)}, u32[]{:S(2)}, u32[]{:S(2)}) %collective-permute-start.2) | collective-permute-done | bytes 262176 | tf_op jit(solution)/shard_map/ppermute | solution.py:216
  29.7 2.7 %collective-permute-start.6 = (f32[1,256,256]{2,1,0:T(8,128)S(1)}, f32[1,256,256]{2,1,0:T(8,128)S(1)}, u32[]{:S(2)}, u32[]{:S(2)}) collective-permute-start(f32[1,256,256]{2,1,0:T(8,128)S(1)} %get-tuple-element.103.refs_2_), channel_id=1, source_target_pairs={{0,16},{4,20},{8,24},{12,28},{16,0},{20,4},{24,8},{28,12},{1,17},{... | collective-permute-start | bytes 786440 | tf_op jit(solution)/shard_map/ppermute | solution.py:216
  35.4 6.7 %collective-permute-done.5.refs_3_ = f32[1,256,256]{2,1,0:T(8,128)S(1)} collective-permute-done((f32[1,256,256]{2,1,0:T(8,128)S(1)}, f32[1,256,256]{2,1,0:T(8,128)S(1)}, u32[]{:S(2)}, u32[]{:S(2)}) %collective-permute-start.5) | collective-permute-done | bytes 262176 | tf_op jit(solution)/shard_map/ppermute | solution.py:216
  44.5 3.6 %collective-permute-start.10 = (f32[1,256,256]{2,1,0:T(8,128)S(1)}, f32[1,256,256]{2,1,0:T(8,128)S(1)}, u32[]{:S(2)}, u32[]{:S(2)}) collective-permute-start(f32[1,256,256]{2,1,0:T(8,128)S(1)} %get-tuple-element.112.refs_2_), channel_id=1, source_target_pairs={{0,4},{4,0},{8,12},{12,8},{16,20},{20,16},{24,28},{28,24},{1,5},{5... | collective-permute-start | bytes 786440 | tf_op jit(solution)/shard_map/ppermute | solution.py:216
  52.7 8.3 %collective-permute-done.9.refs_3_ = f32[1,256,256]{2,1,0:T(8,128)S(1)} collective-permute-done((f32[1,256,256]{2,1,0:T(8,128)S(1)}, f32[1,256,256]{2,1,0:T(8,128)S(1)}, u32[]{:S(2)}, u32[]{:S(2)}) %collective-permute-start.9) | collective-permute-done | bytes 262176 | tf_op jit(solution)/shard_map/ppermute | solution.py:216
  68.3 2.3 %collective-permute-start.17 = (f32[1,256,256]{2,1,0:T(8,128)S(1)}, f32[1,256,256]{2,1,0:T(8,128)S(1)}, u32[]{:S(2)}, u32[]{:S(2)}) collective-permute-start(f32[1,256,256]{2,1,0:T(8,128)S(1)} %get-tuple-element.126.refs_2_), channel_id=1, source_target_pairs={{0,16},{4,20},{8,24},{12,28},{16,0},{20,4},{24,8},{28,12},{1,17},{... | collective-permute-start | bytes 786440 | tf_op jit(solution)/shard_map/ppermute | solution.py:216
  70.8 1.9 %collective-permute-done.14.refs_7_ = f32[1,256,256]{2,1,0:T(8,128)S(1)} collective-permute-done((f32[1,256,256]{2,1,0:T(8,128)S(1)}, f32[1,256,256]{2,1,0:T(8,128)S(1)}, u32[]{:S(2)}, u32[]{:S(2)}) %collective-permute-start.14) | collective-permute-done | bytes 262176 | tf_op jit(solution)/shard_map/ppermute | solution.py:216
  72.7 1.9 %shard_map.42 = (f32[512,1024]{1,0:T(8,128)}, f32[1,256,256]{2,1,0:T(8,128)S(1)}, f32[1,256,256]{2,1,0:T(8,128)S(1)}) custom-call(s32[3]{0:T(128)S(1)} %copy-done.2, f32[512,1024]{1,0:T(8,128)S(1)} %copy-done, f32[512,1024]{1,0:T(8,128)} %get-tuple-element.118.refs_2_, ...), custom_call_target="tpu_custom_call", output_to_operand_aliasing={{0}: (2, {})} | custom-call | flops 1 | bytes 1 | tf_op jit(solution)/shard_map/pallas_call | solution.py:177
  77.6 1.8 %collective-permute-start.20 = (f32[1,256,256]{2,1,0:T(8,128)S(1)}, f32[1,256,256]{2,1,0:T(8,128)S(1)}, u32[]{:S(2)}, u32[]{:S(2)}) collective-permute-start(f32[1,256,256]{2,1,0:T(8,128)S(1)} %get-tuple-element.132.refs_2_), channel_id=1, source_target_pairs={{0,8},{4,12},{8,0},{12,4},{16,24},{20,28},{24,16},{28,20},{1,9},{5... | collective-permute-start | bytes 786440 | tf_op jit(solution)/shard_map/ppermute | solution.py:216
  80.5 4.3 %collective-permute-done.18.refs_6_ = f32[1,256,256]{2,1,0:T(8,128)S(1)} collective-permute-done((f32[1,256,256]{2,1,0:T(8,128)S(1)}, f32[1,256,256]{2,1,0:T(8,128)S(1)}, u32[]{:S(2)}, u32[]{:S(2)}) %collective-permute-start.18) | collective-permute-done | bytes 262176 | tf_op jit(solution)/shard_map/ppermute | solution.py:216
  84.7 1.9 %shard_map.44 = (f32[512,1024]{1,0:T(8,128)}, f32[1,256,256]{2,1,0:T(8,128)S(1)}) custom-call(s32[3]{0:T(128)S(1)} %copy-done.2, f32[512,1024]{1,0:T(8,128)} %get-tuple-element.125.refs_1_, f32[1,256,256]{2,1,0:T(8,128)S(1)} %get-tuple-element.126.refs_2_, f32[1,256,256]{2,1,0:T(8,128)S(1)} %collective-permute-done.17.refs_3_, ...), custom_call_target="tpu_custom_call", output_to_operand_aliasing={{0}: (1, {})} | custom-call | flops 1 | bytes 1 | tf_op jit(solution)/shard_map/pallas_call | solution.py:177
  98.4 3.9 %collective-permute-start.27 = (f32[1,256,256]{2,1,0:T(8,128)S(1)}, f32[1,256,256]{2,1,0:T(8,128)S(1)}, u32[]{:S(2)}, u32[]{:S(2)}) collective-permute-start(f32[1,256,256]{2,1,0:T(8,128)S(1)} %get-tuple-element.145.refs_2_), channel_id=1, source_target_pairs={{0,16},{4,20},{8,24},{12,28},{16,0},{20,4},{24,8},{28,12},{1,17},{... | collective-permute-start | bytes 786440 | tf_op jit(solution)/shard_map/ppermute | solution.py:216
  102.2 2.6 %collective-permute-start.28 = (f32[1,256,256]{2,1,0:T(8,128)S(1)}, f32[1,256,256]{2,1,0:T(8,128)S(1)}, u32[]{:S(2)}, u32[]{:S(2)}) collective-permute-start(f32[1,256,256]{2,1,0:T(8,128)S(1)} %get-tuple-element.148.refs_2_), channel_id=1, source_target_pairs={{0,8},{4,12},{8,0},{12,4},{16,24},{20,28},{24,16},{28,20},{1,9},{5... | collective-permute-start | bytes 786440 | tf_op jit(solution)/shard_map/ppermute | solution.py:216
  105.9 4.4 %collective-permute-done.25.refs_3_ = f32[1,256,256]{2,1,0:T(8,128)S(1)} collective-permute-done((f32[1,256,256]{2,1,0:T(8,128)S(1)}, f32[1,256,256]{2,1,0:T(8,128)S(1)}, u32[]{:S(2)}, u32[]{:S(2)}) %collective-permute-start.25) | collective-permute-done | bytes 262176 | tf_op jit(solution)/shard_map/ppermute | solution.py:216
  111.2 1.9 %collective-permute-start.30 = (f32[1,256,256]{2,1,0:T(8,128)S(1)}, f32[1,256,256]{2,1,0:T(8,128)S(1)}, u32[]{:S(2)}, u32[]{:S(2)}) collective-permute-start(f32[1,256,256]{2,1,0:T(8,128)S(1)} %get-tuple-element.151.refs_2_), channel_id=1, source_target_pairs={{0,16},{4,20},{8,24},{12,28},{16,0},{20,4},{24,8},{28,12},{1,17},{... | collective-permute-start | bytes 786440 | tf_op jit(solution)/shard_map/ppermute | solution.py:216
  114.1 2.8 %collective-permute-start.31 = (f32[1,256,256]{2,1,0:T(8,128)S(1)}, f32[1,256,256]{2,1,0:T(8,128)S(1)}, u32[]{:S(2)}, u32[]{:S(2)}) collective-permute-start(f32[1,256,256]{2,1,0:T(8,128)S(1)} %get-tuple-element.153.refs_2_), channel_id=1, source_target_pairs={{0,8},{4,12},{8,0},{12,4},{16,24},{20,28},{24,16},{28,20},{1,9},{5... | collective-permute-start | bytes 786440 | tf_op jit(solution)/shard_map/ppermute | solution.py:216
  119.8 6.2 %collective-permute-done.29.refs_3_ = f32[1,256,256]{2,1,0:T(8,128)S(1)} collective-permute-done((f32[1,256,256]{2,1,0:T(8,128)S(1)}, f32[1,256,256]{2,1,0:T(8,128)S(1)}, u32[]{:S(2)}, u32[]{:S(2)}) %collective-permute-start.29) | collective-permute-done | bytes 262176 | tf_op jit(solution)/shard_map/ppermute | solution.py:216
  129.4 2.1 %collective-permute-start.34 = (f32[1,256,256]{2,1,0:T(8,128)S(1)}, f32[1,256,256]{2,1,0:T(8,128)S(1)}, u32[]{:S(2)}, u32[]{:S(2)}) collective-permute-start(f32[1,256,256]{2,1,0:T(8,128)S(1)} %get-tuple-element.160.refs_2_), channel_id=1, source_target_pairs={{0,4},{4,0},{8,12},{12,8},{16,20},{20,16},{24,28},{28,24},{1,5},{5... | collective-permute-start | bytes 786440 | tf_op jit(solution)/shard_map/ppermute | solution.py:216
  136.1 8.6 %collective-permute-done.33.refs_3_ = f32[1,256,256]{2,1,0:T(8,128)S(1)} collective-permute-done((f32[1,256,256]{2,1,0:T(8,128)S(1)}, f32[1,256,256]{2,1,0:T(8,128)S(1)}, u32[]{:S(2)}, u32[]{:S(2)}) %collective-permute-start.33) | collective-permute-done | bytes 262176 | tf_op jit(solution)/shard_map/ppermute | solution.py:216
  151.6 2.0 %collective-permute-done.37.refs_3_ = f32[1,256,256]{2,1,0:T(8,128)S(1)} collective-permute-done((f32[1,256,256]{2,1,0:T(8,128)S(1)}, f32[1,256,256]{2,1,0:T(8,128)S(1)}, u32[]{:S(2)}, u32[]{:S(2)}) %collective-permute-start.37) | collective-permute-done | bytes 262176 | tf_op jit(solution)/shard_map/ppermute | solution.py:216
  159.4 3.3 %collective-permute-done.40.refs_3_ = f32[1,256,256]{2,1,0:T(8,128)S(1)} collective-permute-done((f32[1,256,256]{2,1,0:T(8,128)S(1)}, f32[1,256,256]{2,1,0:T(8,128)S(1)}, u32[]{:S(2)}, u32[]{:S(2)}) %collective-permute-start.40) | collective-permute-done | bytes 262176 | tf_op jit(solution)/shard_map/ppermute | solution.py:216
  (108 shorter events, 76.3 us)
Async XLA Ops:
  0.0 13.3 %collective-permute-start.1 = (f32[5,128,512]{2,1,0:T(8,128)}, f32[5,128,512]{2,1,0:T(8,128)S(1)}, u32[]{:S(2)}, u32[]{:S(2)}) collective-permute-start(f32[5,128,512]{2,1,0:T(8,128)} %refs_5_.1), channel_id=1, source_target_pairs={{0,1},{1,0},{2,3},{3,2},{4,5},{5,4},{6,7},{7,6},{8,9},{9,8},{10,11... | collective-permute-start | bytes 3932168 | tf_op jit(solution)/shard_map/ppermute | solution.py:208
  15.1 60.8 %collective-permute-start.16 = (f32[5,256,512]{2,1,0:T(8,128)S(1)}, f32[5,256,512]{2,1,0:T(8,128)S(1)}, u32[]{:S(2)}, u32[]{:S(2)}) collective-permute-start(f32[5,256,512]{2,1,0:T(8,128)S(1)} %get-tuple-element.124), channel_id=1, source_target_pairs={{0,2},{1,3},{2,0},{3,1},{4,6},{5,7},{6,4},{7,5},{8,10},{9,11},{10,... | collective-permute-start | bytes 7864328 | tf_op jit(solution)/shard_map/ppermute | solution.py:222
  27.1 15.0 %collective-permute-start.5 = (f32[1,256,256]{2,1,0:T(8,128)S(1)}, f32[1,256,256]{2,1,0:T(8,128)S(1)}, u32[]{:S(2)}, u32[]{:S(2)}) collective-permute-start(f32[1,256,256]{2,1,0:T(8,128)S(1)} %get-tuple-element.101.refs_2_), channel_id=1, source_target_pairs={{0,8},{4,12},{8,0},{12,4},{16,24},{20,28},{24,16},{28,20},{1,9},{5... | collective-permute-start | bytes 786440 | tf_op jit(solution)/shard_map/ppermute | solution.py:216
  29.7 13.9 %collective-permute-start.6 = (f32[1,256,256]{2,1,0:T(8,128)S(1)}, f32[1,256,256]{2,1,0:T(8,128)S(1)}, u32[]{:S(2)}, u32[]{:S(2)}) collective-permute-start(f32[1,256,256]{2,1,0:T(8,128)S(1)} %get-tuple-element.103.refs_2_), channel_id=1, source_target_pairs={{0,16},{4,20},{8,24},{12,28},{16,0},{20,4},{24,8},{28,12},{1,17},{... | collective-permute-start | bytes 786440 | tf_op jit(solution)/shard_map/ppermute | solution.py:216
  33.3 14.8 %collective-permute-start.7 = (f32[1,256,256]{2,1,0:T(8,128)S(1)}, f32[1,256,256]{2,1,0:T(8,128)S(1)}, u32[]{:S(2)}, u32[]{:S(2)}) collective-permute-start(f32[1,256,256]{2,1,0:T(8,128)S(1)} %get-tuple-element.106.refs_2_), channel_id=1, source_target_pairs={{0,8},{4,12},{8,0},{12,4},{16,24},{20,28},{24,16},{28,20},{1,9},{5... | collective-permute-start | bytes 786440 | tf_op jit(solution)/shard_map/ppermute | solution.py:216
  33.9 16.2 %collective-permute-start.8 = (f32[1,256,256]{2,1,0:T(8,128)S(1)}, f32[1,256,256]{2,1,0:T(8,128)S(1)}, u32[]{:S(2)}, u32[]{:S(2)}) collective-permute-start(f32[1,256,256]{2,1,0:T(8,128)S(1)} %get-tuple-element.108.refs_2_), channel_id=1, source_target_pairs={{0,4},{4,0},{8,12},{12,8},{16,20},{20,16},{24,28},{28,24},{1,5},{5... | collective-permute-start | bytes 786440 | tf_op jit(solution)/shard_map/ppermute | solution.py:216
  43.0 18.0 %collective-permute-start.9 = (f32[1,256,256]{2,1,0:T(8,128)S(1)}, f32[1,256,256]{2,1,0:T(8,128)S(1)}, u32[]{:S(2)}, u32[]{:S(2)}) collective-permute-start(f32[1,256,256]{2,1,0:T(8,128)S(1)} %get-tuple-element.110.refs_2_), channel_id=1, source_target_pairs={{0,16},{4,20},{8,24},{12,28},{16,0},{20,4},{24,8},{28,12},{1,17},{... | collective-permute-start | bytes 786440 | tf_op jit(solution)/shard_map/ppermute | solution.py:216
  44.5 19.0 %collective-permute-start.10 = (f32[1,256,256]{2,1,0:T(8,128)S(1)}, f32[1,256,256]{2,1,0:T(8,128)S(1)}, u32[]{:S(2)}, u32[]{:S(2)}) collective-permute-start(f32[1,256,256]{2,1,0:T(8,128)S(1)} %get-tuple-element.112.refs_2_), channel_id=1, source_target_pairs={{0,4},{4,0},{8,12},{12,8},{16,20},{20,16},{24,28},{28,24},{1,5},{5... | collective-permute-start | bytes 786440 | tf_op jit(solution)/shard_map/ppermute | solution.py:216
  49.1 15.5 %collective-permute-start.11 = (f32[1,256,256]{2,1,0:T(8,128)S(1)}, f32[1,256,256]{2,1,0:T(8,128)S(1)}, u32[]{:S(2)}, u32[]{:S(2)}) collective-permute-start(f32[1,256,256]{2,1,0:T(8,128)S(1)} %get-tuple-element.115.refs_2_), channel_id=1, source_target_pairs={{0,16},{4,20},{8,24},{12,28},{16,0},{20,4},{24,8},{28,12},{1,17},{... | collective-permute-start | bytes 786440 | tf_op jit(solution)/shard_map/ppermute | solution.py:216
  51.0 16.3 %collective-permute-start.12 = (f32[1,256,256]{2,1,0:T(8,128)S(1)}, f32[1,256,256]{2,1,0:T(8,128)S(1)}, u32[]{:S(2)}, u32[]{:S(2)}) collective-permute-start(f32[1,256,256]{2,1,0:T(8,128)S(1)} %get-tuple-element.117.refs_2_), channel_id=1, source_target_pairs={{0,8},{4,12},{8,0},{12,4},{16,24},{20,28},{24,16},{28,20},{1,9},{5... | collective-permute-start | bytes 786440 | tf_op jit(solution)/shard_map/ppermute | solution.py:216
  77.6 12.7 %collective-permute-start.20 = (f32[1,256,256]{2,1,0:T(8,128)S(1)}, f32[1,256,256]{2,1,0:T(8,128)S(1)}, u32[]{:S(2)}, u32[]{:S(2)}) collective-permute-start(f32[1,256,256]{2,1,0:T(8,128)S(1)} %get-tuple-element.132.refs_2_), channel_id=1, source_target_pairs={{0,8},{4,12},{8,0},{12,4},{16,24},{20,28},{24,16},{28,20},{1,9},{5... | collective-permute-start | bytes 786440 | tf_op jit(solution)/shard_map/ppermute | solution.py:216
  88.5 16.3 %collective-permute-start.24 = (f32[1,256,256]{2,1,0:T(8,128)S(1)}, f32[1,256,256]{2,1,0:T(8,128)S(1)}, u32[]{:S(2)}, u32[]{:S(2)}) collective-permute-start(f32[1,256,256]{2,1,0:T(8,128)S(1)} %get-tuple-element.139.refs_2_), channel_id=1, source_target_pairs={{0,4},{4,0},{8,12},{12,8},{16,20},{20,16},{24,28},{28,24},{1,5},{5... | collective-permute-start | bytes 786440 | tf_op jit(solution)/shard_map/ppermute | solution.py:216
  93.2 17.1 %collective-permute-start.25 = (f32[1,256,256]{2,1,0:T(8,128)S(1)}, f32[1,256,256]{2,1,0:T(8,128)S(1)}, u32[]{:S(2)}, u32[]{:S(2)}) collective-permute-start(f32[1,256,256]{2,1,0:T(8,128)S(1)} %get-tuple-element.141.refs_2_), channel_id=1, source_target_pairs={{0,8},{4,12},{8,0},{12,4},{16,24},{20,28},{24,16},{28,20},{1,9},{5... | collective-permute-start | bytes 786440 | tf_op jit(solution)/shard_map/ppermute | solution.py:216
  94.6 18.5 %collective-permute-start.26 = (f32[1,256,256]{2,1,0:T(8,128)S(1)}, f32[1,256,256]{2,1,0:T(8,128)S(1)}, u32[]{:S(2)}, u32[]{:S(2)}) collective-permute-start(f32[1,256,256]{2,1,0:T(8,128)S(1)} %get-tuple-element.143.refs_2_), channel_id=1, source_target_pairs={{0,4},{4,0},{8,12},{12,8},{16,20},{20,16},{24,28},{28,24},{1,5},{5... | collective-permute-start | bytes 786440 | tf_op jit(solution)/shard_map/ppermute | solution.py:216
  98.4 18.5 %collective-permute-start.27 = (f32[1,256,256]{2,1,0:T(8,128)S(1)}, f32[1,256,256]{2,1,0:T(8,128)S(1)}, u32[]{:S(2)}, u32[]{:S(2)}) collective-permute-start(f32[1,256,256]{2,1,0:T(8,128)S(1)} %get-tuple-element.145.refs_2_), channel_id=1, source_target_pairs={{0,16},{4,20},{8,24},{12,28},{16,0},{20,4},{24,8},{28,12},{1,17},{... | collective-permute-start | bytes 786440 | tf_op jit(solution)/shard_map/ppermute | solution.py:216
  102.2 15.9 %collective-permute-start.28 = (f32[1,256,256]{2,1,0:T(8,128)S(1)}, f32[1,256,256]{2,1,0:T(8,128)S(1)}, u32[]{:S(2)}, u32[]{:S(2)}) collective-permute-start(f32[1,256,256]{2,1,0:T(8,128)S(1)} %get-tuple-element.148.refs_2_), channel_id=1, source_target_pairs={{0,8},{4,12},{8,0},{12,4},{16,24},{20,28},{24,16},{28,20},{1,9},{5... | collective-permute-start | bytes 786440 | tf_op jit(solution)/shard_map/ppermute | solution.py:216
  105.8 20.1 %collective-permute-start.29 = (f32[1,256,256]{2,1,0:T(8,128)S(1)}, f32[1,256,256]{2,1,0:T(8,128)S(1)}, u32[]{:S(2)}, u32[]{:S(2)}) collective-permute-start(f32[1,256,256]{2,1,0:T(8,128)S(1)} %get-tuple-element.149.refs_2_), channel_id=1, source_target_pairs={{0,8},{4,12},{8,0},{12,4},{16,24},{20,28},{24,16},{28,20},{1,9},{5... | collective-permute-start | bytes 786440 | tf_op jit(solution)/shard_map/ppermute | solution.py:216
  111.2 17.3 %collective-permute-start.30 = (f32[1,256,256]{2,1,0:T(8,128)S(1)}, f32[1,256,256]{2,1,0:T(8,128)S(1)}, u32[]{:S(2)}, u32[]{:S(2)}) collective-permute-start(f32[1,256,256]{2,1,0:T(8,128)S(1)} %get-tuple-element.151.refs_2_), channel_id=1, source_target_pairs={{0,16},{4,20},{8,24},{12,28},{16,0},{20,4},{24,8},{28,12},{1,17},{... | collective-permute-start | bytes 786440 | tf_op jit(solution)/shard_map/ppermute | solution.py:216
  114.1 17.4 %collective-permute-start.31 = (f32[1,256,256]{2,1,0:T(8,128)S(1)}, f32[1,256,256]{2,1,0:T(8,128)S(1)}, u32[]{:S(2)}, u32[]{:S(2)}) collective-permute-start(f32[1,256,256]{2,1,0:T(8,128)S(1)} %get-tuple-element.153.refs_2_), channel_id=1, source_target_pairs={{0,8},{4,12},{8,0},{12,4},{16,24},{20,28},{24,16},{28,20},{1,9},{5... | collective-permute-start | bytes 786440 | tf_op jit(solution)/shard_map/ppermute | solution.py:216
  117.9 15.8 %collective-permute-start.32 = (f32[1,256,256]{2,1,0:T(8,128)S(1)}, f32[1,256,256]{2,1,0:T(8,128)S(1)}, u32[]{:S(2)}, u32[]{:S(2)}) collective-permute-start(f32[1,256,256]{2,1,0:T(8,128)S(1)} %get-tuple-element.155.refs_2_), channel_id=1, source_target_pairs={{0,4},{4,0},{8,12},{12,8},{16,20},{20,16},{24,28},{28,24},{1,5},{5... | collective-permute-start | bytes 786440 | tf_op jit(solution)/shard_map/ppermute | solution.py:216
  126.9 17.8 %collective-permute-start.33 = (f32[1,256,256]{2,1,0:T(8,128)S(1)}, f32[1,256,256]{2,1,0:T(8,128)S(1)}, u32[]{:S(2)}, u32[]{:S(2)}) collective-permute-start(f32[1,256,256]{2,1,0:T(8,128)S(1)} %get-tuple-element.158.refs_2_), channel_id=1, source_target_pairs={{0,16},{4,20},{8,24},{12,28},{16,0},{20,4},{24,8},{28,12},{1,17},{... | collective-permute-start | bytes 786440 | tf_op jit(solution)/shard_map/ppermute | solution.py:216
  129.4 17.4 %collective-permute-start.34 = (f32[1,256,256]{2,1,0:T(8,128)S(1)}, f32[1,256,256]{2,1,0:T(8,128)S(1)}, u32[]{:S(2)}, u32[]{:S(2)}) collective-permute-start(f32[1,256,256]{2,1,0:T(8,128)S(1)} %get-tuple-element.160.refs_2_), channel_id=1, source_target_pairs={{0,4},{4,0},{8,12},{12,8},{16,20},{20,16},{24,28},{28,24},{1,5},{5... | collective-permute-start | bytes 786440 | tf_op jit(solution)/shard_map/ppermute | solution.py:216
  132.5 15.4 %collective-permute-start.35 = (f32[1,256,256]{2,1,0:T(8,128)S(1)}, f32[1,256,256]{2,1,0:T(8,128)S(1)}, u32[]{:S(2)}, u32[]{:S(2)}) collective-permute-start(f32[1,256,256]{2,1,0:T(8,128)S(1)} %get-tuple-element.162.refs_2_), channel_id=1, source_target_pairs={{0,16},{4,20},{8,24},{12,28},{16,0},{20,4},{24,8},{28,12},{1,17},{... | collective-permute-start | bytes 786440 | tf_op jit(solution)/shard_map/ppermute | solution.py:216
  134.6 15.3 %collective-permute-start.36 = (f32[1,256,256]{2,1,0:T(8,128)S(1)}, f32[1,256,256]{2,1,0:T(8,128)S(1)}, u32[]{:S(2)}, u32[]{:S(2)}) collective-permute-start(f32[1,256,256]{2,1,0:T(8,128)S(1)} %get-tuple-element.164.refs_2_), channel_id=1, source_target_pairs={{0,8},{4,12},{8,0},{12,4},{16,24},{20,28},{24,16},{28,20},{1,9},{5... | collective-permute-start | bytes 786440 | tf_op jit(solution)/shard_map/ppermute | solution.py:216
  (22 other events, 199.9 us)

commit v2 on v1

v2 whole, which is shorter than its diff:
```python
import functools

import jax
import jax.numpy as jnp
from jax import lax
from jax.experimental import pallas as pl
from jax.experimental.pallas import tpu as pltpu
from jax.sharding import PartitionSpec as P

CHUNKS = ((0, 2), (0, 2), (0, 2), (0, 2), (1, 2), (1, 2), (1, 2), (1, 2))
EIGHTHS = 8
STEPS = (
    (((3, 0),), ("across",)),
    (((0, 0),), ("near01",)),
    ((), ("near24",)),
    (((3, 1), (2, 0)), ()),
    (((1, 0), (0, 1), (6, 0)), ()),
    (((3, 2),), ()),
    (((5, 0), (2, 1), (0, 2), (7, 0)), ()),
    (((2, 2), (1, 1), (3, 3)), ("cs0",)),
    (((6, 1), (7, 1), (0, 3), (4, 0)), ("mk0", "cs1")),
    (((1, 2), (5, 1)), ("cs2",)),
    (((2, 3), (5, 2)), ("mk1", "mk2")),
    (((7, 2), (4, 1), (1, 3)), ("cs3",)),
    (((3, 4), (4, 2), (5, 3)), ("cs4",)),
    (((6, 2), (0, 4), (7, 3), (5, 4)), ("mk3",)),
    (((4, 3),), ()),
    (((7, 4), (2, 4), (3, 5)), ()),
    (((1, 4),), ()),
    (((6, 3), (0, 5), (4, 4)), ()),
    (((5, 5), (7, 5), (6, 4), (1, 5)), ("mk4",)),
    (((2, 5), (4, 5)), ()),
    (((6, 5),), ()),
)
NEAR = {"near01": (0, 2), "near24": (2, 5)}
ACROSS = "across"
SHARE = {"cs0": 0, "cs1": 1, "cs2": 2, "cs3": 3, "cs4": 4}
FAR = {"mk0": "cs0", "mk1": "cs1", "mk2": "cs2", "mk3": "cs3", "mk4": "cs4"}


def partner_route(count, mask):
    return [(low, low ^ mask) for low in range(count) if low ^ mask < count]


def two_terms(values):
    high = values.astype(jnp.bfloat16)
    return high, (values - high.astype(jnp.float32)).astype(jnp.bfloat16)


def product(table, first, second):
    high = jnp.concatenate([first[0], second[0]], axis=0)
    low = jnp.concatenate([first[1], second[1]], axis=0)
    dot = functools.partial(jnp.dot, preferred_element_type=jnp.float32)
    return dot(table[0], high) + (dot(table[0], low) + dot(table[1], high))


class Operands:
    def __init__(self):
        self.arrays, self.places = [], {}

    def add(self, array):
        if id(array) not in self.places:
            self.places[id(array)] = len(self.arrays)
            self.arrays.append(array)
        return self.places[id(array)]


def step(weight, blocks, merged, state, tables, rows, tasks, work, chunks, bit_count):
    half = blocks.shape[2] // 2
    stages = blocks.shape[0]
    operands, held, taken = Operands(), {}, {}
    for index, stage in tasks:
        if stage > 0:
            sent, came = state[index]
            held[index] = [(operands.add(sent[0]), sent[1]), (operands.add(came[0]), came[1])]
            key = (chunks[index][0], stage - 1)
            if key in tables:
                taken[key] = operands.add(tables[key])

    making, handing = [], []
    for name in work:
        if name in NEAR:
            mine, other = [operands.add(rows[n]) for n in ("blocks", "cores")]
            making += [((0, k), (mine, k), (other, k)) for k in range(*NEAR[name])]
        elif name in FAR:
            k = SHARE[FAR[name]]
            mine, other = operands.add(rows[ACROSS]), operands.add(rows[FAR[name]])
            making.append(((1, k), (mine, k), (other, 0)))
        elif name == ACROSS:
            handing.append((name, None, 0, stages))
        else:
            handing.append((name, operands.add(rows[ACROSS]), SHARE[name], SHARE[name] + 1))

    arrays, slots = [], {}
    for index, stage in tasks:
        if stage < stages:
            way = stage % bit_count
            for at, (width, other, total) in enumerate(arrays):
                if (width, other) == (chunks[index][2], way):
                    break
            else:
                at, total = len(arrays), 0
                arrays.append(None)
            arrays[at] = (chunks[index][2], way, total + 1)
            slots[index] = (at, total)
    entering = [index for index, stage in tasks if stage == 0]
    leaving = [index for index, stage in tasks if stage == stages]
    whole = {}
    if entering:
        whole["weight"] = weight
    if any(source is None for _, source, _, _ in handing):
        whole["blocks"] = blocks
    if merged is not None:
        whole["merged"] = merged

    def kernel(*refs):
        whole_refs, refs = dict(zip(whole, refs)), refs[len(whole) :]
        ins, refs = refs[: len(operands.arrays)], refs[len(operands.arrays) :]
        merged_ref, refs = refs[0], refs[1:]
        sends, refs = refs[: len(arrays)], refs[len(arrays) :]
        handed, refs = refs[: len(handing)], refs[len(handing) :]
        made, refs = dict(zip([key for key, _, _ in making], refs)), refs[len(making) :]
        result_of, sems = dict(zip(leaving, refs)), refs[len(leaving)]
        col = lax.axis_index("col")
        own_half, low_core = col // 2, col % 2 == 0

        def region(ref, index):
            half_block, column, width = chunks[index]
            first = own_half if half_block == 0 else 1 - own_half
            rows_of = pl.ds(pl.multiple_of(first * half, half), half)
            return ref.at[rows_of, pl.ds(column, width)]

        moves = []

        def move(source, target):
            moves.append(pltpu.make_async_copy(source, target, sems.at[len(moves)]))
            moves[-1].start()

        for index in entering:
            at, slot = slots[index]
            move(region(whole_refs["weight"], index), sends[at].at[slot])
        for (_, source, first, last), target in zip(handing, handed):
            ref = whole_refs["blocks"] if source is None else ins[source]
            move(ref.at[pl.ds(first, last - first)], target)
        for key, mine, other in making:
            one, two = [ins[at][row] for at, row in (mine, other)]
            depth = one.shape[0]
            for side in range(2):
                low, high = (one, two) if side == 0 else (two, one)
                span = pl.ds(side * depth, depth)
                made[key][0, span], made[key][1, span] = two_terms(jnp.where(low_core, low, high))
        for index, stage in tasks:
            if stage > 0:
                mine, theirs = [two_terms(ins[at][slot]) for at, slot in held[index]]
                if stage == stages:
                    target = result_of[index]
                else:
                    at, slot = slots[index]
                    target = sends[at].at[slot]
                key = (chunks[index][0], stage - 1)
                target[...] = product(ins[taken[key]] if key in taken else made[key], mine, theirs)
                if stage == stages:
                    move(target, region(merged_ref, index))
        for each in moves:
            each.wait()

    shape = lambda *dims: jax.ShapeDtypeStruct(dims, jnp.float32)
    outs = [shape(units, half, width) for width, _, units in arrays]
    outs += [shape(last - first, *blocks.shape[1:]) for _, _, first, last in handing]
    outs += [jax.ShapeDtypeStruct((2, half, 2 * half), jnp.bfloat16)] * len(making)
    hbm = pl.BlockSpec(memory_space=pltpu.HBM)
    vmem = pl.BlockSpec(memory_space=pltpu.VMEM)
    room = 62 if merged is None else 40
    merged, *new = pl.pallas_call(
        kernel,
        out_shape=[shape(*weight.shape)] + outs,
        in_specs=[hbm] * len(whole) + [vmem] * len(operands.arrays),
        out_specs=[hbm] + [vmem] * len(outs),
        scratch_shapes=[pltpu.VMEM((half, chunks[index][2]), jnp.float32) for index in leaving]
        + [pltpu.SemaphoreType.DMA((len(entering) + len(handing) + len(leaving) + 1,))],
        input_output_aliases={len(whole) - 1: 0} if merged is not None else {},
        compiler_params=pltpu.CompilerParams(vmem_limit_bytes=room * 2**20),
        cost_estimate=pl.CostEstimate(flops=1, bytes_accessed=1, transcendentals=0),
    )(*whole.values(), *operands.arrays)
    sent, new = new[: len(arrays)], new[len(arrays) :]
    handed, new = dict(zip([hand[0] for hand in handing], new)), new[len(handing) :]
    made = dict(zip([key for key, _, _ in making], new))
    ways = [way for _, way, _ in arrays]
    return merged, sent, ways, slots, handed, made


def pipelined(weight, blocks):
    count, columns = lax.axis_size("row"), lax.axis_size("col")
    bit_count = count.bit_length() - 1
    from_core = lambda array: lax.ppermute(array, "col", partner_route(columns, 1))
    from_across = lambda array: lax.ppermute(array, "col", partner_route(columns, 2))
    chunks, column = [], [0, 0]
    for half_block, eighths in CHUNKS:
        width = weight.shape[1] * eighths // EIGHTHS
        chunks.append((half_block, column[half_block], width))
        column[half_block] += width
    rows = {"blocks": blocks, "cores": from_core(blocks)}
    merged, state, tables = None, {}, {}
    for tasks, work in STEPS:
        merged, sent, ways, slots, handed, made = step(
            weight, blocks, merged, state, tables, rows, tasks, work, chunks, bit_count
        )
        tables.update(made)
        came = [
            lax.ppermute(array, "row", partner_route(count, 1 << way))
            for array, way in zip(sent, ways)
        ]
        for index, (at, slot) in slots.items():
            state[index] = ((sent[at], slot), (came[at], slot))
        for name, array in handed.items():
            rows[name] = from_across(array) if name == ACROSS else from_core(array)
    return merged


def plain(weight, blocks):
    count = lax.axis_size("row")
    bit_count = count.bit_length() - 1
    factors = blocks.shape[0]
    half = blocks.shape[2] // 2
    halves = weight.shape[0] // half
    tables = [lax.all_gather(blocks[k], "col", axis=0, tiled=True) for k in range(factors)]
    bands = []
    for t in range(halves):
        rows = slice(t * half, (t + 1) * half)
        held = weight[rows]
        for factor in range(factors):
            table = tables[factor][rows]
            partner = lax.ppermute(held, "row", partner_route(count, 1 << factor % bit_count))
            dot = functools.partial(jnp.dot, precision=lax.Precision.HIGHEST)
            held = dot(table[:, :half], held) + dot(table[:, half:], partner)
        bands.append(held)
    return jnp.concatenate(bands, axis=0)


def body(weight, blocks):
    fits = lax.axis_size("row") == 8 and lax.axis_size("col") == 4 and blocks.shape[0] == 5
    fits = fits and weight.shape[0] == blocks.shape[2] == 4 * blocks.shape[1]
    fits = fits and weight.shape[1] % (128 * EIGHTHS) == 0
    return (pipelined if fits else plain)(weight, blocks)


def solution(mesh):
    return jax.shard_map(
        body,
        mesh=mesh,
        in_specs=(P("row", "col"), P(None, ("row", "col"), None)),
        out_specs=P("row", "col"),
        check_vma=False,
    )
```

time: 167 us -> 166 us (level); the launches traced: 167 us -> 164 us
  Pallas kernels: 46.1 us -> 22 us
  waiting for transfers between devices: 63.6 us -> 87.1 us
  starting transfers between devices: 56.4 us -> 52.5 us
    pallas_call x39 -> x21, Pallas kernels: 46.1 us -> 22 us  [step(): pl.pallas_call(kernel, out_shape=[shape(*weight.shape)] + outs, in_specs=...]
    ppermute x40 -> x34, waiting for transfers between devices: 63.6 us -> 87.1 us  [pipelined(): lax.ppermute(array, 'row', partner_route(count, 1 << way))]
    ppermute x40 -> x34, starting transfers between devices: 54.1 us -> 48.7 us  [pipelined(): lax.ppermute(array, 'row', partner_route(count, 1 << way))]
    ppermute x2 -> x7, starting transfers between devices: 2.29 us -> 3.72 us  [the longest x1 2.68 us: pipelined(): lax.ppermute(array, 'col', partner_route(columns, 2))]
  transfers between devices with their start and end apart: 42 -> 41, of which waited for: 18 -> 20; matrix products, arithmetic and copies ran while one was open for 0% -> 0% of each run, Pallas kernels for 25% -> 13%
where the time goes in v2:
time: 166 us; the launch traced here: 164 us
  waiting for transfers between devices  87.1 us (52%)
  starting transfers between devices  52.5 us (32%)
  Pallas kernels  22 us (13%)
    ppermute x34, waiting for transfers between devices, pipelined(): lax.ppermute(array, 'row', partner_route(count, 1 << way))  87.1 us
    ppermute x34, starting transfers between devices, pipelined(): lax.ppermute(array, 'row', partner_route(count, 1 << way))  48.7 us
    pallas_call x21, Pallas kernels, step(): pl.pallas_call(kernel, out_shape=[shape(*weight.shape)] + outs, in_specs=...  22 us
  transfers between devices with their start and end apart: 41, of which 20 were waited for; matrix products, arithmetic and copies ran while one was open for 0% of the time, Pallas kernels for 13%

profile of v2, /device:TPU:0, one launch (start us, length us, event | category | flops | bytes accessed | tf_op | source)
XLA Modules:
  0.0 163.5 jit_solution(8777481933673980601)
XLA Ops:
  0.5 2.6 %shard_map.28 = (f32[512,1024]{1,0:T(8,128)}, f32[1,256,256]{2,1,0:T(8,128)}, f32[5,128,512]{2,1,0:T(8,128)}) custom-call(f32[512,1024]{1,0:T(8,128)} %refs_0_.11, f32[5,128,512]{2,1,0:T(8,128)} %refs_1_.3), custom_call_target="tpu_custom_call" | custom-call | flops 1 | bytes 1 | tf_op jit(solution)/shard_map/pallas_call | solution.py:174
  3.1 2.7 %collective-permute-start.9 = (f32[5,128,512]{2,1,0:T(8,128)}, f32[5,128,512]{2,1,0:T(8,128)S(1)}, u32[]{:S(2)}, u32[]{:S(2)}) collective-permute-start(f32[5,128,512]{2,1,0:T(8,128)} %get-tuple-element.92), channel_id=1, source_target_pairs={{0,2},{1,3},{2,0},{3,1},{4,6},{5,7},{6,4},{7,5},{8,10},{9,11},{10,... | collective-permute-start | bytes 3932168 | tf_op jit(solution)/shard_map/ppermute | solution.py:196
  24.7 2.7 %collective-permute-start.8 = (f32[1,256,256]{2,1,0:T(8,128)S(1)}, f32[1,256,256]{2,1,0:T(8,128)S(1)}, u32[]{:S(2)}, u32[]{:S(2)}) collective-permute-start(f32[1,256,256]{2,1,0:T(8,128)S(1)} %get-tuple-element.90.refs_7_), channel_id=1, source_target_pairs={{0,16},{4,20},{8,24},{12,28},{16,0},{20,4},{24,8},{28,12},{1,17},{... | collective-permute-start | bytes 786440 | tf_op jit(solution)/shard_map/ppermute | solution.py:210
  27.4 5.4 %collective-permute-done.5.refs_6_ = f32[1,256,256]{2,1,0:T(8,128)S(1)} collective-permute-done((f32[1,256,256]{2,1,0:T(8,128)S(1)}, f32[1,256,256]{2,1,0:T(8,128)S(1)}, u32[]{:S(2)}, u32[]{:S(2)}) %collective-permute-start.5) | collective-permute-done | bytes 262176 | tf_op jit(solution)/shard_map/ppermute | solution.py:210
  35.8 2.8 %collective-permute-start.11 = (f32[1,256,256]{2,1,0:T(8,128)S(1)}, f32[1,256,256]{2,1,0:T(8,128)S(1)}, u32[]{:S(2)}, u32[]{:S(2)}) collective-permute-start(f32[1,256,256]{2,1,0:T(8,128)S(1)} %get-tuple-element.95.refs_6_), channel_id=1, source_target_pairs={{0,16},{4,20},{8,24},{12,28},{16,0},{20,4},{24,8},{28,12},{1,17},{... | collective-permute-start | bytes 786440 | tf_op jit(solution)/shard_map/ppermute | solution.py:210
  38.6 3.5 %collective-permute-done.6.refs_2_ = f32[1,256,256]{2,1,0:T(8,128)S(1)} collective-permute-done((f32[1,256,256]{2,1,0:T(8,128)S(1)}, f32[1,256,256]{2,1,0:T(8,128)S(1)}, u32[]{:S(2)}, u32[]{:S(2)}) %collective-permute-start.6) | collective-permute-done | bytes 262176 | tf_op jit(solution)/shard_map/ppermute | solution.py:210
  44.9 6.6 %collective-permute-done.11.refs_7_ = f32[1,256,256]{2,1,0:T(8,128)S(1)} collective-permute-done((f32[1,256,256]{2,1,0:T(8,128)S(1)}, f32[1,256,256]{2,1,0:T(8,128)S(1)}, u32[]{:S(2)}, u32[]{:S(2)}) %collective-permute-start.11) | collective-permute-done | bytes 262176 | tf_op jit(solution)/shard_map/ppermute | solution.py:210
  52.3 5.1 %collective-permute-done.13.refs_2_ = f32[1,256,256]{2,1,0:T(8,128)S(1)} collective-permute-done((f32[1,256,256]{2,1,0:T(8,128)S(1)}, f32[1,256,256]{2,1,0:T(8,128)S(1)}, u32[]{:S(2)}, u32[]{:S(2)}) %collective-permute-start.13) | collective-permute-done | bytes 262176 | tf_op jit(solution)/shard_map/ppermute | solution.py:210
  63.0 4.3 %collective-permute-done.15.refs_5_ = f32[1,256,256]{2,1,0:T(8,128)S(1)} collective-permute-done((f32[1,256,256]{2,1,0:T(8,128)S(1)}, f32[1,256,256]{2,1,0:T(8,128)S(1)}, u32[]{:S(2)}, u32[]{:S(2)}) %collective-permute-start.15) | collective-permute-done | bytes 262176 | tf_op jit(solution)/shard_map/ppermute | solution.py:210
  70.8 2.5 %collective-permute-start.23 = (f32[1,256,256]{2,1,0:T(8,128)S(1)}, f32[1,256,256]{2,1,0:T(8,128)S(1)}, u32[]{:S(2)}, u32[]{:S(2)}) collective-permute-start(f32[1,256,256]{2,1,0:T(8,128)S(1)} %get-tuple-element.114.refs_7_), channel_id=1, source_target_pairs={{0,16},{4,20},{8,24},{12,28},{16,0},{20,4},{24,8},{28,12},{1,17},{... | collective-permute-start | bytes 786440 | tf_op jit(solution)/shard_map/ppermute | solution.py:210
  73.4 15.4 %collective-permute-done.20.refs_8_ = f32[1,256,256]{2,1,0:T(8,128)S(1)} collective-permute-done((f32[1,256,256]{2,1,0:T(8,128)S(1)}, f32[1,256,256]{2,1,0:T(8,128)S(1)}, u32[]{:S(2)}, u32[]{:S(2)}) %collective-permute-start.20) | collective-permute-done | bytes 262176 | tf_op jit(solution)/shard_map/ppermute | solution.py:210
  89.9 3.5 %collective-permute-start.24 = (f32[1,256,256]{2,1,0:T(8,128)S(1)}, f32[1,256,256]{2,1,0:T(8,128)S(1)}, u32[]{:S(2)}, u32[]{:S(2)}) collective-permute-start(f32[1,256,256]{2,1,0:T(8,128)S(1)} %get-tuple-element.117.refs_7_), channel_id=1, source_target_pairs={{0,16},{4,20},{8,24},{12,28},{16,0},{20,4},{24,8},{28,12},{1,17},{... | collective-permute-start | bytes 786440 | tf_op jit(solution)/shard_map/ppermute | solution.py:210
  93.4 3.8 %collective-permute-done.23.refs_8_ = f32[1,256,256]{2,1,0:T(8,128)S(1)} collective-permute-done((f32[1,256,256]{2,1,0:T(8,128)S(1)}, f32[1,256,256]{2,1,0:T(8,128)S(1)}, u32[]{:S(2)}, u32[]{:S(2)}) %collective-permute-start.23) | collective-permute-done | bytes 262176 | tf_op jit(solution)/shard_map/ppermute | solution.py:210
  97.2 2.8 %collective-permute-done.22.refs_5_ = f32[1,256,256]{2,1,0:T(8,128)S(1)} collective-permute-done((f32[1,256,256]{2,1,0:T(8,128)S(1)}, f32[1,256,256]{2,1,0:T(8,128)S(1)}, u32[]{:S(2)}, u32[]{:S(2)}) %collective-permute-start.22) | collective-permute-done | bytes 262176 | tf_op jit(solution)/shard_map/ppermute | solution.py:210
  101.1 2.8 %collective-permute-start.25 = (f32[1,256,256]{2,1,0:T(8,128)S(1)}, f32[1,256,256]{2,1,0:T(8,128)S(1)}, u32[]{:S(2)}, u32[]{:S(2)}) collective-permute-start(f32[1,256,256]{2,1,0:T(8,128)S(1)} %get-tuple-element.118.refs_10_), channel_id=1, source_target_pairs={{0,4},{4,0},{8,12},{12,8},{16,20},{20,16},{24,28},{28,24},{1,5},{5... | collective-permute-start | bytes 786440 | tf_op jit(solution)/shard_map/ppermute | solution.py:210
  104.1 2.7 %collective-permute-start.30 = (f32[1,256,256]{2,1,0:T(8,128)S(1)}, f32[1,256,256]{2,1,0:T(8,128)S(1)}, u32[]{:S(2)}, u32[]{:S(2)}) collective-permute-start(f32[1,256,256]{2,1,0:T(8,128)S(1)} %get-tuple-element.126.refs_7_), channel_id=1, source_target_pairs={{0,8},{4,12},{8,0},{12,4},{16,24},{20,28},{24,16},{28,20},{1,9},{5... | collective-permute-start | bytes 786440 | tf_op jit(solution)/shard_map/ppermute | solution.py:210
  106.8 4.3 %collective-permute-done.25.refs_11_ = f32[1,256,256]{2,1,0:T(8,128)S(1)} collective-permute-done((f32[1,256,256]{2,1,0:T(8,128)S(1)}, f32[1,256,256]{2,1,0:T(8,128)S(1)}, u32[]{:S(2)}, u32[]{:S(2)}) %collective-permute-start.25) | collective-permute-done | bytes 262176 | tf_op jit(solution)/shard_map/ppermute | solution.py:210
  114.3 2.8 %collective-permute-done.27.refs_2_ = f32[1,256,256]{2,1,0:T(8,128)S(1)} collective-permute-done((f32[1,256,256]{2,1,0:T(8,128)S(1)}, f32[1,256,256]{2,1,0:T(8,128)S(1)}, u32[]{:S(2)}, u32[]{:S(2)}) %collective-permute-start.27) | collective-permute-done | bytes 262176 | tf_op jit(solution)/shard_map/ppermute | solution.py:210
  124.2 3.8 %collective-permute-done.31.refs_2_ = f32[1,256,256]{2,1,0:T(8,128)S(1)} collective-permute-done((f32[1,256,256]{2,1,0:T(8,128)S(1)}, f32[1,256,256]{2,1,0:T(8,128)S(1)}, u32[]{:S(2)}, u32[]{:S(2)}) %collective-permute-start.31) | collective-permute-done | bytes 262176 | tf_op jit(solution)/shard_map/ppermute | solution.py:210
  128.4 3.9 %collective-permute-done.34.refs_8_ = f32[1,256,256]{2,1,0:T(8,128)S(1)} collective-permute-done((f32[1,256,256]{2,1,0:T(8,128)S(1)}, f32[1,256,256]{2,1,0:T(8,128)S(1)}, u32[]{:S(2)}, u32[]{:S(2)}) %collective-permute-start.34) | collective-permute-done | bytes 262176 | tf_op jit(solution)/shard_map/ppermute | solution.py:210
  136.3 5.1 %collective-permute-start.36 = (f32[1,256,256]{2,1,0:T(8,128)S(1)}, f32[1,256,256]{2,1,0:T(8,128)S(1)}, u32[]{:S(2)}, u32[]{:S(2)}) collective-permute-start(f32[1,256,256]{2,1,0:T(8,128)S(1)} %get-tuple-element.136.refs_5_), channel_id=1, source_target_pairs={{0,4},{4,0},{8,12},{12,8},{16,20},{20,16},{24,28},{28,24},{1,5},{5... | collective-permute-start | bytes 786440 | tf_op jit(solution)/shard_map/ppermute | solution.py:210
  141.7 9.9 %collective-permute-done.37.refs_9_ = f32[1,256,256]{2,1,0:T(8,128)S(1)} collective-permute-done((f32[1,256,256]{2,1,0:T(8,128)S(1)}, f32[1,256,256]{2,1,0:T(8,128)S(1)}, u32[]{:S(2)}, u32[]{:S(2)}) %collective-permute-start.37) | collective-permute-done | bytes 262176 | tf_op jit(solution)/shard_map/ppermute | solution.py:210
  154.4 2.9 %collective-permute-done.39.refs_5_ = f32[1,256,256]{2,1,0:T(8,128)S(1)} collective-permute-done((f32[1,256,256]{2,1,0:T(8,128)S(1)}, f32[1,256,256]{2,1,0:T(8,128)S(1)}, u32[]{:S(2)}, u32[]{:S(2)}) %collective-permute-start.39) | collective-permute-done | bytes 262176 | tf_op jit(solution)/shard_map/ppermute | solution.py:210
  158.7 3.6 %collective-permute-done.40.refs_2_ = f32[1,256,256]{2,1,0:T(8,128)S(1)} collective-permute-done((f32[1,256,256]{2,1,0:T(8,128)S(1)}, f32[1,256,256]{2,1,0:T(8,128)S(1)}, u32[]{:S(2)}, u32[]{:S(2)}) %collective-permute-start.40) | collective-permute-done | bytes 262176 | tf_op jit(solution)/shard_map/ppermute | solution.py:210
  (87 shorter events, 57.6 us)
Async XLA Ops:
  3.1 32.7 %collective-permute-start.9 = (f32[5,128,512]{2,1,0:T(8,128)}, f32[5,128,512]{2,1,0:T(8,128)S(1)}, u32[]{:S(2)}, u32[]{:S(2)}) collective-permute-start(f32[5,128,512]{2,1,0:T(8,128)} %get-tuple-element.92), channel_id=1, source_target_pairs={{0,2},{1,3},{2,0},{3,1},{4,6},{5,7},{6,4},{7,5},{8,10},{9,11},{10,... | collective-permute-start | bytes 3932168 | tf_op jit(solution)/shard_map/ppermute | solution.py:196
  22.8 19.3 %collective-permute-start.7 = (f32[2,256,256]{2,1,0:T(8,128)S(1)}, f32[2,256,256]{2,1,0:T(8,128)S(1)}, u32[]{:S(2)}, u32[]{:S(2)}) collective-permute-start(f32[2,256,256]{2,1,0:T(8,128)S(1)} %get-tuple-element.89.refs_4_.refs_2_), channel_id=1, source_target_pairs={{0,4},{4,0},{8,12},{12,8},{16,20},{20,16},{24,28},{28,24},{1,5},{5... | collective-permute-start | bytes 1572872 | tf_op jit(solution)/shard_map/ppermute | solution.py:210
  24.7 13.9 %collective-permute-start.8 = (f32[1,256,256]{2,1,0:T(8,128)S(1)}, f32[1,256,256]{2,1,0:T(8,128)S(1)}, u32[]{:S(2)}, u32[]{:S(2)}) collective-permute-start(f32[1,256,256]{2,1,0:T(8,128)S(1)} %get-tuple-element.90.refs_7_), channel_id=1, source_target_pairs={{0,16},{4,20},{8,24},{12,28},{16,0},{20,4},{24,8},{28,12},{1,17},{... | collective-permute-start | bytes 786440 | tf_op jit(solution)/shard_map/ppermute | solution.py:210
  33.5 17.9 %collective-permute-start.10 = (f32[2,256,256]{2,1,0:T(8,128)S(1)}, f32[2,256,256]{2,1,0:T(8,128)S(1)}, u32[]{:S(2)}, u32[]{:S(2)}) collective-permute-start(f32[2,256,256]{2,1,0:T(8,128)S(1)} %get-tuple-element.94.refs_4_), channel_id=1, source_target_pairs={{0,4},{4,0},{8,12},{12,8},{16,20},{20,16},{24,28},{28,24},{1,5},{5... | collective-permute-start | bytes 1572872 | tf_op jit(solution)/shard_map/ppermute | solution.py:210
  35.8 15.6 %collective-permute-start.11 = (f32[1,256,256]{2,1,0:T(8,128)S(1)}, f32[1,256,256]{2,1,0:T(8,128)S(1)}, u32[]{:S(2)}, u32[]{:S(2)}) collective-permute-start(f32[1,256,256]{2,1,0:T(8,128)S(1)} %get-tuple-element.95.refs_6_), channel_id=1, source_target_pairs={{0,16},{4,20},{8,24},{12,28},{16,0},{20,4},{24,8},{28,12},{1,17},{... | collective-permute-start | bytes 786440 | tf_op jit(solution)/shard_map/ppermute | solution.py:210
  43.0 14.3 %collective-permute-start.13 = (f32[1,256,256]{2,1,0:T(8,128)S(1)}, f32[1,256,256]{2,1,0:T(8,128)S(1)}, u32[]{:S(2)}, u32[]{:S(2)}) collective-permute-start(f32[1,256,256]{2,1,0:T(8,128)S(1)} %get-tuple-element.98.refs_1_), channel_id=1, source_target_pairs={{0,8},{4,12},{8,0},{12,4},{16,24},{20,28},{24,16},{28,20},{1,9},{5... | collective-permute-start | bytes 786440 | tf_op jit(solution)/shard_map/ppermute | solution.py:210
  43.1 19.4 %collective-permute-start.14 = (f32[1,256,256]{2,1,0:T(8,128)S(1)}, f32[1,256,256]{2,1,0:T(8,128)S(1)}, u32[]{:S(2)}, u32[]{:S(2)}) collective-permute-start(f32[1,256,256]{2,1,0:T(8,128)S(1)} %get-tuple-element.101.refs_1_), channel_id=1, source_target_pairs={{0,16},{4,20},{8,24},{12,28},{16,0},{20,4},{24,8},{28,12},{1,17},{... | collective-permute-start | bytes 786440 | tf_op jit(solution)/shard_map/ppermute | solution.py:210
  58.1 30.7 %collective-permute-start.18 = (f32[2,256,256]{2,1,0:T(8,128)S(1)}, f32[2,256,256]{2,1,0:T(8,128)S(1)}, u32[]{:S(2)}, u32[]{:S(2)}) collective-permute-start(f32[2,256,256]{2,1,0:T(8,128)S(1)} %get-tuple-element.106.refs_1_), channel_id=1, source_target_pairs={{0,8},{4,12},{8,0},{12,4},{16,24},{20,28},{24,16},{28,20},{1,9},{5... | collective-permute-start | bytes 1572872 | tf_op jit(solution)/shard_map/ppermute | solution.py:210
  60.1 28.7 %collective-permute-start.19 = (f32[2,256,256]{2,1,0:T(8,128)S(1)}, f32[2,256,256]{2,1,0:T(8,128)S(1)}, u32[]{:S(2)}, u32[]{:S(2)}) collective-permute-start(f32[2,256,256]{2,1,0:T(8,128)S(1)} %get-tuple-element.108.refs_4_), channel_id=1, source_target_pairs={{0,4},{4,0},{8,12},{12,8},{16,20},{20,16},{24,28},{28,24},{1,5},{5... | collective-permute-start | bytes 1572872 | tf_op jit(solution)/shard_map/ppermute | solution.py:210
  67.3 21.5 %collective-permute-start.20 = (f32[1,256,256]{2,1,0:T(8,128)S(1)}, f32[1,256,256]{2,1,0:T(8,128)S(1)}, u32[]{:S(2)}, u32[]{:S(2)}) collective-permute-start(f32[1,256,256]{2,1,0:T(8,128)S(1)} %get-tuple-element.109.refs_7_), channel_id=1, source_target_pairs={{0,16},{4,20},{8,24},{12,28},{16,0},{20,4},{24,8},{28,12},{1,17},{... | collective-permute-start | bytes 786440 | tf_op jit(solution)/shard_map/ppermute | solution.py:210
  69.1 24.3 %collective-permute-start.21 = (f32[1,256,256]{2,1,0:T(8,128)S(1)}, f32[1,256,256]{2,1,0:T(8,128)S(1)}, u32[]{:S(2)}, u32[]{:S(2)}) collective-permute-start(f32[1,256,256]{2,1,0:T(8,128)S(1)} %get-tuple-element.111.refs_1_), channel_id=1, source_target_pairs={{0,4},{4,0},{8,12},{12,8},{16,20},{20,16},{24,28},{28,24},{1,5},{5... | collective-permute-start | bytes 786440 | tf_op jit(solution)/shard_map/ppermute | solution.py:210
  70.8 26.4 %collective-permute-start.23 = (f32[1,256,256]{2,1,0:T(8,128)S(1)}, f32[1,256,256]{2,1,0:T(8,128)S(1)}, u32[]{:S(2)}, u32[]{:S(2)}) collective-permute-start(f32[1,256,256]{2,1,0:T(8,128)S(1)} %get-tuple-element.114.refs_7_), channel_id=1, source_target_pairs={{0,16},{4,20},{8,24},{12,28},{16,0},{20,4},{24,8},{28,12},{1,17},{... | collective-permute-start | bytes 786440 | tf_op jit(solution)/shard_map/ppermute | solution.py:210
  89.9 14.2 %collective-permute-start.24 = (f32[1,256,256]{2,1,0:T(8,128)S(1)}, f32[1,256,256]{2,1,0:T(8,128)S(1)}, u32[]{:S(2)}, u32[]{:S(2)}) collective-permute-start(f32[1,256,256]{2,1,0:T(8,128)S(1)} %get-tuple-element.117.refs_7_), channel_id=1, source_target_pairs={{0,16},{4,20},{8,24},{12,28},{16,0},{20,4},{24,8},{28,12},{1,17},{... | collective-permute-start | bytes 786440 | tf_op jit(solution)/shard_map/ppermute | solution.py:210
  93.4 13.4 %collective-permute-start.26 = (f32[1,128,512]{2,1,0:T(8,128)S(1)}, f32[1,128,512]{2,1,0:T(8,128)S(1)}, u32[]{:S(2)}, u32[]{:S(2)}) collective-permute-start(f32[1,128,512]{2,1,0:T(8,128)S(1)} %get-tuple-element.119), channel_id=1, source_target_pairs={{0,1},{1,0},{2,3},{3,2},{4,5},{5,4},{6,7},{7,6},{8,9},{9,8},{10,11... | collective-permute-start | bytes 786440 | tf_op jit(solution)/shard_map/ppermute | solution.py:195
  103.9 13.9 %collective-permute-start.29 = (f32[1,256,256]{2,1,0:T(8,128)S(1)}, f32[1,256,256]{2,1,0:T(8,128)S(1)}, u32[]{:S(2)}, u32[]{:S(2)}) collective-permute-start(f32[1,256,256]{2,1,0:T(8,128)S(1)} %get-tuple-element.125.refs_4_), channel_id=1, source_target_pairs={{0,4},{4,0},{8,12},{12,8},{16,20},{20,16},{24,28},{28,24},{1,5},{5... | collective-permute-start | bytes 786440 | tf_op jit(solution)/shard_map/ppermute | solution.py:210
  104.1 15.5 %collective-permute-start.30 = (f32[1,256,256]{2,1,0:T(8,128)S(1)}, f32[1,256,256]{2,1,0:T(8,128)S(1)}, u32[]{:S(2)}, u32[]{:S(2)}) collective-permute-start(f32[1,256,256]{2,1,0:T(8,128)S(1)} %get-tuple-element.126.refs_7_), channel_id=1, source_target_pairs={{0,8},{4,12},{8,0},{12,4},{16,24},{20,28},{24,16},{28,20},{1,9},{5... | collective-permute-start | bytes 786440 | tf_op jit(solution)/shard_map/ppermute | solution.py:210
  114.3 20.5 %collective-permute-start.33 = (f32[2,256,256]{2,1,0:T(8,128)S(1)}, f32[2,256,256]{2,1,0:T(8,128)S(1)}, u32[]{:S(2)}, u32[]{:S(2)}) collective-permute-start(f32[2,256,256]{2,1,0:T(8,128)S(1)} %get-tuple-element.132.refs_4_.refs_1_), channel_id=1, source_target_pairs={{0,8},{4,12},{8,0},{12,4},{16,24},{20,28},{24,16},{28,20},{1,9},{5... | collective-permute-start | bytes 1572872 | tf_op jit(solution)/shard_map/ppermute | solution.py:210
  117.8 14.4 %collective-permute-start.34 = (f32[1,256,256]{2,1,0:T(8,128)S(1)}, f32[1,256,256]{2,1,0:T(8,128)S(1)}, u32[]{:S(2)}, u32[]{:S(2)}) collective-permute-start(f32[1,256,256]{2,1,0:T(8,128)S(1)} %get-tuple-element.133.refs_7_), channel_id=1, source_target_pairs={{0,4},{4,0},{8,12},{12,8},{16,20},{20,16},{24,28},{28,24},{1,5},{5... | collective-permute-start | bytes 786440 | tf_op jit(solution)/shard_map/ppermute | solution.py:210
  119.6 13.6 %collective-permute-start.32 = (f32[1,256,256]{2,1,0:T(8,128)S(1)}, f32[1,256,256]{2,1,0:T(8,128)S(1)}, u32[]{:S(2)}, u32[]{:S(2)}) collective-permute-start(f32[1,256,256]{2,1,0:T(8,128)S(1)} %get-tuple-element.131.refs_1_), channel_id=1, source_target_pairs={{0,16},{4,20},{8,24},{12,28},{16,0},{20,4},{24,8},{28,12},{1,17},{... | collective-permute-start | bytes 786440 | tf_op jit(solution)/shard_map/ppermute | solution.py:210
  123.9 27.8 %collective-permute-start.35 = (f32[2,256,256]{2,1,0:T(8,128)S(1)}, f32[2,256,256]{2,1,0:T(8,128)S(1)}, u32[]{:S(2)}, u32[]{:S(2)}) collective-permute-start(f32[2,256,256]{2,1,0:T(8,128)S(1)} %get-tuple-element.135.refs_3_.refs_1_), channel_id=1, source_target_pairs={{0,8},{4,12},{8,0},{12,4},{16,24},{20,28},{24,16},{28,20},{1,9},{5... | collective-permute-start | bytes 1572872 | tf_op jit(solution)/shard_map/ppermute | solution.py:210
  128.0 13.7 %collective-permute-start.38 = (f32[1,128,512]{2,1,0:T(8,128)S(1)}, f32[1,128,512]{2,1,0:T(8,128)S(1)}, u32[]{:S(2)}, u32[]{:S(2)}) collective-permute-start(f32[1,128,512]{2,1,0:T(8,128)S(1)} %get-tuple-element.138), channel_id=1, source_target_pairs={{0,1},{1,0},{2,3},{3,2},{4,5},{5,4},{6,7},{7,6},{8,9},{9,8},{10,11... | collective-permute-start | bytes 786440 | tf_op jit(solution)/shard_map/ppermute | solution.py:195
  132.3 19.3 %collective-permute-start.37 = (f32[1,256,256]{2,1,0:T(8,128)S(1)}, f32[1,256,256]{2,1,0:T(8,128)S(1)}, u32[]{:S(2)}, u32[]{:S(2)}) collective-permute-start(f32[1,256,256]{2,1,0:T(8,128)S(1)} %get-tuple-element.137.refs_8_), channel_id=1, source_target_pairs={{0,8},{4,12},{8,0},{12,4},{16,24},{20,28},{24,16},{28,20},{1,9},{5... | collective-permute-start | bytes 786440 | tf_op jit(solution)/shard_map/ppermute | solution.py:210
  136.3 15.3 %collective-permute-start.36 = (f32[1,256,256]{2,1,0:T(8,128)S(1)}, f32[1,256,256]{2,1,0:T(8,128)S(1)}, u32[]{:S(2)}, u32[]{:S(2)}) collective-permute-start(f32[1,256,256]{2,1,0:T(8,128)S(1)} %get-tuple-element.136.refs_5_), channel_id=1, source_target_pairs={{0,4},{4,0},{8,12},{12,8},{16,20},{20,16},{24,28},{28,24},{1,5},{5... | collective-permute-start | bytes 786440 | tf_op jit(solution)/shard_map/ppermute | solution.py:210
  141.4 15.8 %collective-permute-start.39 = (f32[1,256,256]{2,1,0:T(8,128)S(1)}, f32[1,256,256]{2,1,0:T(8,128)S(1)}, u32[]{:S(2)}, u32[]{:S(2)}) collective-permute-start(f32[1,256,256]{2,1,0:T(8,128)S(1)} %get-tuple-element.140.refs_4_), channel_id=1, source_target_pairs={{0,8},{4,12},{8,0},{12,4},{16,24},{20,28},{24,16},{28,20},{1,9},{5... | collective-permute-start | bytes 786440 | tf_op jit(solution)/shard_map/ppermute | solution.py:210
  (21 other events, 178.7 us)

commit v3 on v2

--- a/solution.py
+++ b/solution.py
@@ -10,27 +10,33 @@
 CHUNKS = ((0, 2), (0, 2), (0, 2), (0, 2), (1, 2), (1, 2), (1, 2), (1, 2))
 EIGHTHS = 8
 STEPS = (
-    (((3, 0),), ("across",)),
-    (((0, 0),), ("near01",)),
-    ((), ("near24",)),
-    (((3, 1), (2, 0)), ()),
-    (((1, 0), (0, 1), (6, 0)), ()),
+    (((0, 0),), ("across",)),
+    (((2, 0),), ()),
+    (((1, 0),), ("near01", "near24")),
+    (((0, 1),), ()),
+    (((5, 0), (1, 1)), ()),
+    (((0, 2), (4, 0), (3, 0)), ()),
+    (((1, 2), (2, 1)), ()),
+    (((0, 3), (3, 1), (2, 2)), ()),
+    (((1, 3), (0, 4)), ("cs0",)),
     (((3, 2),), ()),
-    (((5, 0), (2, 1), (0, 2), (7, 0)), ()),
-    (((2, 2), (1, 1), (3, 3)), ("cs0",)),
-    (((6, 1), (7, 1), (0, 3), (4, 0)), ("mk0", "cs1")),
-    (((1, 2), (5, 1)), ("cs2",)),
-    (((2, 3), (5, 2)), ("mk1", "mk2")),
-    (((7, 2), (4, 1), (1, 3)), ("cs3",)),
-    (((3, 4), (4, 2), (5, 3)), ("cs4",)),
-    (((6, 2), (0, 4), (7, 3), (5, 4)), ("mk3",)),
-    (((4, 3),), ()),
-    (((7, 4), (2, 4), (3, 5)), ()),
-    (((1, 4),), ()),
-    (((6, 3), (0, 5), (4, 4)), ()),
-    (((5, 5), (7, 5), (6, 4), (1, 5)), ("mk4",)),
+    (((2, 3), (6, 0), (1, 4), (5, 1)), ("mk0", "cs2")),
+    (((3, 3), (0, 5), (4, 1)), ("cs1", "cs3", "cs4")),
+    (((2, 4), (6, 1)), ()),
+    (((5, 2),), ("mk1", "mk3")),
+    (((7, 0), (4, 2)), ()),
+    (((5, 3), (1, 5)), ("mk2",)),
+    (((7, 1),), ()),
+    (((3, 4), (6, 2), (4, 3), (5, 4)), ()),
+    (((7, 2),), ("mk4",)),
+    (((6, 3),), ()),
+    (((4, 4),), ()),
+    (((7, 3),), ()),
+    (((6, 4), (3, 5)), ()),
     (((2, 5), (4, 5)), ()),
-    (((6, 5),), ()),
+    (((7, 4),), ()),
+    (((5, 5), (6, 5)), ()),
+    (((7, 5),), ()),
 )
 NEAR = {"near01": (0, 2), "near24": (2, 5)}
 ACROSS = "across"
@@ -170,7 +176,7 @@
     outs += [jax.ShapeDtypeStruct((2, half, 2 * half), jnp.bfloat16)] * len(making)
     hbm = pl.BlockSpec(memory_space=pltpu.HBM)
     vmem = pl.BlockSpec(memory_space=pltpu.VMEM)
-    room = 62 if merged is None else 40
+    room = 60 if merged is None else 40
     merged, *new = pl.pallas_call(
         kernel,
         out_shape=[shape(*weight.shape)] + outs,

time: 166 us -> 157 us (0.946); the launches traced: 164 us -> 156 us
  starting transfers between devices: 52.5 us -> 46.2 us
    ppermute x34 -> x35, starting transfers between devices: 48.7 us -> 43.6 us  [pipelined(): lax.ppermute(array, 'row', partner_route(count, 1 << way))]
    ppermute x34 -> x35, waiting for transfers between devices: 87.1 us -> 86.4 us  [pipelined(): lax.ppermute(array, 'row', partner_route(count, 1 << way))]
    pallas_call x21 -> x27, Pallas kernels: 22 us -> 21.4 us  [step(): pl.pallas_call(kernel, out_shape=[shape(*weight.shape)] + outs, in_specs=...]
  transfers between devices with their start and end apart: 41 -> 42, of which waited for: 20 -> 27; matrix products, arithmetic and copies ran while one was open for 0% -> 0% of each run, Pallas kernels for 13% -> 13%
where the time goes in v3:
time: 157 us; the launch traced here: 156 us
  waiting for transfers between devices  87.1 us (55%)
  starting transfers between devices  46.2 us (29%)
  Pallas kernels  21.4 us (14%)
    ppermute x35, waiting for transfers between devices, pipelined(): lax.ppermute(array, 'row', partner_route(count, 1 << way))  86.4 us
    ppermute x35, starting transfers between devices, pipelined(): lax.ppermute(array, 'row', partner_route(count, 1 << way))  43.6 us
    pallas_call x27, Pallas kernels, step(): pl.pallas_call(kernel, out_shape=[shape(*weight.shape)] + outs, in_specs=...  21.4 us
  transfers between devices with their start and end apart: 42, of which 27 were waited for; matrix products, arithmetic and copies ran while one was open for 0% of the time, Pallas kernels for 13%

profile of v3, /device:TPU:0, one launch (start us, length us, event | category | flops | bytes accessed | tf_op | source)
XLA Modules:
  0.0 156.5 jit_solution(12889158265515364125)
XLA Ops:
  0.5 2.8 %shard_map.28 = (f32[512,1024]{1,0:T(8,128)}, f32[1,256,256]{2,1,0:T(8,128)}, f32[5,128,512]{2,1,0:T(8,128)}) custom-call(f32[512,1024]{1,0:T(8,128)} %refs_0_.13, f32[5,128,512]{2,1,0:T(8,128)} %refs_2_.1), custom_call_target="tpu_custom_call" | custom-call | flops 1 | bytes 1 | tf_op jit(solution)/shard_map/pallas_call | solution.py:180
  3.2 2.6 %collective-permute-start.1 = (f32[1,256,256]{2,1,0:T(8,128)}, f32[1,256,256]{2,1,0:T(8,128)S(1)}, u32[]{:S(2)}, u32[]{:S(2)}) collective-permute-start(f32[1,256,256]{2,1,0:T(8,128)} %get-tuple-element.83.refs_1_), channel_id=1, source_target_pairs={{0,4},{4,0},{8,12},{12,8},{16,20},{20,16},{24,28},{28,24},{1,5},{5... | collective-permute-start | bytes 786440 | tf_op jit(solution)/shard_map/ppermute | solution.py:216
  9.9 3.3 %collective-permute-done.1.refs_2_ = f32[1,256,256]{2,1,0:T(8,128)S(1)} collective-permute-done((f32[1,256,256]{2,1,0:T(8,128)}, f32[1,256,256]{2,1,0:T(8,128)S(1)}, u32[]{:S(2)}, u32[]{:S(2)}) %collective-permute-start.1) | collective-permute-done | bytes 262176 | tf_op jit(solution)/shard_map/ppermute | solution.py:216
  23.3 2.6 %collective-permute-start.6 = (f32[1,256,256]{2,1,0:T(8,128)S(1)}, f32[1,256,256]{2,1,0:T(8,128)S(1)}, u32[]{:S(2)}, u32[]{:S(2)}) collective-permute-start(f32[1,256,256]{2,1,0:T(8,128)S(1)} %get-tuple-element.94.refs_1_), channel_id=1, source_target_pairs={{0,16},{4,20},{8,24},{12,28},{16,0},{20,4},{24,8},{28,12},{1,17},{... | collective-permute-start | bytes 786440 | tf_op jit(solution)/shard_map/ppermute | solution.py:216
  25.9 5.4 %collective-permute-done.4.refs_2_ = f32[1,256,256]{2,1,0:T(8,128)S(1)} collective-permute-done((f32[1,256,256]{2,1,0:T(8,128)S(1)}, f32[1,256,256]{2,1,0:T(8,128)S(1)}, u32[]{:S(2)}, u32[]{:S(2)}) %collective-permute-start.4) | collective-permute-done | bytes 262176 | tf_op jit(solution)/shard_map/ppermute | solution.py:216
  34.0 4.5 %collective-permute-done.6.refs_2_ = f32[1,256,256]{2,1,0:T(8,128)S(1)} collective-permute-done((f32[1,256,256]{2,1,0:T(8,128)S(1)}, f32[1,256,256]{2,1,0:T(8,128)S(1)}, u32[]{:S(2)}, u32[]{:S(2)}) %collective-permute-start.6) | collective-permute-done | bytes 262176 | tf_op jit(solution)/shard_map/ppermute | solution.py:216
  38.5 4.5 %collective-permute-done.8.refs_8_ = f32[1,256,256]{2,1,0:T(8,128)S(1)} collective-permute-done((f32[1,256,256]{2,1,0:T(8,128)S(1)}, f32[1,256,256]{2,1,0:T(8,128)S(1)}, u32[]{:S(2)}, u32[]{:S(2)}) %collective-permute-start.8) | collective-permute-done | bytes 262176 | tf_op jit(solution)/shard_map/ppermute | solution.py:216
  43.8 2.4 %collective-permute-start.10 = (f32[1,256,256]{2,1,0:T(8,128)S(1)}, f32[1,256,256]{2,1,0:T(8,128)S(1)}, u32[]{:S(2)}, u32[]{:S(2)}) collective-permute-start(f32[1,256,256]{2,1,0:T(8,128)S(1)} %get-tuple-element.100.refs_4_), channel_id=1, source_target_pairs={{0,4},{4,0},{8,12},{12,8},{16,20},{20,16},{24,28},{28,24},{1,5},{5... | collective-permute-start | bytes 786440 | tf_op jit(solution)/shard_map/ppermute | solution.py:216
  48.3 2.4 %collective-permute-done.9.refs_2_ = f32[1,256,256]{2,1,0:T(8,128)S(1)} collective-permute-done((f32[1,256,256]{2,1,0:T(8,128)S(1)}, f32[1,256,256]{2,1,0:T(8,128)S(1)}, u32[]{:S(2)}, u32[]{:S(2)}) %collective-permute-start.9) | collective-permute-done | bytes 262176 | tf_op jit(solution)/shard_map/ppermute | solution.py:216
  53.4 2.5 %collective-permute-start.14 = (f32[1,256,256]{2,1,0:T(8,128)S(1)}, f32[1,256,256]{2,1,0:T(8,128)S(1)}, u32[]{:S(2)}, u32[]{:S(2)}) collective-permute-start(f32[1,256,256]{2,1,0:T(8,128)S(1)} %get-tuple-element.107.refs_5_), channel_id=1, source_target_pairs={{0,4},{4,0},{8,12},{12,8},{16,20},{20,16},{24,28},{28,24},{1,5},{5... | collective-permute-start | bytes 786440 | tf_op jit(solution)/shard_map/ppermute | solution.py:216
  56.5 2.5 %collective-permute-start.18 = (f32[1,256,256]{2,1,0:T(8,128)S(1)}, f32[1,256,256]{2,1,0:T(8,128)S(1)}, u32[]{:S(2)}, u32[]{:S(2)}) collective-permute-start(f32[1,256,256]{2,1,0:T(8,128)S(1)} %get-tuple-element.112.refs_4_), channel_id=1, source_target_pairs={{0,8},{4,12},{8,0},{12,4},{16,24},{20,28},{24,16},{28,20},{1,9},{5... | collective-permute-start | bytes 786440 | tf_op jit(solution)/shard_map/ppermute | solution.py:216
  63.3 3.2 %collective-permute-start.20 = (f32[2,256,256]{2,1,0:T(8,128)S(1)}, f32[2,256,256]{2,1,0:T(8,128)S(1)}, u32[]{:S(2)}, u32[]{:S(2)}) collective-permute-start(f32[2,256,256]{2,1,0:T(8,128)S(1)} %get-tuple-element.118.refs_1_.refs_3_), channel_id=1, source_target_pairs={{0,8},{4,12},{8,0},{12,4},{16,24},{20,28},{24,16},{28,20},{1,9},{5... | collective-permute-start | bytes 1572872 | tf_op jit(solution)/shard_map/ppermute | solution.py:216
  66.5 4.2 %collective-permute-done.17.refs_2_ = f32[1,256,256]{2,1,0:T(8,128)S(1)} collective-permute-done((f32[1,256,256]{2,1,0:T(8,128)S(1)}, f32[1,256,256]{2,1,0:T(8,128)S(1)}, u32[]{:S(2)}, u32[]{:S(2)}) %collective-permute-start.17) | collective-permute-done | bytes 262176 | tf_op jit(solution)/shard_map/ppermute | solution.py:216
  75.3 7.7 %collective-permute-done.20.refs_2_.refs_4_ = f32[2,256,256]{2,1,0:T(8,128)S(1)} collective-permute-done((f32[2,256,256]{2,1,0:T(8,128)S(1)}, f32[2,256,256]{2,1,0:T(8,128)S(1)}, u32[]{:S(2)}, u32[]{:S(2)}) %collective-permute-start.20) | collective-permute-done | bytes 524320 | tf_op jit(solution)/shard_map/ppermute | solution.py:216
  85.9 4.7 %collective-permute-done.23.refs_3_ = f32[1,256,256]{2,1,0:T(8,128)S(1)} collective-permute-done((f32[1,256,256]{2,1,0:T(8,128)S(1)}, f32[1,256,256]{2,1,0:T(8,128)S(1)}, u32[]{:S(2)}, u32[]{:S(2)}) %collective-permute-start.23) | collective-permute-done | bytes 262176 | tf_op jit(solution)/shard_map/ppermute | solution.py:216
  93.3 5.5 %collective-permute-done.24.refs_2_ = f32[1,256,256]{2,1,0:T(8,128)S(1)} collective-permute-done((f32[1,256,256]{2,1,0:T(8,128)S(1)}, f32[1,256,256]{2,1,0:T(8,128)S(1)}, u32[]{:S(2)}, u32[]{:S(2)}) %collective-permute-start.24) | collective-permute-done | bytes 262176 | tf_op jit(solution)/shard_map/ppermute | solution.py:216
  100.9 5.2 %collective-permute-done.27.refs_2_ = f32[1,256,256]{2,1,0:T(8,128)S(1)} collective-permute-done((f32[1,256,256]{2,1,0:T(8,128)S(1)}, f32[1,256,256]{2,1,0:T(8,128)S(1)}, u32[]{:S(2)}, u32[]{:S(2)}) %collective-permute-start.27) | collective-permute-done | bytes 262176 | tf_op jit(solution)/shard_map/ppermute | solution.py:216
  108.2 2.8 %collective-permute-done.28.refs_5_.refs_2_ = f32[2,256,256]{2,1,0:T(8,128)S(1)} collective-permute-done((f32[2,256,256]{2,1,0:T(8,128)S(1)}, f32[2,256,256]{2,1,0:T(8,128)S(1)}, u32[]{:S(2)}, u32[]{:S(2)}) %collective-permute-start.28) | collective-permute-done | bytes 524320 | tf_op jit(solution)/shard_map/ppermute | solution.py:216
  113.9 2.3 %collective-permute-start.37 = (f32[2,256,256]{2,1,0:T(8,128)S(1)}, f32[2,256,256]{2,1,0:T(8,128)S(1)}, u32[]{:S(2)}, u32[]{:S(2)}) collective-permute-start(f32[2,256,256]{2,1,0:T(8,128)S(1)} %get-tuple-element.147.refs_4_.refs_1_), channel_id=1, source_target_pairs={{0,8},{4,12},{8,0},{12,4},{16,24},{20,28},{24,16},{28,20},{1,9},{5... | collective-permute-start | bytes 1572872 | tf_op jit(solution)/shard_map/ppermute | solution.py:216
  118.9 8.2 %collective-permute-done.33.refs_2_ = f32[1,256,256]{2,1,0:T(8,128)S(1)} collective-permute-done((f32[1,256,256]{2,1,0:T(8,128)S(1)}, f32[1,256,256]{2,1,0:T(8,128)S(1)}, u32[]{:S(2)}, u32[]{:S(2)}) %collective-permute-start.33) | collective-permute-done | bytes 262176 | tf_op jit(solution)/shard_map/ppermute | solution.py:216
  128.9 7.5 %collective-permute-done.35.refs_2_ = f32[1,256,256]{2,1,0:T(8,128)S(1)} collective-permute-done((f32[1,256,256]{2,1,0:T(8,128)S(1)}, f32[1,256,256]{2,1,0:T(8,128)S(1)}, u32[]{:S(2)}, u32[]{:S(2)}) %collective-permute-start.35) | collective-permute-done | bytes 262176 | tf_op jit(solution)/shard_map/ppermute | solution.py:216
  142.5 2.2 %collective-permute-done.38.refs_5_ = f32[1,256,256]{2,1,0:T(8,128)S(1)} collective-permute-done((f32[1,256,256]{2,1,0:T(8,128)S(1)}, f32[1,256,256]{2,1,0:T(8,128)S(1)}, u32[]{:S(2)}, u32[]{:S(2)}) %collective-permute-start.38) | collective-permute-done | bytes 262176 | tf_op jit(solution)/shard_map/ppermute | solution.py:216
  147.3 3.1 %collective-permute-done.40.refs_5_ = f32[1,256,256]{2,1,0:T(8,128)S(1)} collective-permute-done((f32[1,256,256]{2,1,0:T(8,128)S(1)}, f32[1,256,256]{2,1,0:T(8,128)S(1)}, u32[]{:S(2)}, u32[]{:S(2)}) %collective-permute-start.40) | collective-permute-done | bytes 262176 | tf_op jit(solution)/shard_map/ppermute | solution.py:216
  151.8 3.4 %collective-permute-done.41.refs_2_ = f32[1,256,256]{2,1,0:T(8,128)S(1)} collective-permute-done((f32[1,256,256]{2,1,0:T(8,128)S(1)}, f32[1,256,256]{2,1,0:T(8,128)S(1)}, u32[]{:S(2)}, u32[]{:S(2)}) %collective-permute-start.41) | collective-permute-done | bytes 262176 | tf_op jit(solution)/shard_map/ppermute | solution.py:216
  (93 shorter events, 60.3 us)
Async XLA Ops:
  5.8 40.5 %collective-permute-start.11 = (f32[5,128,512]{2,1,0:T(8,128)}, f32[5,128,512]{2,1,0:T(8,128)S(1)}, u32[]{:S(2)}, u32[]{:S(2)}) collective-permute-start(f32[5,128,512]{2,1,0:T(8,128)} %get-tuple-element.102), channel_id=1, source_target_pairs={{0,2},{1,3},{2,0},{3,1},{4,6},{5,7},{6,4},{7,5},{8,10},{9,11},{10,... | collective-permute-start | bytes 3932168 | tf_op jit(solution)/shard_map/ppermute | solution.py:202
  19.2 12.2 %collective-permute-start.4 = (f32[1,256,256]{2,1,0:T(8,128)S(1)}, f32[1,256,256]{2,1,0:T(8,128)S(1)}, u32[]{:S(2)}, u32[]{:S(2)}) collective-permute-start(f32[1,256,256]{2,1,0:T(8,128)S(1)} %get-tuple-element.91.refs_1_), channel_id=1, source_target_pairs={{0,8},{4,12},{8,0},{12,4},{16,24},{20,28},{24,16},{28,20},{1,9},{5... | collective-permute-start | bytes 786440 | tf_op jit(solution)/shard_map/ppermute | solution.py:216
  21.8 21.2 %collective-permute-start.7 = (f32[2,256,256]{2,1,0:T(8,128)S(1)}, f32[2,256,256]{2,1,0:T(8,128)S(1)}, u32[]{:S(2)}, u32[]{:S(2)}) collective-permute-start(f32[2,256,256]{2,1,0:T(8,128)S(1)} %get-tuple-element.96.refs_4_.refs_7_), channel_id=1, source_target_pairs={{0,4},{4,0},{8,12},{12,8},{16,20},{20,16},{24,28},{28,24},{1,5},{5... | collective-permute-start | bytes 1572872 | tf_op jit(solution)/shard_map/ppermute | solution.py:216
  23.3 15.2 %collective-permute-start.6 = (f32[1,256,256]{2,1,0:T(8,128)S(1)}, f32[1,256,256]{2,1,0:T(8,128)S(1)}, u32[]{:S(2)}, u32[]{:S(2)}) collective-permute-start(f32[1,256,256]{2,1,0:T(8,128)S(1)} %get-tuple-element.94.refs_1_), channel_id=1, source_target_pairs={{0,16},{4,20},{8,24},{12,28},{16,0},{20,4},{24,8},{28,12},{1,17},{... | collective-permute-start | bytes 786440 | tf_op jit(solution)/shard_map/ppermute | solution.py:216
  32.0 18.7 %collective-permute-start.9 = (f32[1,256,256]{2,1,0:T(8,128)S(1)}, f32[1,256,256]{2,1,0:T(8,128)S(1)}, u32[]{:S(2)}, u32[]{:S(2)}) collective-permute-start(f32[1,256,256]{2,1,0:T(8,128)S(1)} %get-tuple-element.99.refs_1_), channel_id=1, source_target_pairs={{0,16},{4,20},{8,24},{12,28},{16,0},{20,4},{24,8},{28,12},{1,17},{... | collective-permute-start | bytes 786440 | tf_op jit(solution)/shard_map/ppermute | solution.py:216
  46.3 12.7 %collective-permute-start.13 = (f32[1,256,256]{2,1,0:T(8,128)S(1)}, f32[1,256,256]{2,1,0:T(8,128)S(1)}, u32[]{:S(2)}, u32[]{:S(2)}) collective-permute-start(f32[1,256,256]{2,1,0:T(8,128)S(1)} %get-tuple-element.106.refs_2_), channel_id=1, source_target_pairs={{0,16},{4,20},{8,24},{12,28},{16,0},{20,4},{24,8},{28,12},{1,17},{... | collective-permute-start | bytes 786440 | tf_op jit(solution)/shard_map/ppermute | solution.py:216
  56.4 14.4 %collective-permute-start.17 = (f32[1,256,256]{2,1,0:T(8,128)S(1)}, f32[1,256,256]{2,1,0:T(8,128)S(1)}, u32[]{:S(2)}, u32[]{:S(2)}) collective-permute-start(f32[1,256,256]{2,1,0:T(8,128)S(1)} %get-tuple-element.111.refs_1_), channel_id=1, source_target_pairs={{0,16},{4,20},{8,24},{12,28},{16,0},{20,4},{24,8},{28,12},{1,17},{... | collective-permute-start | bytes 786440 | tf_op jit(solution)/shard_map/ppermute | solution.py:216
  56.5 15.2 %collective-permute-start.18 = (f32[1,256,256]{2,1,0:T(8,128)S(1)}, f32[1,256,256]{2,1,0:T(8,128)S(1)}, u32[]{:S(2)}, u32[]{:S(2)}) collective-permute-start(f32[1,256,256]{2,1,0:T(8,128)S(1)} %get-tuple-element.112.refs_4_), channel_id=1, source_target_pairs={{0,8},{4,12},{8,0},{12,4},{16,24},{20,28},{24,16},{28,20},{1,9},{5... | collective-permute-start | bytes 786440 | tf_op jit(solution)/shard_map/ppermute | solution.py:216
  61.2 12.7 %collective-permute-start.19 = (f32[2,256,256]{2,1,0:T(8,128)S(1)}, f32[2,256,256]{2,1,0:T(8,128)S(1)}, u32[]{:S(2)}, u32[]{:S(2)}) collective-permute-start(f32[2,256,256]{2,1,0:T(8,128)S(1)} %get-tuple-element.116.refs_1_), channel_id=1, source_target_pairs={{0,4},{4,0},{8,12},{12,8},{16,20},{20,16},{24,28},{28,24},{1,5},{5... | collective-permute-start | bytes 1572872 | tf_op jit(solution)/shard_map/ppermute | solution.py:216
  63.3 19.6 %collective-permute-start.20 = (f32[2,256,256]{2,1,0:T(8,128)S(1)}, f32[2,256,256]{2,1,0:T(8,128)S(1)}, u32[]{:S(2)}, u32[]{:S(2)}) collective-permute-start(f32[2,256,256]{2,1,0:T(8,128)S(1)} %get-tuple-element.118.refs_1_.refs_3_), channel_id=1, source_target_pairs={{0,8},{4,12},{8,0},{12,4},{16,24},{20,28},{24,16},{28,20},{1,9},{5... | collective-permute-start | bytes 1572872 | tf_op jit(solution)/shard_map/ppermute | solution.py:216
  73.9 16.7 %collective-permute-start.23 = (f32[1,256,256]{2,1,0:T(8,128)S(1)}, f32[1,256,256]{2,1,0:T(8,128)S(1)}, u32[]{:S(2)}, u32[]{:S(2)}) collective-permute-start(f32[1,256,256]{2,1,0:T(8,128)S(1)} %get-tuple-element.122.refs_2_), channel_id=1, source_target_pairs={{0,8},{4,12},{8,0},{12,4},{16,24},{20,28},{24,16},{28,20},{1,9},{5... | collective-permute-start | bytes 786440 | tf_op jit(solution)/shard_map/ppermute | solution.py:216
  73.9 19.4 %collective-permute-start.25 = (f32[1,128,512]{2,1,0:T(8,128)S(1)}, f32[1,128,512]{2,1,0:T(8,128)S(1)}, u32[]{:S(2)}, u32[]{:S(2)}) collective-permute-start(f32[1,128,512]{2,1,0:T(8,128)S(1)} %get-tuple-element.126), channel_id=1, source_target_pairs={{0,1},{1,0},{2,3},{3,2},{4,5},{5,4},{6,7},{7,6},{8,9},{9,8},{10,11... | collective-permute-start | bytes 786440 | tf_op jit(solution)/shard_map/ppermute | solution.py:201
  83.5 15.3 %collective-permute-start.24 = (f32[1,256,256]{2,1,0:T(8,128)S(1)}, f32[1,256,256]{2,1,0:T(8,128)S(1)}, u32[]{:S(2)}, u32[]{:S(2)}) collective-permute-start(f32[1,256,256]{2,1,0:T(8,128)S(1)} %get-tuple-element.125.refs_1_), channel_id=1, source_target_pairs={{0,16},{4,20},{8,24},{12,28},{16,0},{20,4},{24,8},{28,12},{1,17},{... | collective-permute-start | bytes 786440 | tf_op jit(solution)/shard_map/ppermute | solution.py:216
  83.9 27.2 %collective-permute-start.28 = (f32[2,256,256]{2,1,0:T(8,128)S(1)}, f32[2,256,256]{2,1,0:T(8,128)S(1)}, u32[]{:S(2)}, u32[]{:S(2)}) collective-permute-start(f32[2,256,256]{2,1,0:T(8,128)S(1)} %get-tuple-element.131.refs_4_.refs_1_), channel_id=1, source_target_pairs={{0,8},{4,12},{8,0},{12,4},{16,24},{20,28},{24,16},{28,20},{1,9},{5... | collective-permute-start | bytes 1572872 | tf_op jit(solution)/shard_map/ppermute | solution.py:216
  93.2 12.9 %collective-permute-start.27 = (f32[1,256,256]{2,1,0:T(8,128)S(1)}, f32[1,256,256]{2,1,0:T(8,128)S(1)}, u32[]{:S(2)}, u32[]{:S(2)}) collective-permute-start(f32[1,256,256]{2,1,0:T(8,128)S(1)} %get-tuple-element.130.refs_1_), channel_id=1, source_target_pairs={{0,4},{4,0},{8,12},{12,8},{16,20},{20,16},{24,28},{28,24},{1,5},{5... | collective-permute-start | bytes 786440 | tf_op jit(solution)/shard_map/ppermute | solution.py:216
  93.3 15.0 %collective-permute-start.29 = (f32[1,256,256]{2,1,0:T(8,128)S(1)}, f32[1,256,256]{2,1,0:T(8,128)S(1)}, u32[]{:S(2)}, u32[]{:S(2)}) collective-permute-start(f32[1,256,256]{2,1,0:T(8,128)S(1)} %get-tuple-element.132.refs_7_), channel_id=1, source_target_pairs={{0,16},{4,20},{8,24},{12,28},{16,0},{20,4},{24,8},{28,12},{1,17},{... | collective-permute-start | bytes 786440 | tf_op jit(solution)/shard_map/ppermute | solution.py:216
  100.5 15.7 %collective-permute-start.32 = (f32[1,128,512]{2,1,0:T(8,128)S(1)}, f32[1,128,512]{2,1,0:T(8,128)S(1)}, u32[]{:S(2)}, u32[]{:S(2)}) collective-permute-start(f32[1,128,512]{2,1,0:T(8,128)S(1)} %get-tuple-element.138), channel_id=1, source_target_pairs={{0,1},{1,0},{2,3},{3,2},{4,5},{5,4},{6,7},{7,6},{8,9},{9,8},{10,11... | collective-permute-start | bytes 786440 | tf_op jit(solution)/shard_map/ppermute | solution.py:201
  106.1 12.2 %collective-permute-start.31 = (f32[1,256,256]{2,1,0:T(8,128)S(1)}, f32[1,256,256]{2,1,0:T(8,128)S(1)}, u32[]{:S(2)}, u32[]{:S(2)}) collective-permute-start(f32[1,256,256]{2,1,0:T(8,128)S(1)} %get-tuple-element.137.refs_1_), channel_id=1, source_target_pairs={{0,8},{4,12},{8,0},{12,4},{16,24},{20,28},{24,16},{28,20},{1,9},{5... | collective-permute-start | bytes 786440 | tf_op jit(solution)/shard_map/ppermute | solution.py:216
  112.1 15.1 %collective-permute-start.33 = (f32[1,256,256]{2,1,0:T(8,128)S(1)}, f32[1,256,256]{2,1,0:T(8,128)S(1)}, u32[]{:S(2)}, u32[]{:S(2)}) collective-permute-start(f32[1,256,256]{2,1,0:T(8,128)S(1)} %get-tuple-element.140.refs_1_), channel_id=1, source_target_pairs={{0,16},{4,20},{8,24},{12,28},{16,0},{20,4},{24,8},{28,12},{1,17},{... | collective-permute-start | bytes 786440 | tf_op jit(solution)/shard_map/ppermute | solution.py:216
  112.7 15.7 %collective-permute-start.34 = (f32[1,256,256]{2,1,0:T(8,128)S(1)}, f32[1,256,256]{2,1,0:T(8,128)S(1)}, u32[]{:S(2)}, u32[]{:S(2)}) collective-permute-start(f32[1,256,256]{2,1,0:T(8,128)S(1)} %get-tuple-element.142.refs_1_), channel_id=1, source_target_pairs={{0,4},{4,0},{8,12},{12,8},{16,20},{20,16},{24,28},{28,24},{1,5},{5... | collective-permute-start | bytes 786440 | tf_op jit(solution)/shard_map/ppermute | solution.py:216
  113.9 25.2 %collective-permute-start.37 = (f32[2,256,256]{2,1,0:T(8,128)S(1)}, f32[2,256,256]{2,1,0:T(8,128)S(1)}, u32[]{:S(2)}, u32[]{:S(2)}) collective-permute-start(f32[2,256,256]{2,1,0:T(8,128)S(1)} %get-tuple-element.147.refs_4_.refs_1_), channel_id=1, source_target_pairs={{0,8},{4,12},{8,0},{12,4},{16,24},{20,28},{24,16},{28,20},{1,9},{5... | collective-permute-start | bytes 1572872 | tf_op jit(solution)/shard_map/ppermute | solution.py:216
  118.9 17.5 %collective-permute-start.35 = (f32[1,256,256]{2,1,0:T(8,128)S(1)}, f32[1,256,256]{2,1,0:T(8,128)S(1)}, u32[]{:S(2)}, u32[]{:S(2)}) collective-permute-start(f32[1,256,256]{2,1,0:T(8,128)S(1)} %get-tuple-element.144.refs_1_), channel_id=1, source_target_pairs={{0,16},{4,20},{8,24},{12,28},{16,0},{20,4},{24,8},{28,12},{1,17},{... | collective-permute-start | bytes 786440 | tf_op jit(solution)/shard_map/ppermute | solution.py:216
  127.6 11.6 %collective-permute-start.36 = (f32[1,256,256]{2,1,0:T(8,128)S(1)}, f32[1,256,256]{2,1,0:T(8,128)S(1)}, u32[]{:S(2)}, u32[]{:S(2)}) collective-permute-start(f32[1,256,256]{2,1,0:T(8,128)S(1)} %get-tuple-element.146.refs_1_), channel_id=1, source_target_pairs={{0,4},{4,0},{8,12},{12,8},{16,20},{20,16},{24,28},{28,24},{1,5},{5... | collective-permute-start | bytes 786440 | tf_op jit(solution)/shard_map/ppermute | solution.py:216
  128.8 16.0 %collective-permute-start.38 = (f32[1,256,256]{2,1,0:T(8,128)S(1)}, f32[1,256,256]{2,1,0:T(8,128)S(1)}, u32[]{:S(2)}, u32[]{:S(2)}) collective-permute-start(f32[1,256,256]{2,1,0:T(8,128)S(1)} %get-tuple-element.149.refs_4_), channel_id=1, source_target_pairs={{0,8},{4,12},{8,0},{12,4},{16,24},{20,28},{24,16},{28,20},{1,9},{5... | collective-permute-start | bytes 786440 | tf_op jit(solution)/shard_map/ppermute | solution.py:216
  (21 other events, 160.7 us)

commit v4 on v3

--- a/solution.py
+++ b/solution.py
@@ -10,8 +10,8 @@
 CHUNKS = ((0, 2), (0, 2), (0, 2), (0, 2), (1, 2), (1, 2), (1, 2), (1, 2))
 EIGHTHS = 8
 STEPS = (
-    (((0, 0),), ("across",)),
-    (((2, 0),), ()),
+    (((0, 0),), ()),
+    (((2, 0),), ("across",)),
     (((1, 0),), ("near01", "near24")),
     (((0, 1),), ()),
     (((5, 0), (1, 1)), ()),
@@ -176,7 +176,7 @@
     outs += [jax.ShapeDtypeStruct((2, half, 2 * half), jnp.bfloat16)] * len(making)
     hbm = pl.BlockSpec(memory_space=pltpu.HBM)
     vmem = pl.BlockSpec(memory_space=pltpu.VMEM)
-    room = 60 if merged is None else 40
+    room = 52 if merged is None else 40
     merged, *new = pl.pallas_call(
         kernel,
         out_shape=[shape(*weight.shape)] + outs,

time: 157 us -> 155 us (0.987)
  Pallas kernels: 21.4 us -> 19.8 us
  transfers between devices with their start and end apart: 42 -> 42, of which waited for: 27 -> 27; matrix products, arithmetic and copies ran while one was open for 0% -> 0% of each run, Pallas kernels for 13% -> 12%
where the time goes in v4:
time: 155 us
  waiting for transfers between devices  86.2 us (56%)
  starting transfers between devices  46.8 us (30%)
  Pallas kernels  19.8 us (13%)
    ppermute x35, waiting for transfers between devices, pipelined(): lax.ppermute(array, 'row', partner_route(count, 1 << way))  85.5 us
    ppermute x35, starting transfers between devices, pipelined(): lax.ppermute(array, 'row', partner_route(count, 1 << way))  44.1 us
    pallas_call x27, Pallas kernels, step(): pl.pallas_call(kernel, out_shape=[shape(*weight.shape)] + outs, in_specs=...  19.8 us
  transfers between devices with their start and end apart: 42, of which 27 were waited for; matrix products, arithmetic and copies ran while one was open for 0% of the time, Pallas kernels for 12%

profile of v4, /device:TPU:0, one launch (start us, length us, event | category | flops | bytes accessed | tf_op | source)
XLA Modules:
  0.0 154.6 jit_solution(1256965079007647243)
XLA Ops:
  1.6 2.5 %collective-permute-start.1 = (f32[1,256,256]{2,1,0:T(8,128)S(1)}, f32[1,256,256]{2,1,0:T(8,128)S(1)}, u32[]{:S(2)}, u32[]{:S(2)}) collective-permute-start(f32[1,256,256]{2,1,0:T(8,128)S(1)} %get-tuple-element.83.refs_1_), channel_id=1, source_target_pairs={{0,4},{4,0},{8,12},{12,8},{16,20},{20,16},{24,28},{28,24},{1,5},{5... | collective-permute-start | bytes 786440 | tf_op jit(solution)/shard_map/ppermute | solution.py:216
  8.4 2.9 %collective-permute-done.1.refs_2_ = f32[1,256,256]{2,1,0:T(8,128)S(1)} collective-permute-done((f32[1,256,256]{2,1,0:T(8,128)S(1)}, f32[1,256,256]{2,1,0:T(8,128)S(1)}, u32[]{:S(2)}, u32[]{:S(2)}) %collective-permute-start.1) | collective-permute-done | bytes 262176 | tf_op jit(solution)/shard_map/ppermute | solution.py:216
  11.7 2.1 %collective-permute-start.3 = (f32[1,256,256]{2,1,0:T(8,128)S(1)}, f32[1,256,256]{2,1,0:T(8,128)S(1)}, u32[]{:S(2)}, u32[]{:S(2)}) collective-permute-start(f32[1,256,256]{2,1,0:T(8,128)S(1)} %get-tuple-element.88.refs_2_), channel_id=1, source_target_pairs={{0,8},{4,12},{8,0},{12,4},{16,24},{20,28},{24,16},{28,20},{1,9},{5... | collective-permute-start | bytes 786440 | tf_op jit(solution)/shard_map/ppermute | solution.py:216
  21.5 2.6 %collective-permute-start.6 = (f32[1,256,256]{2,1,0:T(8,128)S(1)}, f32[1,256,256]{2,1,0:T(8,128)S(1)}, u32[]{:S(2)}, u32[]{:S(2)}) collective-permute-start(f32[1,256,256]{2,1,0:T(8,128)S(1)} %get-tuple-element.94.refs_1_), channel_id=1, source_target_pairs={{0,16},{4,20},{8,24},{12,28},{16,0},{20,4},{24,8},{28,12},{1,17},{... | collective-permute-start | bytes 786440 | tf_op jit(solution)/shard_map/ppermute | solution.py:216
  24.1 5.5 %collective-permute-done.4.refs_2_ = f32[1,256,256]{2,1,0:T(8,128)S(1)} collective-permute-done((f32[1,256,256]{2,1,0:T(8,128)S(1)}, f32[1,256,256]{2,1,0:T(8,128)S(1)}, u32[]{:S(2)}, u32[]{:S(2)}) %collective-permute-start.4) | collective-permute-done | bytes 262176 | tf_op jit(solution)/shard_map/ppermute | solution.py:216
  32.1 4.5 %collective-permute-done.6.refs_2_ = f32[1,256,256]{2,1,0:T(8,128)S(1)} collective-permute-done((f32[1,256,256]{2,1,0:T(8,128)S(1)}, f32[1,256,256]{2,1,0:T(8,128)S(1)}, u32[]{:S(2)}, u32[]{:S(2)}) %collective-permute-start.6) | collective-permute-done | bytes 262176 | tf_op jit(solution)/shard_map/ppermute | solution.py:216
  36.7 4.5 %collective-permute-done.8.refs_8_ = f32[1,256,256]{2,1,0:T(8,128)S(1)} collective-permute-done((f32[1,256,256]{2,1,0:T(8,128)S(1)}, f32[1,256,256]{2,1,0:T(8,128)S(1)}, u32[]{:S(2)}, u32[]{:S(2)}) %collective-permute-start.8) | collective-permute-done | bytes 262176 | tf_op jit(solution)/shard_map/ppermute | solution.py:216
  42.0 2.3 %collective-permute-start.10 = (f32[1,256,256]{2,1,0:T(8,128)S(1)}, f32[1,256,256]{2,1,0:T(8,128)S(1)}, u32[]{:S(2)}, u32[]{:S(2)}) collective-permute-start(f32[1,256,256]{2,1,0:T(8,128)S(1)} %get-tuple-element.100.refs_4_), channel_id=1, source_target_pairs={{0,4},{4,0},{8,12},{12,8},{16,20},{20,16},{24,28},{28,24},{1,5},{5... | collective-permute-start | bytes 786440 | tf_op jit(solution)/shard_map/ppermute | solution.py:216
  46.4 2.4 %collective-permute-done.9.refs_2_ = f32[1,256,256]{2,1,0:T(8,128)S(1)} collective-permute-done((f32[1,256,256]{2,1,0:T(8,128)S(1)}, f32[1,256,256]{2,1,0:T(8,128)S(1)}, u32[]{:S(2)}, u32[]{:S(2)}) %collective-permute-start.9) | collective-permute-done | bytes 262176 | tf_op jit(solution)/shard_map/ppermute | solution.py:216
  51.4 2.6 %collective-permute-start.14 = (f32[1,256,256]{2,1,0:T(8,128)S(1)}, f32[1,256,256]{2,1,0:T(8,128)S(1)}, u32[]{:S(2)}, u32[]{:S(2)}) collective-permute-start(f32[1,256,256]{2,1,0:T(8,128)S(1)} %get-tuple-element.107.refs_5_), channel_id=1, source_target_pairs={{0,4},{4,0},{8,12},{12,8},{16,20},{20,16},{24,28},{28,24},{1,5},{5... | collective-permute-start | bytes 786440 | tf_op jit(solution)/shard_map/ppermute | solution.py:216
  54.7 2.5 %collective-permute-start.18 = (f32[1,256,256]{2,1,0:T(8,128)S(1)}, f32[1,256,256]{2,1,0:T(8,128)S(1)}, u32[]{:S(2)}, u32[]{:S(2)}) collective-permute-start(f32[1,256,256]{2,1,0:T(8,128)S(1)} %get-tuple-element.112.refs_4_), channel_id=1, source_target_pairs={{0,8},{4,12},{8,0},{12,4},{16,24},{20,28},{24,16},{28,20},{1,9},{5... | collective-permute-start | bytes 786440 | tf_op jit(solution)/shard_map/ppermute | solution.py:216
  61.3 3.3 %collective-permute-start.20 = (f32[2,256,256]{2,1,0:T(8,128)S(1)}, f32[2,256,256]{2,1,0:T(8,128)S(1)}, u32[]{:S(2)}, u32[]{:S(2)}) collective-permute-start(f32[2,256,256]{2,1,0:T(8,128)S(1)} %get-tuple-element.118.refs_1_.refs_3_), channel_id=1, source_target_pairs={{0,8},{4,12},{8,0},{12,4},{16,24},{20,28},{24,16},{28,20},{1,9},{5... | collective-permute-start | bytes 1572872 | tf_op jit(solution)/shard_map/ppermute | solution.py:216
  64.7 4.2 %collective-permute-done.17.refs_2_ = f32[1,256,256]{2,1,0:T(8,128)S(1)} collective-permute-done((f32[1,256,256]{2,1,0:T(8,128)S(1)}, f32[1,256,256]{2,1,0:T(8,128)S(1)}, u32[]{:S(2)}, u32[]{:S(2)}) %collective-permute-start.17) | collective-permute-done | bytes 262176 | tf_op jit(solution)/shard_map/ppermute | solution.py:216
  73.4 7.7 %collective-permute-done.20.refs_2_.refs_4_ = f32[2,256,256]{2,1,0:T(8,128)S(1)} collective-permute-done((f32[2,256,256]{2,1,0:T(8,128)S(1)}, f32[2,256,256]{2,1,0:T(8,128)S(1)}, u32[]{:S(2)}, u32[]{:S(2)}) %collective-permute-start.20) | collective-permute-done | bytes 524320 | tf_op jit(solution)/shard_map/ppermute | solution.py:216
  84.0 4.7 %collective-permute-done.23.refs_3_ = f32[1,256,256]{2,1,0:T(8,128)S(1)} collective-permute-done((f32[1,256,256]{2,1,0:T(8,128)S(1)}, f32[1,256,256]{2,1,0:T(8,128)S(1)}, u32[]{:S(2)}, u32[]{:S(2)}) %collective-permute-start.23) | collective-permute-done | bytes 262176 | tf_op jit(solution)/shard_map/ppermute | solution.py:216
  91.4 5.6 %collective-permute-done.24.refs_2_ = f32[1,256,256]{2,1,0:T(8,128)S(1)} collective-permute-done((f32[1,256,256]{2,1,0:T(8,128)S(1)}, f32[1,256,256]{2,1,0:T(8,128)S(1)}, u32[]{:S(2)}, u32[]{:S(2)}) %collective-permute-start.24) | collective-permute-done | bytes 262176 | tf_op jit(solution)/shard_map/ppermute | solution.py:216
  99.0 5.2 %collective-permute-done.27.refs_2_ = f32[1,256,256]{2,1,0:T(8,128)S(1)} collective-permute-done((f32[1,256,256]{2,1,0:T(8,128)S(1)}, f32[1,256,256]{2,1,0:T(8,128)S(1)}, u32[]{:S(2)}, u32[]{:S(2)}) %collective-permute-start.27) | collective-permute-done | bytes 262176 | tf_op jit(solution)/shard_map/ppermute | solution.py:216
  106.3 2.9 %collective-permute-done.28.refs_5_.refs_2_ = f32[2,256,256]{2,1,0:T(8,128)S(1)} collective-permute-done((f32[2,256,256]{2,1,0:T(8,128)S(1)}, f32[2,256,256]{2,1,0:T(8,128)S(1)}, u32[]{:S(2)}, u32[]{:S(2)}) %collective-permute-start.28) | collective-permute-done | bytes 524320 | tf_op jit(solution)/shard_map/ppermute | solution.py:216
  112.1 2.5 %collective-permute-start.37 = (f32[2,256,256]{2,1,0:T(8,128)S(1)}, f32[2,256,256]{2,1,0:T(8,128)S(1)}, u32[]{:S(2)}, u32[]{:S(2)}) collective-permute-start(f32[2,256,256]{2,1,0:T(8,128)S(1)} %get-tuple-element.147.refs_4_.refs_1_), channel_id=1, source_target_pairs={{0,8},{4,12},{8,0},{12,4},{16,24},{20,28},{24,16},{28,20},{1,9},{5... | collective-permute-start | bytes 1572872 | tf_op jit(solution)/shard_map/ppermute | solution.py:216
  117.0 8.3 %collective-permute-done.33.refs_2_ = f32[1,256,256]{2,1,0:T(8,128)S(1)} collective-permute-done((f32[1,256,256]{2,1,0:T(8,128)S(1)}, f32[1,256,256]{2,1,0:T(8,128)S(1)}, u32[]{:S(2)}, u32[]{:S(2)}) %collective-permute-start.33) | collective-permute-done | bytes 262176 | tf_op jit(solution)/shard_map/ppermute | solution.py:216
  127.0 7.4 %collective-permute-done.35.refs_2_ = f32[1,256,256]{2,1,0:T(8,128)S(1)} collective-permute-done((f32[1,256,256]{2,1,0:T(8,128)S(1)}, f32[1,256,256]{2,1,0:T(8,128)S(1)}, u32[]{:S(2)}, u32[]{:S(2)}) %collective-permute-start.35) | collective-permute-done | bytes 262176 | tf_op jit(solution)/shard_map/ppermute | solution.py:216
  138.6 2.2 %collective-permute-start.40 = (f32[1,256,256]{2,1,0:T(8,128)S(1)}, f32[1,256,256]{2,1,0:T(8,128)S(1)}, u32[]{:S(2)}, u32[]{:S(2)}) collective-permute-start(f32[1,256,256]{2,1,0:T(8,128)S(1)} %get-tuple-element.153.refs_4_), channel_id=1, source_target_pairs={{0,8},{4,12},{8,0},{12,4},{16,24},{20,28},{24,16},{28,20},{1,9},{5... | collective-permute-start | bytes 786440 | tf_op jit(solution)/shard_map/ppermute | solution.py:216
  145.4 3.1 %collective-permute-done.40.refs_5_ = f32[1,256,256]{2,1,0:T(8,128)S(1)} collective-permute-done((f32[1,256,256]{2,1,0:T(8,128)S(1)}, f32[1,256,256]{2,1,0:T(8,128)S(1)}, u32[]{:S(2)}, u32[]{:S(2)}) %collective-permute-start.40) | collective-permute-done | bytes 262176 | tf_op jit(solution)/shard_map/ppermute | solution.py:216
  149.9 3.4 %collective-permute-done.41.refs_2_ = f32[1,256,256]{2,1,0:T(8,128)S(1)} collective-permute-done((f32[1,256,256]{2,1,0:T(8,128)S(1)}, f32[1,256,256]{2,1,0:T(8,128)S(1)}, u32[]{:S(2)}, u32[]{:S(2)}) %collective-permute-start.41) | collective-permute-done | bytes 262176 | tf_op jit(solution)/shard_map/ppermute | solution.py:216
  (91 shorter events, 59.3 us)
Async XLA Ops:
  5.6 38.8 %collective-permute-start.11 = (f32[5,128,512]{2,1,0:T(8,128)S(1)}, f32[5,128,512]{2,1,0:T(8,128)S(1)}, u32[]{:S(2)}, u32[]{:S(2)}) collective-permute-start(f32[5,128,512]{2,1,0:T(8,128)S(1)} %get-tuple-element.102), channel_id=1, source_target_pairs={{0,2},{1,3},{2,0},{3,1},{4,6},{5,7},{6,4},{7,5},{8,10},{9,11},{10,... | collective-permute-start | bytes 3932168 | tf_op jit(solution)/shard_map/ppermute | solution.py:202
  17.6 12.0 %collective-permute-start.4 = (f32[1,256,256]{2,1,0:T(8,128)S(1)}, f32[1,256,256]{2,1,0:T(8,128)S(1)}, u32[]{:S(2)}, u32[]{:S(2)}) collective-permute-start(f32[1,256,256]{2,1,0:T(8,128)S(1)} %get-tuple-element.91.refs_1_), channel_id=1, source_target_pairs={{0,8},{4,12},{8,0},{12,4},{16,24},{20,28},{24,16},{28,20},{1,9},{5... | collective-permute-start | bytes 786440 | tf_op jit(solution)/shard_map/ppermute | solution.py:216
  19.9 21.3 %collective-permute-start.7 = (f32[2,256,256]{2,1,0:T(8,128)S(1)}, f32[2,256,256]{2,1,0:T(8,128)S(1)}, u32[]{:S(2)}, u32[]{:S(2)}) collective-permute-start(f32[2,256,256]{2,1,0:T(8,128)S(1)} %get-tuple-element.96.refs_4_.refs_7_), channel_id=1, source_target_pairs={{0,4},{4,0},{8,12},{12,8},{16,20},{20,16},{24,28},{28,24},{1,5},{5... | collective-permute-start | bytes 1572872 | tf_op jit(solution)/shard_map/ppermute | solution.py:216
  21.5 15.2 %collective-permute-start.6 = (f32[1,256,256]{2,1,0:T(8,128)S(1)}, f32[1,256,256]{2,1,0:T(8,128)S(1)}, u32[]{:S(2)}, u32[]{:S(2)}) collective-permute-start(f32[1,256,256]{2,1,0:T(8,128)S(1)} %get-tuple-element.94.refs_1_), channel_id=1, source_target_pairs={{0,16},{4,20},{8,24},{12,28},{16,0},{20,4},{24,8},{28,12},{1,17},{... | collective-permute-start | bytes 786440 | tf_op jit(solution)/shard_map/ppermute | solution.py:216
  30.2 18.6 %collective-permute-start.9 = (f32[1,256,256]{2,1,0:T(8,128)S(1)}, f32[1,256,256]{2,1,0:T(8,128)S(1)}, u32[]{:S(2)}, u32[]{:S(2)}) collective-permute-start(f32[1,256,256]{2,1,0:T(8,128)S(1)} %get-tuple-element.99.refs_1_), channel_id=1, source_target_pairs={{0,16},{4,20},{8,24},{12,28},{16,0},{20,4},{24,8},{28,12},{1,17},{... | collective-permute-start | bytes 786440 | tf_op jit(solution)/shard_map/ppermute | solution.py:216
  44.4 12.8 %collective-permute-start.13 = (f32[1,256,256]{2,1,0:T(8,128)S(1)}, f32[1,256,256]{2,1,0:T(8,128)S(1)}, u32[]{:S(2)}, u32[]{:S(2)}) collective-permute-start(f32[1,256,256]{2,1,0:T(8,128)S(1)} %get-tuple-element.106.refs_2_), channel_id=1, source_target_pairs={{0,16},{4,20},{8,24},{12,28},{16,0},{20,4},{24,8},{28,12},{1,17},{... | collective-permute-start | bytes 786440 | tf_op jit(solution)/shard_map/ppermute | solution.py:216
  54.4 14.5 %collective-permute-start.17 = (f32[1,256,256]{2,1,0:T(8,128)S(1)}, f32[1,256,256]{2,1,0:T(8,128)S(1)}, u32[]{:S(2)}, u32[]{:S(2)}) collective-permute-start(f32[1,256,256]{2,1,0:T(8,128)S(1)} %get-tuple-element.111.refs_1_), channel_id=1, source_target_pairs={{0,16},{4,20},{8,24},{12,28},{16,0},{20,4},{24,8},{28,12},{1,17},{... | collective-permute-start | bytes 786440 | tf_op jit(solution)/shard_map/ppermute | solution.py:216
  54.7 15.2 %collective-permute-start.18 = (f32[1,256,256]{2,1,0:T(8,128)S(1)}, f32[1,256,256]{2,1,0:T(8,128)S(1)}, u32[]{:S(2)}, u32[]{:S(2)}) collective-permute-start(f32[1,256,256]{2,1,0:T(8,128)S(1)} %get-tuple-element.112.refs_4_), channel_id=1, source_target_pairs={{0,8},{4,12},{8,0},{12,4},{16,24},{20,28},{24,16},{28,20},{1,9},{5... | collective-permute-start | bytes 786440 | tf_op jit(solution)/shard_map/ppermute | solution.py:216
  59.3 12.8 %collective-permute-start.19 = (f32[2,256,256]{2,1,0:T(8,128)S(1)}, f32[2,256,256]{2,1,0:T(8,128)S(1)}, u32[]{:S(2)}, u32[]{:S(2)}) collective-permute-start(f32[2,256,256]{2,1,0:T(8,128)S(1)} %get-tuple-element.116.refs_1_), channel_id=1, source_target_pairs={{0,4},{4,0},{8,12},{12,8},{16,20},{20,16},{24,28},{28,24},{1,5},{5... | collective-permute-start | bytes 1572872 | tf_op jit(solution)/shard_map/ppermute | solution.py:216
  61.3 19.8 %collective-permute-start.20 = (f32[2,256,256]{2,1,0:T(8,128)S(1)}, f32[2,256,256]{2,1,0:T(8,128)S(1)}, u32[]{:S(2)}, u32[]{:S(2)}) collective-permute-start(f32[2,256,256]{2,1,0:T(8,128)S(1)} %get-tuple-element.118.refs_1_.refs_3_), channel_id=1, source_target_pairs={{0,8},{4,12},{8,0},{12,4},{16,24},{20,28},{24,16},{28,20},{1,9},{5... | collective-permute-start | bytes 1572872 | tf_op jit(solution)/shard_map/ppermute | solution.py:216
  72.0 16.7 %collective-permute-start.23 = (f32[1,256,256]{2,1,0:T(8,128)S(1)}, f32[1,256,256]{2,1,0:T(8,128)S(1)}, u32[]{:S(2)}, u32[]{:S(2)}) collective-permute-start(f32[1,256,256]{2,1,0:T(8,128)S(1)} %get-tuple-element.122.refs_2_), channel_id=1, source_target_pairs={{0,8},{4,12},{8,0},{12,4},{16,24},{20,28},{24,16},{28,20},{1,9},{5... | collective-permute-start | bytes 786440 | tf_op jit(solution)/shard_map/ppermute | solution.py:216
  72.0 19.4 %collective-permute-start.25 = (f32[1,128,512]{2,1,0:T(8,128)S(1)}, f32[1,128,512]{2,1,0:T(8,128)S(1)}, u32[]{:S(2)}, u32[]{:S(2)}) collective-permute-start(f32[1,128,512]{2,1,0:T(8,128)S(1)} %get-tuple-element.126), channel_id=1, source_target_pairs={{0,1},{1,0},{2,3},{3,2},{4,5},{5,4},{6,7},{7,6},{8,9},{9,8},{10,11... | collective-permute-start | bytes 786440 | tf_op jit(solution)/shard_map/ppermute | solution.py:201
  81.7 15.3 %collective-permute-start.24 = (f32[1,256,256]{2,1,0:T(8,128)S(1)}, f32[1,256,256]{2,1,0:T(8,128)S(1)}, u32[]{:S(2)}, u32[]{:S(2)}) collective-permute-start(f32[1,256,256]{2,1,0:T(8,128)S(1)} %get-tuple-element.125.refs_1_), channel_id=1, source_target_pairs={{0,16},{4,20},{8,24},{12,28},{16,0},{20,4},{24,8},{28,12},{1,17},{... | collective-permute-start | bytes 786440 | tf_op jit(solution)/shard_map/ppermute | solution.py:216
  82.0 27.2 %collective-permute-start.28 = (f32[2,256,256]{2,1,0:T(8,128)S(1)}, f32[2,256,256]{2,1,0:T(8,128)S(1)}, u32[]{:S(2)}, u32[]{:S(2)}) collective-permute-start(f32[2,256,256]{2,1,0:T(8,128)S(1)} %get-tuple-element.131.refs_4_.refs_1_), channel_id=1, source_target_pairs={{0,8},{4,12},{8,0},{12,4},{16,24},{20,28},{24,16},{28,20},{1,9},{5... | collective-permute-start | bytes 1572872 | tf_op jit(solution)/shard_map/ppermute | solution.py:216
  91.3 12.9 %collective-permute-start.27 = (f32[1,256,256]{2,1,0:T(8,128)S(1)}, f32[1,256,256]{2,1,0:T(8,128)S(1)}, u32[]{:S(2)}, u32[]{:S(2)}) collective-permute-start(f32[1,256,256]{2,1,0:T(8,128)S(1)} %get-tuple-element.130.refs_1_), channel_id=1, source_target_pairs={{0,4},{4,0},{8,12},{12,8},{16,20},{20,16},{24,28},{28,24},{1,5},{5... | collective-permute-start | bytes 786440 | tf_op jit(solution)/shard_map/ppermute | solution.py:216
  91.4 14.9 %collective-permute-start.29 = (f32[1,256,256]{2,1,0:T(8,128)S(1)}, f32[1,256,256]{2,1,0:T(8,128)S(1)}, u32[]{:S(2)}, u32[]{:S(2)}) collective-permute-start(f32[1,256,256]{2,1,0:T(8,128)S(1)} %get-tuple-element.132.refs_7_), channel_id=1, source_target_pairs={{0,16},{4,20},{8,24},{12,28},{16,0},{20,4},{24,8},{28,12},{1,17},{... | collective-permute-start | bytes 786440 | tf_op jit(solution)/shard_map/ppermute | solution.py:216
  98.6 16.0 %collective-permute-start.32 = (f32[1,128,512]{2,1,0:T(8,128)S(1)}, f32[1,128,512]{2,1,0:T(8,128)S(1)}, u32[]{:S(2)}, u32[]{:S(2)}) collective-permute-start(f32[1,128,512]{2,1,0:T(8,128)S(1)} %get-tuple-element.138), channel_id=1, source_target_pairs={{0,1},{1,0},{2,3},{3,2},{4,5},{5,4},{6,7},{7,6},{8,9},{9,8},{10,11... | collective-permute-start | bytes 786440 | tf_op jit(solution)/shard_map/ppermute | solution.py:201
  104.2 12.2 %collective-permute-start.31 = (f32[1,256,256]{2,1,0:T(8,128)S(1)}, f32[1,256,256]{2,1,0:T(8,128)S(1)}, u32[]{:S(2)}, u32[]{:S(2)}) collective-permute-start(f32[1,256,256]{2,1,0:T(8,128)S(1)} %get-tuple-element.137.refs_1_), channel_id=1, source_target_pairs={{0,8},{4,12},{8,0},{12,4},{16,24},{20,28},{24,16},{28,20},{1,9},{5... | collective-permute-start | bytes 786440 | tf_op jit(solution)/shard_map/ppermute | solution.py:216
  110.2 15.1 %collective-permute-start.33 = (f32[1,256,256]{2,1,0:T(8,128)S(1)}, f32[1,256,256]{2,1,0:T(8,128)S(1)}, u32[]{:S(2)}, u32[]{:S(2)}) collective-permute-start(f32[1,256,256]{2,1,0:T(8,128)S(1)} %get-tuple-element.140.refs_1_), channel_id=1, source_target_pairs={{0,16},{4,20},{8,24},{12,28},{16,0},{20,4},{24,8},{28,12},{1,17},{... | collective-permute-start | bytes 786440 | tf_op jit(solution)/shard_map/ppermute | solution.py:216
  110.8 15.8 %collective-permute-start.34 = (f32[1,256,256]{2,1,0:T(8,128)S(1)}, f32[1,256,256]{2,1,0:T(8,128)S(1)}, u32[]{:S(2)}, u32[]{:S(2)}) collective-permute-start(f32[1,256,256]{2,1,0:T(8,128)S(1)} %get-tuple-element.142.refs_1_), channel_id=1, source_target_pairs={{0,4},{4,0},{8,12},{12,8},{16,20},{20,16},{24,28},{28,24},{1,5},{5... | collective-permute-start | bytes 786440 | tf_op jit(solution)/shard_map/ppermute | solution.py:216
  112.1 25.2 %collective-permute-start.37 = (f32[2,256,256]{2,1,0:T(8,128)S(1)}, f32[2,256,256]{2,1,0:T(8,128)S(1)}, u32[]{:S(2)}, u32[]{:S(2)}) collective-permute-start(f32[2,256,256]{2,1,0:T(8,128)S(1)} %get-tuple-element.147.refs_4_.refs_1_), channel_id=1, source_target_pairs={{0,8},{4,12},{8,0},{12,4},{16,24},{20,28},{24,16},{28,20},{1,9},{5... | collective-permute-start | bytes 1572872 | tf_op jit(solution)/shard_map/ppermute | solution.py:216
  117.0 17.5 %collective-permute-start.35 = (f32[1,256,256]{2,1,0:T(8,128)S(1)}, f32[1,256,256]{2,1,0:T(8,128)S(1)}, u32[]{:S(2)}, u32[]{:S(2)}) collective-permute-start(f32[1,256,256]{2,1,0:T(8,128)S(1)} %get-tuple-element.144.refs_1_), channel_id=1, source_target_pairs={{0,16},{4,20},{8,24},{12,28},{16,0},{20,4},{24,8},{28,12},{1,17},{... | collective-permute-start | bytes 786440 | tf_op jit(solution)/shard_map/ppermute | solution.py:216
  125.7 11.6 %collective-permute-start.36 = (f32[1,256,256]{2,1,0:T(8,128)S(1)}, f32[1,256,256]{2,1,0:T(8,128)S(1)}, u32[]{:S(2)}, u32[]{:S(2)}) collective-permute-start(f32[1,256,256]{2,1,0:T(8,128)S(1)} %get-tuple-element.146.refs_1_), channel_id=1, source_target_pairs={{0,4},{4,0},{8,12},{12,8},{16,20},{20,16},{24,28},{28,24},{1,5},{5... | collective-permute-start | bytes 786440 | tf_op jit(solution)/shard_map/ppermute | solution.py:216
  126.9 16.0 %collective-permute-start.38 = (f32[1,256,256]{2,1,0:T(8,128)S(1)}, f32[1,256,256]{2,1,0:T(8,128)S(1)}, u32[]{:S(2)}, u32[]{:S(2)}) collective-permute-start(f32[1,256,256]{2,1,0:T(8,128)S(1)} %get-tuple-element.149.refs_4_), channel_id=1, source_target_pairs={{0,8},{4,12},{8,0},{12,4},{16,24},{20,28},{24,16},{28,20},{1,9},{5... | collective-permute-start | bytes 786440 | tf_op jit(solution)/shard_map/ppermute | solution.py:216
  (20 other events, 152.4 us)

commit v5 on v4

--- a/solution.py
+++ b/solution.py
@@ -164,9 +164,15 @@
                     at, slot = slots[index]
                     target = sends[at].at[slot]
                 key = (chunks[index][0], stage - 1)
-                target[...] = product(ins[taken[key]] if key in taken else made[key], mine, theirs)
-                if stage == stages:
-                    move(target, region(merged_ref, index))
+                table = ins[taken[key]] if key in taken else made[key]
+                if stage < stages:
+                    target[...] = product(table, mine, theirs)
+                    continue
+                place = region(merged_ref, index)
+                for first in range(0, half, half // 2):
+                    span = pl.ds(first, half // 2)
+                    target[span] = product(table.at[:, span], mine, theirs)
+                    move(target.at[span], place.at[span])
         for each in moves:
             each.wait()
 
@@ -183,7 +189,7 @@
         in_specs=[hbm] * len(whole) + [vmem] * len(operands.arrays),
         out_specs=[hbm] + [vmem] * len(outs),
         scratch_shapes=[pltpu.VMEM((half, chunks[index][2]), jnp.float32) for index in leaving]
-        + [pltpu.SemaphoreType.DMA((len(entering) + len(handing) + len(leaving) + 1,))],
+        + [pltpu.SemaphoreType.DMA((len(entering) + len(handing) + 2 * len(leaving) + 1,))],
         input_output_aliases={len(whole) - 1: 0} if merged is not None else {},
         compiler_params=pltpu.CompilerParams(vmem_limit_bytes=room * 2**20),
         cost_estimate=pl.CostEstimate(flops=1, bytes_accessed=1, transcendentals=0),

time: 155 us -> 155 us (level)
  no operation moved by 1% of the time
where the time goes in v5:
time: 155 us
  waiting for transfers between devices  86.4 us (56%)
  starting transfers between devices  46.9 us (30%)
  Pallas kernels  19.6 us (13%)
    ppermute x35, waiting for transfers between devices, pipelined(): lax.ppermute(array, 'row', partner_route(count, 1 << way))  85.6 us
    ppermute x35, starting transfers between devices, pipelined(): lax.ppermute(array, 'row', partner_route(count, 1 << way))  44.2 us
    pallas_call x27, Pallas kernels, step(): pl.pallas_call(kernel, out_shape=[shape(*weight.shape)] + outs, in_specs=...  19.6 us
  transfers between devices with their start and end apart: 42, of which 27 were waited for; matrix products, arithmetic and copies ran while one was open for 0% of the time, Pallas kernels for 12%

profile of v5, /device:TPU:0, one launch (start us, length us, event | category | flops | bytes accessed | tf_op | source)
XLA Modules:
  0.0 154.6 jit_solution(2810694014786636485)
XLA Ops:
  1.6 2.5 %collective-permute-start.1 = (f32[1,256,256]{2,1,0:T(8,128)S(1)}, f32[1,256,256]{2,1,0:T(8,128)S(1)}, u32[]{:S(2)}, u32[]{:S(2)}) collective-permute-start(f32[1,256,256]{2,1,0:T(8,128)S(1)} %get-tuple-element.83.refs_1_), channel_id=1, source_target_pairs={{0,4},{4,0},{8,12},{12,8},{16,20},{20,16},{24,28},{28,24},{1,5},{5... | collective-permute-start | bytes 786440 | tf_op jit(solution)/shard_map/ppermute | solution.py:222
  8.4 2.9 %collective-permute-done.1.refs_2_ = f32[1,256,256]{2,1,0:T(8,128)S(1)} collective-permute-done((f32[1,256,256]{2,1,0:T(8,128)S(1)}, f32[1,256,256]{2,1,0:T(8,128)S(1)}, u32[]{:S(2)}, u32[]{:S(2)}) %collective-permute-start.1) | collective-permute-done | bytes 262176 | tf_op jit(solution)/shard_map/ppermute | solution.py:222
  21.5 2.6 %collective-permute-start.6 = (f32[1,256,256]{2,1,0:T(8,128)S(1)}, f32[1,256,256]{2,1,0:T(8,128)S(1)}, u32[]{:S(2)}, u32[]{:S(2)}) collective-permute-start(f32[1,256,256]{2,1,0:T(8,128)S(1)} %get-tuple-element.94.refs_1_), channel_id=1, source_target_pairs={{0,16},{4,20},{8,24},{12,28},{16,0},{20,4},{24,8},{28,12},{1,17},{... | collective-permute-start | bytes 786440 | tf_op jit(solution)/shard_map/ppermute | solution.py:222
  24.1 5.5 %collective-permute-done.4.refs_2_ = f32[1,256,256]{2,1,0:T(8,128)S(1)} collective-permute-done((f32[1,256,256]{2,1,0:T(8,128)S(1)}, f32[1,256,256]{2,1,0:T(8,128)S(1)}, u32[]{:S(2)}, u32[]{:S(2)}) %collective-permute-start.4) | collective-permute-done | bytes 262176 | tf_op jit(solution)/shard_map/ppermute | solution.py:222
  32.1 4.5 %collective-permute-done.6.refs_2_ = f32[1,256,256]{2,1,0:T(8,128)S(1)} collective-permute-done((f32[1,256,256]{2,1,0:T(8,128)S(1)}, f32[1,256,256]{2,1,0:T(8,128)S(1)}, u32[]{:S(2)}, u32[]{:S(2)}) %collective-permute-start.6) | collective-permute-done | bytes 262176 | tf_op jit(solution)/shard_map/ppermute | solution.py:222
  36.7 4.5 %collective-permute-done.8.refs_8_ = f32[1,256,256]{2,1,0:T(8,128)S(1)} collective-permute-done((f32[1,256,256]{2,1,0:T(8,128)S(1)}, f32[1,256,256]{2,1,0:T(8,128)S(1)}, u32[]{:S(2)}, u32[]{:S(2)}) %collective-permute-start.8) | collective-permute-done | bytes 262176 | tf_op jit(solution)/shard_map/ppermute | solution.py:222
  42.0 2.3 %collective-permute-start.10 = (f32[1,256,256]{2,1,0:T(8,128)S(1)}, f32[1,256,256]{2,1,0:T(8,128)S(1)}, u32[]{:S(2)}, u32[]{:S(2)}) collective-permute-start(f32[1,256,256]{2,1,0:T(8,128)S(1)} %get-tuple-element.100.refs_4_), channel_id=1, source_target_pairs={{0,4},{4,0},{8,12},{12,8},{16,20},{20,16},{24,28},{28,24},{1,5},{5... | collective-permute-start | bytes 786440 | tf_op jit(solution)/shard_map/ppermute | solution.py:222
  46.4 2.4 %collective-permute-done.9.refs_2_ = f32[1,256,256]{2,1,0:T(8,128)S(1)} collective-permute-done((f32[1,256,256]{2,1,0:T(8,128)S(1)}, f32[1,256,256]{2,1,0:T(8,128)S(1)}, u32[]{:S(2)}, u32[]{:S(2)}) %collective-permute-start.9) | collective-permute-done | bytes 262176 | tf_op jit(solution)/shard_map/ppermute | solution.py:222
  51.4 2.6 %collective-permute-start.14 = (f32[1,256,256]{2,1,0:T(8,128)S(1)}, f32[1,256,256]{2,1,0:T(8,128)S(1)}, u32[]{:S(2)}, u32[]{:S(2)}) collective-permute-start(f32[1,256,256]{2,1,0:T(8,128)S(1)} %get-tuple-element.107.refs_5_), channel_id=1, source_target_pairs={{0,4},{4,0},{8,12},{12,8},{16,20},{20,16},{24,28},{28,24},{1,5},{5... | collective-permute-start | bytes 786440 | tf_op jit(solution)/shard_map/ppermute | solution.py:222
  54.7 2.5 %collective-permute-start.18 = (f32[1,256,256]{2,1,0:T(8,128)S(1)}, f32[1,256,256]{2,1,0:T(8,128)S(1)}, u32[]{:S(2)}, u32[]{:S(2)}) collective-permute-start(f32[1,256,256]{2,1,0:T(8,128)S(1)} %get-tuple-element.112.refs_4_), channel_id=1, source_target_pairs={{0,8},{4,12},{8,0},{12,4},{16,24},{20,28},{24,16},{28,20},{1,9},{5... | collective-permute-start | bytes 786440 | tf_op jit(solution)/shard_map/ppermute | solution.py:222
  61.3 3.3 %collective-permute-start.20 = (f32[2,256,256]{2,1,0:T(8,128)S(1)}, f32[2,256,256]{2,1,0:T(8,128)S(1)}, u32[]{:S(2)}, u32[]{:S(2)}) collective-permute-start(f32[2,256,256]{2,1,0:T(8,128)S(1)} %get-tuple-element.118.refs_1_.refs_3_), channel_id=1, source_target_pairs={{0,8},{4,12},{8,0},{12,4},{16,24},{20,28},{24,16},{28,20},{1,9},{5... | collective-permute-start | bytes 1572872 | tf_op jit(solution)/shard_map/ppermute | solution.py:222
  64.7 4.2 %collective-permute-done.17.refs_2_ = f32[1,256,256]{2,1,0:T(8,128)S(1)} collective-permute-done((f32[1,256,256]{2,1,0:T(8,128)S(1)}, f32[1,256,256]{2,1,0:T(8,128)S(1)}, u32[]{:S(2)}, u32[]{:S(2)}) %collective-permute-start.17) | collective-permute-done | bytes 262176 | tf_op jit(solution)/shard_map/ppermute | solution.py:222
  73.4 7.7 %collective-permute-done.20.refs_2_.refs_4_ = f32[2,256,256]{2,1,0:T(8,128)S(1)} collective-permute-done((f32[2,256,256]{2,1,0:T(8,128)S(1)}, f32[2,256,256]{2,1,0:T(8,128)S(1)}, u32[]{:S(2)}, u32[]{:S(2)}) %collective-permute-start.20) | collective-permute-done | bytes 524320 | tf_op jit(solution)/shard_map/ppermute | solution.py:222
  84.0 4.7 %collective-permute-done.23.refs_3_ = f32[1,256,256]{2,1,0:T(8,128)S(1)} collective-permute-done((f32[1,256,256]{2,1,0:T(8,128)S(1)}, f32[1,256,256]{2,1,0:T(8,128)S(1)}, u32[]{:S(2)}, u32[]{:S(2)}) %collective-permute-start.23) | collective-permute-done | bytes 262176 | tf_op jit(solution)/shard_map/ppermute | solution.py:222
  91.4 5.6 %collective-permute-done.24.refs_2_ = f32[1,256,256]{2,1,0:T(8,128)S(1)} collective-permute-done((f32[1,256,256]{2,1,0:T(8,128)S(1)}, f32[1,256,256]{2,1,0:T(8,128)S(1)}, u32[]{:S(2)}, u32[]{:S(2)}) %collective-permute-start.24) | collective-permute-done | bytes 262176 | tf_op jit(solution)/shard_map/ppermute | solution.py:222
  99.0 5.2 %collective-permute-done.27.refs_2_ = f32[1,256,256]{2,1,0:T(8,128)S(1)} collective-permute-done((f32[1,256,256]{2,1,0:T(8,128)S(1)}, f32[1,256,256]{2,1,0:T(8,128)S(1)}, u32[]{:S(2)}, u32[]{:S(2)}) %collective-permute-start.27) | collective-permute-done | bytes 262176 | tf_op jit(solution)/shard_map/ppermute | solution.py:222
  106.3 2.9 %collective-permute-done.28.refs_5_.refs_2_ = f32[2,256,256]{2,1,0:T(8,128)S(1)} collective-permute-done((f32[2,256,256]{2,1,0:T(8,128)S(1)}, f32[2,256,256]{2,1,0:T(8,128)S(1)}, u32[]{:S(2)}, u32[]{:S(2)}) %collective-permute-start.28) | collective-permute-done | bytes 524320 | tf_op jit(solution)/shard_map/ppermute | solution.py:222
  112.1 2.5 %collective-permute-start.37 = (f32[2,256,256]{2,1,0:T(8,128)S(1)}, f32[2,256,256]{2,1,0:T(8,128)S(1)}, u32[]{:S(2)}, u32[]{:S(2)}) collective-permute-start(f32[2,256,256]{2,1,0:T(8,128)S(1)} %get-tuple-element.147.refs_4_.refs_1_), channel_id=1, source_target_pairs={{0,8},{4,12},{8,0},{12,4},{16,24},{20,28},{24,16},{28,20},{1,9},{5... | collective-permute-start | bytes 1572872 | tf_op jit(solution)/shard_map/ppermute | solution.py:222
  117.0 8.3 %collective-permute-done.33.refs_2_ = f32[1,256,256]{2,1,0:T(8,128)S(1)} collective-permute-done((f32[1,256,256]{2,1,0:T(8,128)S(1)}, f32[1,256,256]{2,1,0:T(8,128)S(1)}, u32[]{:S(2)}, u32[]{:S(2)}) %collective-permute-start.33) | collective-permute-done | bytes 262176 | tf_op jit(solution)/shard_map/ppermute | solution.py:222
  127.0 7.4 %collective-permute-done.35.refs_2_ = f32[1,256,256]{2,1,0:T(8,128)S(1)} collective-permute-done((f32[1,256,256]{2,1,0:T(8,128)S(1)}, f32[1,256,256]{2,1,0:T(8,128)S(1)}, u32[]{:S(2)}, u32[]{:S(2)}) %collective-permute-start.35) | collective-permute-done | bytes 262176 | tf_op jit(solution)/shard_map/ppermute | solution.py:222
  138.5 2.2 %collective-permute-start.40 = (f32[1,256,256]{2,1,0:T(8,128)S(1)}, f32[1,256,256]{2,1,0:T(8,128)S(1)}, u32[]{:S(2)}, u32[]{:S(2)}) collective-permute-start(f32[1,256,256]{2,1,0:T(8,128)S(1)} %get-tuple-element.153.refs_4_), channel_id=1, source_target_pairs={{0,8},{4,12},{8,0},{12,4},{16,24},{20,28},{24,16},{28,20},{1,9},{5... | collective-permute-start | bytes 786440 | tf_op jit(solution)/shard_map/ppermute | solution.py:222
  140.7 2.2 %collective-permute-done.38.refs_5_ = f32[1,256,256]{2,1,0:T(8,128)S(1)} collective-permute-done((f32[1,256,256]{2,1,0:T(8,128)S(1)}, f32[1,256,256]{2,1,0:T(8,128)S(1)}, u32[]{:S(2)}, u32[]{:S(2)}) %collective-permute-start.38) | collective-permute-done | bytes 262176 | tf_op jit(solution)/shard_map/ppermute | solution.py:222
  145.4 3.1 %collective-permute-done.40.refs_5_ = f32[1,256,256]{2,1,0:T(8,128)S(1)} collective-permute-done((f32[1,256,256]{2,1,0:T(8,128)S(1)}, f32[1,256,256]{2,1,0:T(8,128)S(1)}, u32[]{:S(2)}, u32[]{:S(2)}) %collective-permute-start.40) | collective-permute-done | bytes 262176 | tf_op jit(solution)/shard_map/ppermute | solution.py:222
  149.8 3.5 %collective-permute-done.41.refs_2_ = f32[1,256,256]{2,1,0:T(8,128)S(1)} collective-permute-done((f32[1,256,256]{2,1,0:T(8,128)S(1)}, f32[1,256,256]{2,1,0:T(8,128)S(1)}, u32[]{:S(2)}, u32[]{:S(2)}) %collective-permute-start.41) | collective-permute-done | bytes 262176 | tf_op jit(solution)/shard_map/ppermute | solution.py:222
  (91 shorter events, 59.1 us)
Async XLA Ops:
  5.6 38.8 %collective-permute-start.11 = (f32[5,128,512]{2,1,0:T(8,128)S(1)}, f32[5,128,512]{2,1,0:T(8,128)S(1)}, u32[]{:S(2)}, u32[]{:S(2)}) collective-permute-start(f32[5,128,512]{2,1,0:T(8,128)S(1)} %get-tuple-element.102), channel_id=1, source_target_pairs={{0,2},{1,3},{2,0},{3,1},{4,6},{5,7},{6,4},{7,5},{8,10},{9,11},{10,... | collective-permute-start | bytes 3932168 | tf_op jit(solution)/shard_map/ppermute | solution.py:208
  17.6 12.0 %collective-permute-start.4 = (f32[1,256,256]{2,1,0:T(8,128)S(1)}, f32[1,256,256]{2,1,0:T(8,128)S(1)}, u32[]{:S(2)}, u32[]{:S(2)}) collective-permute-start(f32[1,256,256]{2,1,0:T(8,128)S(1)} %get-tuple-element.91.refs_1_), channel_id=1, source_target_pairs={{0,8},{4,12},{8,0},{12,4},{16,24},{20,28},{24,16},{28,20},{1,9},{5... | collective-permute-start | bytes 786440 | tf_op jit(solution)/shard_map/ppermute | solution.py:222
  19.9 21.3 %collective-permute-start.7 = (f32[2,256,256]{2,1,0:T(8,128)S(1)}, f32[2,256,256]{2,1,0:T(8,128)S(1)}, u32[]{:S(2)}, u32[]{:S(2)}) collective-permute-start(f32[2,256,256]{2,1,0:T(8,128)S(1)} %get-tuple-element.96.refs_4_.refs_7_), channel_id=1, source_target_pairs={{0,4},{4,0},{8,12},{12,8},{16,20},{20,16},{24,28},{28,24},{1,5},{5... | collective-permute-start | bytes 1572872 | tf_op jit(solution)/shard_map/ppermute | solution.py:222
  21.5 15.2 %collective-permute-start.6 = (f32[1,256,256]{2,1,0:T(8,128)S(1)}, f32[1,256,256]{2,1,0:T(8,128)S(1)}, u32[]{:S(2)}, u32[]{:S(2)}) collective-permute-start(f32[1,256,256]{2,1,0:T(8,128)S(1)} %get-tuple-element.94.refs_1_), channel_id=1, source_target_pairs={{0,16},{4,20},{8,24},{12,28},{16,0},{20,4},{24,8},{28,12},{1,17},{... | collective-permute-start | bytes 786440 | tf_op jit(solution)/shard_map/ppermute | solution.py:222
  30.2 18.6 %collective-permute-start.9 = (f32[1,256,256]{2,1,0:T(8,128)S(1)}, f32[1,256,256]{2,1,0:T(8,128)S(1)}, u32[]{:S(2)}, u32[]{:S(2)}) collective-permute-start(f32[1,256,256]{2,1,0:T(8,128)S(1)} %get-tuple-element.99.refs_1_), channel_id=1, source_target_pairs={{0,16},{4,20},{8,24},{12,28},{16,0},{20,4},{24,8},{28,12},{1,17},{... | collective-permute-start | bytes 786440 | tf_op jit(solution)/shard_map/ppermute | solution.py:222
  44.4 12.8 %collective-permute-start.13 = (f32[1,256,256]{2,1,0:T(8,128)S(1)}, f32[1,256,256]{2,1,0:T(8,128)S(1)}, u32[]{:S(2)}, u32[]{:S(2)}) collective-permute-start(f32[1,256,256]{2,1,0:T(8,128)S(1)} %get-tuple-element.106.refs_2_), channel_id=1, source_target_pairs={{0,16},{4,20},{8,24},{12,28},{16,0},{20,4},{24,8},{28,12},{1,17},{... | collective-permute-start | bytes 786440 | tf_op jit(solution)/shard_map/ppermute | solution.py:222
  54.4 14.5 %collective-permute-start.17 = (f32[1,256,256]{2,1,0:T(8,128)S(1)}, f32[1,256,256]{2,1,0:T(8,128)S(1)}, u32[]{:S(2)}, u32[]{:S(2)}) collective-permute-start(f32[1,256,256]{2,1,0:T(8,128)S(1)} %get-tuple-element.111.refs_1_), channel_id=1, source_target_pairs={{0,16},{4,20},{8,24},{12,28},{16,0},{20,4},{24,8},{28,12},{1,17},{... | collective-permute-start | bytes 786440 | tf_op jit(solution)/shard_map/ppermute | solution.py:222
  54.7 15.2 %collective-permute-start.18 = (f32[1,256,256]{2,1,0:T(8,128)S(1)}, f32[1,256,256]{2,1,0:T(8,128)S(1)}, u32[]{:S(2)}, u32[]{:S(2)}) collective-permute-start(f32[1,256,256]{2,1,0:T(8,128)S(1)} %get-tuple-element.112.refs_4_), channel_id=1, source_target_pairs={{0,8},{4,12},{8,0},{12,4},{16,24},{20,28},{24,16},{28,20},{1,9},{5... | collective-permute-start | bytes 786440 | tf_op jit(solution)/shard_map/ppermute | solution.py:222
  59.3 12.7 %collective-permute-start.19 = (f32[2,256,256]{2,1,0:T(8,128)S(1)}, f32[2,256,256]{2,1,0:T(8,128)S(1)}, u32[]{:S(2)}, u32[]{:S(2)}) collective-permute-start(f32[2,256,256]{2,1,0:T(8,128)S(1)} %get-tuple-element.116.refs_1_), channel_id=1, source_target_pairs={{0,4},{4,0},{8,12},{12,8},{16,20},{20,16},{24,28},{28,24},{1,5},{5... | collective-permute-start | bytes 1572872 | tf_op jit(solution)/shard_map/ppermute | solution.py:222
  61.3 19.8 %collective-permute-start.20 = (f32[2,256,256]{2,1,0:T(8,128)S(1)}, f32[2,256,256]{2,1,0:T(8,128)S(1)}, u32[]{:S(2)}, u32[]{:S(2)}) collective-permute-start(f32[2,256,256]{2,1,0:T(8,128)S(1)} %get-tuple-element.118.refs_1_.refs_3_), channel_id=1, source_target_pairs={{0,8},{4,12},{8,0},{12,4},{16,24},{20,28},{24,16},{28,20},{1,9},{5... | collective-permute-start | bytes 1572872 | tf_op jit(solution)/shard_map/ppermute | solution.py:222
  72.0 16.7 %collective-permute-start.23 = (f32[1,256,256]{2,1,0:T(8,128)S(1)}, f32[1,256,256]{2,1,0:T(8,128)S(1)}, u32[]{:S(2)}, u32[]{:S(2)}) collective-permute-start(f32[1,256,256]{2,1,0:T(8,128)S(1)} %get-tuple-element.122.refs_2_), channel_id=1, source_target_pairs={{0,8},{4,12},{8,0},{12,4},{16,24},{20,28},{24,16},{28,20},{1,9},{5... | collective-permute-start | bytes 786440 | tf_op jit(solution)/shard_map/ppermute | solution.py:222
  72.0 19.4 %collective-permute-start.25 = (f32[1,128,512]{2,1,0:T(8,128)S(1)}, f32[1,128,512]{2,1,0:T(8,128)S(1)}, u32[]{:S(2)}, u32[]{:S(2)}) collective-permute-start(f32[1,128,512]{2,1,0:T(8,128)S(1)} %get-tuple-element.126), channel_id=1, source_target_pairs={{0,1},{1,0},{2,3},{3,2},{4,5},{5,4},{6,7},{7,6},{8,9},{9,8},{10,11... | collective-permute-start | bytes 786440 | tf_op jit(solution)/shard_map/ppermute | solution.py:207
  81.7 15.3 %collective-permute-start.24 = (f32[1,256,256]{2,1,0:T(8,128)S(1)}, f32[1,256,256]{2,1,0:T(8,128)S(1)}, u32[]{:S(2)}, u32[]{:S(2)}) collective-permute-start(f32[1,256,256]{2,1,0:T(8,128)S(1)} %get-tuple-element.125.refs_1_), channel_id=1, source_target_pairs={{0,16},{4,20},{8,24},{12,28},{16,0},{20,4},{24,8},{28,12},{1,17},{... | collective-permute-start | bytes 786440 | tf_op jit(solution)/shard_map/ppermute | solution.py:222
  82.0 27.2 %collective-permute-start.28 = (f32[2,256,256]{2,1,0:T(8,128)S(1)}, f32[2,256,256]{2,1,0:T(8,128)S(1)}, u32[]{:S(2)}, u32[]{:S(2)}) collective-permute-start(f32[2,256,256]{2,1,0:T(8,128)S(1)} %get-tuple-element.131.refs_4_.refs_1_), channel_id=1, source_target_pairs={{0,8},{4,12},{8,0},{12,4},{16,24},{20,28},{24,16},{28,20},{1,9},{5... | collective-permute-start | bytes 1572872 | tf_op jit(solution)/shard_map/ppermute | solution.py:222
  91.3 12.9 %collective-permute-start.27 = (f32[1,256,256]{2,1,0:T(8,128)S(1)}, f32[1,256,256]{2,1,0:T(8,128)S(1)}, u32[]{:S(2)}, u32[]{:S(2)}) collective-permute-start(f32[1,256,256]{2,1,0:T(8,128)S(1)} %get-tuple-element.130.refs_1_), channel_id=1, source_target_pairs={{0,4},{4,0},{8,12},{12,8},{16,20},{20,16},{24,28},{28,24},{1,5},{5... | collective-permute-start | bytes 786440 | tf_op jit(solution)/shard_map/ppermute | solution.py:222
  91.4 14.9 %collective-permute-start.29 = (f32[1,256,256]{2,1,0:T(8,128)S(1)}, f32[1,256,256]{2,1,0:T(8,128)S(1)}, u32[]{:S(2)}, u32[]{:S(2)}) collective-permute-start(f32[1,256,256]{2,1,0:T(8,128)S(1)} %get-tuple-element.132.refs_7_), channel_id=1, source_target_pairs={{0,16},{4,20},{8,24},{12,28},{16,0},{20,4},{24,8},{28,12},{1,17},{... | collective-permute-start | bytes 786440 | tf_op jit(solution)/shard_map/ppermute | solution.py:222
  98.6 16.0 %collective-permute-start.32 = (f32[1,128,512]{2,1,0:T(8,128)S(1)}, f32[1,128,512]{2,1,0:T(8,128)S(1)}, u32[]{:S(2)}, u32[]{:S(2)}) collective-permute-start(f32[1,128,512]{2,1,0:T(8,128)S(1)} %get-tuple-element.138), channel_id=1, source_target_pairs={{0,1},{1,0},{2,3},{3,2},{4,5},{5,4},{6,7},{7,6},{8,9},{9,8},{10,11... | collective-permute-start | bytes 786440 | tf_op jit(solution)/shard_map/ppermute | solution.py:207
  104.2 12.2 %collective-permute-start.31 = (f32[1,256,256]{2,1,0:T(8,128)S(1)}, f32[1,256,256]{2,1,0:T(8,128)S(1)}, u32[]{:S(2)}, u32[]{:S(2)}) collective-permute-start(f32[1,256,256]{2,1,0:T(8,128)S(1)} %get-tuple-element.137.refs_1_), channel_id=1, source_target_pairs={{0,8},{4,12},{8,0},{12,4},{16,24},{20,28},{24,16},{28,20},{1,9},{5... | collective-permute-start | bytes 786440 | tf_op jit(solution)/shard_map/ppermute | solution.py:222
  110.2 15.1 %collective-permute-start.33 = (f32[1,256,256]{2,1,0:T(8,128)S(1)}, f32[1,256,256]{2,1,0:T(8,128)S(1)}, u32[]{:S(2)}, u32[]{:S(2)}) collective-permute-start(f32[1,256,256]{2,1,0:T(8,128)S(1)} %get-tuple-element.140.refs_1_), channel_id=1, source_target_pairs={{0,16},{4,20},{8,24},{12,28},{16,0},{20,4},{24,8},{28,12},{1,17},{... | collective-permute-start | bytes 786440 | tf_op jit(solution)/shard_map/ppermute | solution.py:222
  110.8 15.8 %collective-permute-start.34 = (f32[1,256,256]{2,1,0:T(8,128)S(1)}, f32[1,256,256]{2,1,0:T(8,128)S(1)}, u32[]{:S(2)}, u32[]{:S(2)}) collective-permute-start(f32[1,256,256]{2,1,0:T(8,128)S(1)} %get-tuple-element.142.refs_1_), channel_id=1, source_target_pairs={{0,4},{4,0},{8,12},{12,8},{16,20},{20,16},{24,28},{28,24},{1,5},{5... | collective-permute-start | bytes 786440 | tf_op jit(solution)/shard_map/ppermute | solution.py:222
  112.1 25.2 %collective-permute-start.37 = (f32[2,256,256]{2,1,0:T(8,128)S(1)}, f32[2,256,256]{2,1,0:T(8,128)S(1)}, u32[]{:S(2)}, u32[]{:S(2)}) collective-permute-start(f32[2,256,256]{2,1,0:T(8,128)S(1)} %get-tuple-element.147.refs_4_.refs_1_), channel_id=1, source_target_pairs={{0,8},{4,12},{8,0},{12,4},{16,24},{20,28},{24,16},{28,20},{1,9},{5... | collective-permute-start | bytes 1572872 | tf_op jit(solution)/shard_map/ppermute | solution.py:222
  117.0 17.5 %collective-permute-start.35 = (f32[1,256,256]{2,1,0:T(8,128)S(1)}, f32[1,256,256]{2,1,0:T(8,128)S(1)}, u32[]{:S(2)}, u32[]{:S(2)}) collective-permute-start(f32[1,256,256]{2,1,0:T(8,128)S(1)} %get-tuple-element.144.refs_1_), channel_id=1, source_target_pairs={{0,16},{4,20},{8,24},{12,28},{16,0},{20,4},{24,8},{28,12},{1,17},{... | collective-permute-start | bytes 786440 | tf_op jit(solution)/shard_map/ppermute | solution.py:222
  125.7 11.6 %collective-permute-start.36 = (f32[1,256,256]{2,1,0:T(8,128)S(1)}, f32[1,256,256]{2,1,0:T(8,128)S(1)}, u32[]{:S(2)}, u32[]{:S(2)}) collective-permute-start(f32[1,256,256]{2,1,0:T(8,128)S(1)} %get-tuple-element.146.refs_1_), channel_id=1, source_target_pairs={{0,4},{4,0},{8,12},{12,8},{16,20},{20,16},{24,28},{28,24},{1,5},{5... | collective-permute-start | bytes 786440 | tf_op jit(solution)/shard_map/ppermute | solution.py:222
  126.9 16.0 %collective-permute-start.38 = (f32[1,256,256]{2,1,0:T(8,128)S(1)}, f32[1,256,256]{2,1,0:T(8,128)S(1)}, u32[]{:S(2)}, u32[]{:S(2)}) collective-permute-start(f32[1,256,256]{2,1,0:T(8,128)S(1)} %get-tuple-element.149.refs_4_), channel_id=1, source_target_pairs={{0,8},{4,12},{8,0},{12,4},{16,24},{20,28},{24,16},{28,20},{1,9},{5... | collective-permute-start | bytes 786440 | tf_op jit(solution)/shard_map/ppermute | solution.py:222
  (20 other events, 152.5 us)
